TPU v7x, 32 devices: a whole 2x2x4 slice. The times are simulated.
32 devices in a mesh: dp: 16 (over z, y, x), tensor: 2 (over core).
Axes of the slice: x: 2, y: 2, z: 4, core: 2. Of those that a mesh axis runs over, the one named last changes fastest.
Arguments:
- tokens: bfloat16 [6144, 1536], P(('dp', 'tensor')), may hold values from -6 to 6
- out_grad: bfloat16 [6144, 1536], P(('dp', 'tensor')), may hold values from -6 to 6
- lengths: int32 [16, 7], P('dp'), may hold values from 1 to 240, as said below
- attn_gain: bfloat16 [1536], replicated, may hold values from 0.5 to 1.5
- q_weight: bfloat16 [1536, 1536], P('dp', 'tensor'), may hold values from -0.21875 to 0.21875
- q_bias: bfloat16 [1536], P('tensor'), may hold values from -3 to 3
- k_weight: bfloat16 [1536, 256], P('dp', 'tensor'), may hold values from -0.21875 to 0.21875
- k_bias: bfloat16 [256], P('tensor'), may hold values from -3 to 3
- v_weight: bfloat16 [1536, 256], P('dp', 'tensor'), may hold values from -0.15625 to 0.15625
- v_bias: bfloat16 [256], P('tensor'), may hold values from -3 to 3
- o_weight: bfloat16 [1536, 1536], P('dp', 'tensor'), may hold values from -0.875 to 0.875
- mlp_gain: bfloat16 [1536], replicated, may hold values from 0.5 to 1.5
- gate_weight: bfloat16 [1536, 8960], P('dp', 'tensor'), may hold values from -0.15625 to 0.15625
- up_weight: bfloat16 [1536, 8960], P('dp', 'tensor'), may hold values from -0.15625 to 0.15625
- down_weight: bfloat16 [1536, 8960], P('dp', 'tensor'), may hold values from -0.0625 to 0.0625
Outputs:
- block_out: bfloat16 [6144, 1536], P(('dp', 'tensor'))
- tokens_grad: bfloat16 [6144, 1536], P(('dp', 'tensor'))
- attn_gain_grad: float32 [1536], replicated
- q_weight_grad: float32 [1536, 1536], P('dp', 'tensor')
- q_bias_grad: float32 [1536], P('tensor')
- k_weight_grad: float32 [1536, 256], P('dp', 'tensor')
- k_bias_grad: float32 [256], P('tensor')
- v_weight_grad: float32 [1536, 256], P('dp', 'tensor')
- v_bias_grad: float32 [256], P('tensor')
- o_weight_grad: float32 [1536, 1536], P('dp', 'tensor')
- mlp_gain_grad: float32 [1536], replicated
- gate_weight_grad: float32 [1536, 8960], P('dp', 'tensor')
- up_weight_grad: float32 [1536, 8960], P('dp', 'tensor')
- down_weight_grad: float32 [1536, 8960], P('dp', 'tensor')
Inputs may be any that keep to these rules, and one draw needn't show every extreme that they name: Each row holds the lengths of the 7 sequences packed, in order, into the 384 tokens of one index of dp; they sum to 384, and the longest is exactly 240 tokens.
All inputs are finite; a program needn't handle non-finite values.
Results may differ from a plain program's by a relative error of at most 0.022.
Values may be sent and summed in bfloat16 or wider, within the bound.
No kernel may reach another device: no remote copies, remote signals or barrier semaphores. Data moves between devices by JAX's collectives and lax.ppermute only.
A program may use at most 320 MiB of HBM per device.

v0:
```python
import math

import jax
import jax.numpy as jnp
from jax import lax
from jax.sharding import PartitionSpec as P

HEAD_DIM = 128


EPSILON = 1e-06
ROPE_BASE = 1000000.0
MASKED = -1e30


def normalize(values):
    factor = lax.rsqrt(jnp.mean(values * values, axis=1, keepdims=True) + EPSILON)
    return (values * factor, factor)


def norm_back(grad_normed, normed, factor, gain_vec):
    scaled = grad_normed * gain_vec[None, :]
    row_inner = jnp.mean(scaled * normed, axis=1, keepdims=True)
    return (factor * (scaled - normed * row_inner), jnp.sum(grad_normed * normed, axis=0))


def rope_tables(positions, width):
    half_width = width // 2
    frequency = jnp.power(ROPE_BASE, -2.0 * jnp.arange(half_width, dtype=jnp.float32) / width)
    angles = positions.astype(jnp.float32)[:, None] * frequency[None, :]
    return (jnp.cos(angles), jnp.sin(angles))


def rotate(values, cosine_table, sine_table):
    half_width = values.shape[-1] // 2
    lower_half = values[..., :half_width]
    upper_half = values[..., half_width:]
    return jnp.concatenate(
        [
            lower_half * cosine_table - upper_half * sine_table,
            upper_half * cosine_table + lower_half * sine_table,
        ],
        axis=-1,
    )


def unrotate(values, cosine_table, sine_table):
    half_width = values.shape[-1] // 2
    lower_half = values[..., :half_width]
    upper_half = values[..., half_width:]
    return jnp.concatenate(
        [
            lower_half * cosine_table + upper_half * sine_table,
            upper_half * cosine_table - lower_half * sine_table,
        ],
        axis=-1,
    )


def segment_info(length_row, group_rows):
    seq_ends = jnp.cumsum(length_row)
    starts = seq_ends - length_row
    places = jnp.arange(group_rows, dtype=jnp.int32)
    segment = jnp.sum((places[:, None] >= seq_ends[None, :]).astype(jnp.int32), axis=1)
    slot_ids = jnp.arange(length_row.shape[0], dtype=jnp.int32)
    offset = jnp.sum(jnp.where(segment[:, None] == slot_ids[None, :], starts[None, :], 0), axis=1)
    return (segment, places - offset)


def rows_of_group(local_rows):
    return lax.all_gather(local_rows, "tensor", axis=0, tiled=True)


def grads_of_group(local_rows):
    return lax.all_gather(local_rows, "tensor", axis=0, tiled=True)


def group_sum(partial_rows):
    return lax.psum_scatter(partial_rows, "tensor", scatter_dimension=0, tiled=True)


def input_sum(partial_rows):
    return lax.psum_scatter(partial_rows, "tensor", scatter_dimension=0, tiled=True)


def rows_product(left_rows, stacked):
    return jnp.dot(
        left_rows,
        lax.all_gather(stacked, "dp", axis=0, tiled=True),
        preferred_element_type=jnp.float32,
    )


def columns_product(right_rows, stacked):
    return lax.dot_general(
        right_rows,
        lax.all_gather(stacked, "dp", axis=0, tiled=True),
        (((1,), (1,)), ((), ())),
        preferred_element_type=jnp.float32,
    )


def term_maker(grad_pairs):
    blocks = [
        lax.dot_general(
            left_rows, right_rows, (((0,), (0,)), ((), ())), preferred_element_type=jnp.float32
        )
        for left_rows, right_rows in grad_pairs
    ]
    return jnp.concatenate(blocks, axis=1)


def reduce_ff(grad_pairs):
    return lax.psum_scatter(term_maker(grad_pairs), "dp", scatter_dimension=0, tiled=True)


def reduce_late(grad_pairs):
    return lax.psum_scatter(term_maker(grad_pairs), "dp", scatter_dimension=0, tiled=True)


def attention_scores(queries, key_rows, allowed):
    score_scale = 1.0 / math.sqrt(queries.shape[-1])
    raw_scores = jnp.einsum("qgpd,kgd->gpqk", queries, key_rows, preferred_element_type=jnp.float32)
    return jnp.where(allowed[None, None], raw_scores * score_scale, MASKED)


def per_device(
    tokens,
    out_grad,
    lengths,
    attn_gain,
    q_weight,
    q_bias,
    k_weight,
    k_bias,
    v_weight,
    v_bias,
    o_weight,
    mlp_gain,
    gate_weight,
    up_weight,
    down_weight,
):
    inputs = tokens.astype(jnp.float32)
    local_rows = inputs.shape[0]
    tensor_count = lax.axis_size("tensor")
    tensor_place = lax.axis_index("tensor")
    group_rows = local_rows * tensor_count
    q_cols = q_weight.shape[1]
    kv_cols = k_weight.shape[1]
    qkv_cols = q_cols + 2 * kv_cols
    ff_cols = gate_weight.shape[1]
    kv_groups = kv_cols // HEAD_DIM
    per_group = q_cols // HEAD_DIM // kv_groups
    score_scale = 1.0 / math.sqrt(HEAD_DIM)
    segment, positions = segment_info(lengths[0], group_rows)
    places = jnp.arange(group_rows, dtype=jnp.int32)
    allowed = (segment[:, None] == segment[None, :]) & (places[None, :] <= places[:, None])
    cosine_table, sine_table = rope_tables(positions, HEAD_DIM)
    q_cosine = cosine_table[:, None, None, :]
    q_sine = sine_table[:, None, None, :]
    k_cosine = cosine_table[:, None, :]
    k_sine = sine_table[:, None, :]
    gain_one = attn_gain.astype(jnp.float32)
    gain_two = mlp_gain.astype(jnp.float32)
    bias_all = jnp.concatenate([q_bias, k_bias, v_bias]).astype(jnp.float32)
    qkv_local = jnp.concatenate([q_weight, k_weight, v_weight], axis=1)
    gate_up = jnp.concatenate([gate_weight, up_weight], axis=1)
    normed_one, factor_one = normalize(inputs)
    attn_in = rows_of_group((normed_one * gain_one[None, :]).astype(jnp.bfloat16))
    linear = rows_product(attn_in, qkv_local)
    linear = linear + bias_all[None, :]
    queries = rotate(
        linear[:, :q_cols].reshape(group_rows, kv_groups, per_group, HEAD_DIM), q_cosine, q_sine
    ).astype(jnp.bfloat16)
    key_rows = rotate(
        linear[:, q_cols : q_cols + kv_cols].reshape(group_rows, kv_groups, HEAD_DIM),
        k_cosine,
        k_sine,
    ).astype(jnp.bfloat16)
    values = (
        linear[:, q_cols + kv_cols :].reshape(group_rows, kv_groups, HEAD_DIM).astype(jnp.bfloat16)
    )
    scores = attention_scores(queries, key_rows, allowed)
    row_peak = jnp.max(scores, axis=-1, keepdims=True)
    exponent = jnp.exp(scores - row_peak)
    row_mass = jnp.sum(exponent, axis=-1, keepdims=True)
    log_mass = row_peak + jnp.log(row_mass)
    probs_low = (exponent / row_mass).astype(jnp.bfloat16)
    mixed_heads = jnp.einsum(
        "gpqk,kgd->qgpd", probs_low, values, preferred_element_type=jnp.float32
    )
    mixed_heads = mixed_heads.reshape(group_rows, q_cols).astype(jnp.bfloat16)
    attn_part = columns_product(mixed_heads, o_weight)
    hidden_state = inputs + group_sum(attn_part)
    normed_two, factor_two = normalize(hidden_state)
    mlp_in = rows_of_group((normed_two * gain_two[None, :]).astype(jnp.bfloat16))
    gate_up_out = rows_product(mlp_in, gate_up)
    gate_val = gate_up_out[:, :ff_cols]
    up_val = gate_up_out[:, ff_cols:]
    sigmoid_gate = jax.nn.sigmoid(gate_val)
    activated = gate_val * sigmoid_gate
    hidden_units = (activated * up_val).astype(jnp.bfloat16)
    mlp_part = columns_product(hidden_units, down_weight)
    outputs = hidden_state + group_sum(mlp_part)
    block_out = outputs.astype(jnp.bfloat16)
    grad_out_all = grads_of_group(out_grad)
    grad_hidden = rows_product(grad_out_all, down_weight)
    grad_gate = (
        grad_hidden * up_val * sigmoid_gate * (1.0 + gate_val * (1.0 - sigmoid_gate))
    ).astype(jnp.bfloat16)
    grad_up = (grad_hidden * activated).astype(jnp.bfloat16)
    grad_gate_up = jnp.concatenate([grad_gate, grad_up], axis=1)
    grad_normed_two = input_sum(columns_product(grad_gate_up, gate_up))
    gate_grads = reduce_ff([(mlp_in, grad_gate)])
    up_grads = reduce_ff([(mlp_in, grad_up)])
    down_pair = [(grad_out_all, hidden_units)]
    down_grads = reduce_late(down_pair)
    back_two, gain_two_grad = norm_back(grad_normed_two, normed_two, factor_two, gain_two)
    grad_state = out_grad.astype(jnp.float32) + back_two
    grad_state_all = grads_of_group(grad_state.astype(jnp.bfloat16))
    grad_mixed = rows_product(grad_state_all, o_weight)
    grad_heads = grad_mixed.astype(jnp.bfloat16).reshape(group_rows, kv_groups, per_group, HEAD_DIM)
    scores_again = attention_scores(queries, key_rows, allowed)
    prob_rows = jnp.exp(scores_again - log_mass)
    grad_probs = jnp.einsum(
        "qgpd,kgd->gpqk", grad_heads, values, preferred_element_type=jnp.float32
    )
    row_inner = jnp.sum(prob_rows * grad_probs, axis=-1, keepdims=True)
    grad_scores = (prob_rows * (grad_probs - row_inner) * score_scale).astype(jnp.bfloat16)
    grad_values = jnp.einsum(
        "gpqk,qgpd->kgd",
        prob_rows.astype(jnp.bfloat16),
        grad_heads,
        preferred_element_type=jnp.float32,
    )
    grad_queries = jnp.einsum(
        "gpqk,kgd->qgpd", grad_scores, key_rows, preferred_element_type=jnp.float32
    )
    grad_keys = jnp.einsum(
        "gpqk,qgpd->kgd", grad_scores, queries, preferred_element_type=jnp.float32
    )
    grad_linear = jnp.concatenate(
        [
            unrotate(grad_queries, q_cosine, q_sine).reshape(group_rows, q_cols),
            unrotate(grad_keys, k_cosine, k_sine).reshape(group_rows, kv_cols),
            grad_values.reshape(group_rows, kv_cols),
        ],
        axis=1,
    ).astype(jnp.bfloat16)
    bias_grad = jnp.sum(grad_linear.astype(jnp.float32), axis=0)
    grad_part = columns_product(grad_linear, qkv_local)
    grad_normed_one = input_sum(grad_part)
    back_one, gain_one_grad = norm_back(grad_normed_one, normed_one, factor_one, gain_one)
    tokens_grad = (grad_state + back_one).astype(jnp.bfloat16)
    attn_pairs = [(attn_in, grad_linear), (grad_state_all, mixed_heads)]
    attn_grads = reduce_late(attn_pairs)
    owner_mask = (jnp.arange(tensor_count, dtype=jnp.int32) == tensor_place).astype(jnp.float32)
    bias_table = owner_mask[:, None] * bias_grad[None, :]
    bias_sum, gain_sum = lax.psum(
        (bias_table, jnp.stack([gain_one_grad, gain_two_grad])), ("dp", "tensor")
    )
    own_bias = lax.dynamic_index_in_dim(bias_sum, tensor_place, 0, keepdims=False)
    return (
        block_out,
        tokens_grad,
        gain_sum[0],
        attn_grads[:, :q_cols],
        own_bias[:q_cols],
        attn_grads[:, q_cols : q_cols + kv_cols],
        own_bias[q_cols : q_cols + kv_cols],
        attn_grads[:, q_cols + kv_cols : qkv_cols],
        own_bias[q_cols + kv_cols :],
        attn_grads[:, qkv_cols:],
        gain_sum[1],
        gate_grads,
        up_grads,
        down_grads,
    )


def solution(mesh):
    in_specs = (
        P(("dp", "tensor"), None),
        P(("dp", "tensor"), None),
        P("dp", None),
        P(),
        P("dp", "tensor"),
        P("tensor"),
        P("dp", "tensor"),
        P("tensor"),
        P("dp", "tensor"),
        P("tensor"),
        P("dp", "tensor"),
        P(),
        P("dp", "tensor"),
        P("dp", "tensor"),
        P("dp", "tensor"),
    )
    out_specs = (
        P(("dp", "tensor"), None),
        P(("dp", "tensor"), None),
        P(),
        P("dp", "tensor"),
        P("tensor"),
        P("dp", "tensor"),
        P("tensor"),
        P("dp", "tensor"),
        P("tensor"),
        P("dp", "tensor"),
        P(),
        P("dp", "tensor"),
        P("dp", "tensor"),
        P("dp", "tensor"),
    )
    return jax.shard_map(
        per_device, mesh=mesh, in_specs=in_specs, out_specs=out_specs, check_vma=False
    )
```

profile of v0, /device:TPU:0, one launch (start us, length us, event | category | flops | bytes accessed | tf_op | source)
XLA Modules:
  0.0 2165.6 jit_solution(11938159285182174296)
XLA Ops:
  15.6 8.5 all-gather.9.cloned.1.call-done
  24.1 72.7 %all-gather.11.cloned.1.call-done = bf16[1536,1024]{1,0:T(8,128)(2,1)} async-done(((bf16[96,1024]{1,0:T(8,128)(2,1)}), bf16[1536,1024]{1,0:T(8,128)(2,1)}) %all-gather.11.cloned.1.call-update) | async-done | bytes 3145744 | tf_op jit(solution)/shard_map/all_gather | solution.py:89
  96.8 3.6 convolution_add_fusion
  110.5 49.9 %all-gather.13.cloned.1.call-done = bf16[1536,768]{1,0:T(8,128)(2,1)} async-done(((bf16[96,768]{1,0:T(8,128)(2,1)}), bf16[1536,768]{1,0:T(8,128)(2,1)}) %all-gather.13.cloned.1.call-update) | async-done | bytes 2359312 | tf_op jit(solution)/shard_map/all_gather | solution.py:97
  160.4 4.4 fusion.79
  165.5 8.2 reduce-scatter.13.cloned.1.call-done
  182.0 6.0 all-gather.15.cloned.1.call-done
  188.0 298.7 %all-gather.17.cloned.1.call-done = bf16[1536,8960]{1,0:T(8,128)(2,1)} async-done(((bf16[96,8960]{1,0:T(8,128)(2,1)}), bf16[1536,8960]{1,0:T(8,128)(2,1)}) %all-gather.17.cloned.1.call-update) | async-done | bytes 27525136 | tf_op jit(solution)/shard_map/all_gather | solution.py:89
  486.7 19.5 fusion.80
  506.2 157.1 %all-gather.19.cloned.1.call-done = bf16[1536,4480]{1,0:T(8,128)(2,1)} async-done(((bf16[96,4480]{1,0:T(8,128)(2,1)}), bf16[1536,4480]{1,0:T(8,128)(2,1)}) %all-gather.19.cloned.1.call-update) | async-done | bytes 13762576 | tf_op jit(solution)/shard_map/all_gather | solution.py:97
  663.3 15.3 multiply_convert_fusion.1
  678.6 17.9 fusion
  696.5 8.2 reduce-scatter.17.cloned.1.call-done
  704.8 2.8 multiply_reduce_fusion
  712.0 8.9 all-gather.23.cloned.1.call-done
  720.9 3.9 convolution_convert_fusion
  736.8 4.7 fusion.73
  741.6 10.9 fusion.81
  753.9 3.5 fusion.84
  757.5 4.4 fusion.72
  761.9 10.1 pad_maximum_fusion
  772.0 12.2 copy.124
  785.4 14.5 fusion.82
  800.0 14.4 fusion.83
  815.6 15.3 convolution_bitcast_fusion
  830.9 27.7 %copy.126 = f32[1536,4480]{1,0:T(8,128)} copy(f32[1536,4480]{0,1:T(8,128)} %convolution_bitcast_fusion) | data formatting | bytes 55050240
  863.2 40.8 %all-reduce = (f32[2,1536]{1,0:T(2,128)S(1)}, f32[2,1024]{1,0:T(2,128)S(1)}) all-reduce(f32[2,1536]{1,0:T(2,128)S(1)} %pad_maximum_fusion.8, f32[2,1024]{1,0:T(2,128)S(1)} %broadcast_multiply_fusion), channel_id=1, replica_groups=mesh['dp'=16,'tensor'=2] {'dp','tensor'}, use_global_device_ids=true, to_apply=%region_16.17 | all-reduce | flops 5120 | bytes 40960 | tf_op jit(solution)/shard_map/psum | solution.py:260
  905.9 3.4 fusion.30
  909.3 62.5 %reduce-scatter.25.cloned.1.call-done = f32[96,1792]{1,0:T(8,128)} async-done(((f32[1536,1792]{1,0:T(8,128)}), f32[96,1792]{1,0:T(8,128)}) %reduce-scatter.25.cloned.1.call-update) | async-done | bytes 688144
  975.1 392.7 %reduce-scatter.21.cloned.1.call-done = f32[96,4480]{1,0:T(8,128)} async-done(((f32[1536,4480]{1,0:T(8,128)}), f32[96,4480]{1,0:T(8,128)}) %reduce-scatter.21.cloned.1.call-update) | async-done | bytes 1720336 | tf_op jit(solution)/shard_map/reduce_scatter | solution.py:114
  1367.8 394.8 %reduce-scatter.23.cloned.1.call-done = f32[96,4480]{1,0:T(8,128)} async-done(((f32[1536,4480]{1,0:T(8,128)}), f32[96,4480]{1,0:T(8,128)}) %reduce-scatter.23.cloned.1.call-update) | async-done | bytes 1720336 | tf_op jit(solution)/shard_map/reduce_scatter | solution.py:114
  1762.6 395.9 %reduce-scatter.27.cloned.1.call-done = f32[96,4480]{1,0:T(8,128)} async-done(((f32[1536,4480]{1,0:T(8,128)}), f32[96,4480]{1,0:T(8,128)}) %reduce-scatter.27.cloned.1.call-update) | async-done | bytes 1720336
  (197 shorter events, 57.1 us)
Async XLA Ops:
  7.2 4.9 copy-start.38
  7.2 6.4 copy-start.51
  7.2 6.6 copy-start.49
  7.2 6.6 copy-start.50
  7.2 6.6 copy-start.48
  7.3 16.9 all-gather.9.cloned.1.call-start
  12.0 84.8 %all-gather.11.cloned.1.call-start = ((), (), s32[]{:S(2)}) async-start(), calls=%async_computation.9 | async-start | bytes 3342336 | tf_op jit(solution)/shard_map/all_gather | solution.py:89
  12.8 147.6 %all-gather.13.cloned.1.call-start = ((), (), s32[]{:S(2)}) async-start(), calls=%async_computation.10 | async-start | bytes 2506752 | tf_op jit(solution)/shard_map/all_gather | solution.py:97
  13.6 160.2 %reduce-scatter.13.cloned.1.call-start = ((), (), s32[]{:S(2)}) async-start(), calls=%async_computation.11 | async-start | bytes 3538944 | tf_op jit(solution)/shard_map/reduce_scatter | solution.py:79
  13.8 90.0 %copy-start.45 = (f32[64]{0:T(128)}, f32[64]{0:T(128)S(1)}, u32[]{:S(2)}) copy-start(f32[64]{0:T(128)S(1)} %multiply_power_fusion) | copy-start | bytes 772
  15.6 89.1 %copy-start.12 = (f32[384,64]{1,0:T(8,128)}, f32[384,64]{1,0:T(8,128)S(1)}, u32[]{:S(2)}) copy-start(f32[384,64]{1,0:T(8,128)S(1)} %get-tuple-element.101) | copy-start | bytes 294916
  15.6 89.1 %copy-start.14 = (f32[384,64]{1,0:T(8,128)}, f32[384,64]{1,0:T(8,128)S(1)}, u32[]{:S(2)}) copy-start(f32[384,64]{1,0:T(8,128)S(1)} %get-tuple-element.102) | copy-start | bytes 294916
  164.9 23.1 %all-gather.15.cloned.1.call-start = ((), (), s32[]{:S(2)}) async-start(), calls=%async_computation.12 | async-start | bytes 1769472 | tf_op jit(solution)/shard_map/all_gather | solution.py:71
  175.4 532.1 %copy-start.36 = (f32[192]{0:T(256)}, f32[192]{0:T(256)S(1)}, u32[]{:S(2)}) copy-start(f32[192]{0:T(256)S(1)} %add_rsqrt_fusion) | copy-start | bytes 2308
  177.5 309.2 %all-gather.17.cloned.1.call-start = ((), (), s32[]{:S(2)}) async-start(), calls=%async_computation.13 | async-start | bytes 29245440 | tf_op jit(solution)/shard_map/all_gather | solution.py:89
  180.3 325.9 %all-gather.21.cloned.1.call-start = ((), (), s32[]{:S(2)}) async-start(), calls=%async_computation.16 | async-start | bytes 1769472 | tf_op jit(solution)/shard_map/all_gather | solution.py:75
  181.0 482.3 %all-gather.19.cloned.1.call-start = ((), (), s32[]{:S(2)}) async-start(), calls=%async_computation.14 | async-start | bytes 14622720 | tf_op jit(solution)/shard_map/all_gather | solution.py:97
  181.8 523.0 %reduce-scatter.17.cloned.1.call-start = ((), (), s32[]{:S(2)}) async-start(), calls=%async_computation.17 | async-start | bytes 3538944 | tf_op jit(solution)/shard_map/reduce_scatter | solution.py:83
  696.5 24.4 %all-gather.23.cloned.1.call-start = ((), (), s32[]{:S(2)}) async-start(), calls=%async_computation.18 | async-start | bytes 1769472 | tf_op jit(solution)/shard_map/all_gather | solution.py:75
  710.4 151.0 %reduce-scatter.19.cloned.1.call-start = ((), (), s32[]{:S(2)}) async-start(), calls=%async_computation.19 | async-start | bytes 3538944 | tf_op jit(solution)/shard_map/reduce_scatter | solution.py:83
  736.1 5.5 copy-start.21
  741.5 164.3 %reduce-scatter.15.cloned.1.call-start = ((), (), s32[]{:S(2)}) async-start(), calls=%async_computation.15 | async-start | bytes 3538944 | tf_op jit(solution)/shard_map/reduce_scatter | solution.py:79
  752.5 4.9 copy-start.17
  752.5 219.2 %reduce-scatter.25.cloned.1.call-start = ((), (), s32[]{:S(2)}) async-start(), calls=%async_computation.22 | async-start | bytes 11698176
  784.2 583.7 %reduce-scatter.21.cloned.1.call-start = ((), (), s32[]{:S(2)}) async-start(), calls=%async_computation.20 | async-start | bytes 29245440 | tf_op jit(solution)/shard_map/reduce_scatter | solution.py:114
  799.9 962.7 %reduce-scatter.23.cloned.1.call-start = ((), (), s32[]{:S(2)}) async-start(), calls=%async_computation.21 | async-start | bytes 29245440 | tf_op jit(solution)/shard_map/reduce_scatter | solution.py:114
  814.4 1344.2 %reduce-scatter.27.cloned.1.call-start = ((), (), s32[]{:S(2)}) async-start(), calls=%async_computation.23 | async-start | bytes 29245440
  858.7 47.2 %copy-start.2 = (f32[192,1536]{1,0:T(8,128)S(1)}, f32[192,1536]{1,0:T(8,128)}, u32[]{:S(2)}) copy-start(f32[192,1536]{1,0:T(8,128)} %copy-done) | copy-start | bytes 3538948
  858.7 47.2 %copy-start.5 = (f32[192,1536]{1,0:T(8,128)S(1)}, f32[192,1536]{1,0:T(8,128)}, u32[]{:S(2)}) copy-start(f32[192,1536]{1,0:T(8,128)} %reduce-scatter.17.cloned.1.call-done) | copy-start | bytes 3538948
  861.3 44.6 %copy-start.37 = (f32[192]{0:T(256)S(1)}, f32[192]{0:T(256)}, u32[]{:S(2)}) copy-start(f32[192]{0:T(256)} %copy-done.36) | copy-start | bytes 2308
  861.3 44.6 %copy-start.42 = (f32[192]{0:T(256)S(1)}, f32[192]{0:T(256)}, u32[]{:S(2)}) copy-start(f32[192]{0:T(256)} %copy-done.41) | copy-start | bytes 2308
  861.3 44.6 %copy-start.44 = (f32[192]{0:T(256)S(1)}, f32[192]{0:T(256)}, u32[]{:S(2)}) copy-start(f32[192]{0:T(256)} %copy-done.43) | copy-start | bytes 2308
  (36 other events, 60.4 us)
Sparse Core Ops, SparseCore 0:
  12.1 11.9 all-gather.8
  27.5 69.2 all-gather.10
  99.6 60.7 all-gather.12
  165.0 8.7 reduce-scatter.12
  177.6 10.3 all-gather.14
  191.6 295.0 all-gather.16
  488.3 7.4 all-gather.20
  499.0 164.3 all-gather.18
  696.6 8.0 reduce-scatter.16
  710.5 10.3 all-gather.22
  741.7 11.0 reduce-scatter.18
  755.0 11.0 reduce-scatter.14
  784.3 187.4 reduce-scatter.24
  979.2 388.5 reduce-scatter.20
  1374.3 388.3 reduce-scatter.22
  1770.1 388.3 reduce-scatter.26
where the time goes:
time: 2170 us
  waiting for transfers between devices  1870 us (86%)
  matrix products  142 us (7%)
  local copies, waits for them, and re-layouts  60.7 us (3%)
  blocking collectives  40.8 us (2%)
  other arithmetic  39.3 us (2%)
    reduce_scatter x2, waiting for transfers between devices, reduce_ff(): lax.psum_scatter(term_maker(grad_pairs), 'dp', scatter_dimension=0, tiled...  788 us
    unnamed x18, waiting for transfers between devices  461 us
    all_gather x2, waiting for transfers between devices, rows_product(): lax.all_gather(stacked, 'dp', axis=0, tiled=True)  371 us
    all_gather x2, waiting for transfers between devices, columns_product(): lax.all_gather(stacked, 'dp', axis=0, tiled=True)  207 us
    dot_general x5, matrix products, term_maker(): lax.dot_general(left_rows, right_rows, (((0,), (0,)), ((), ())), preferre...  52.1 us
    unnamed x108, local copies, waits for them, and re-layouts  50 us
  transfers between devices with their start and end apart: 16, of which 13 were waited for; matrix products, arithmetic and copies ran while one was open for 8% of the time, Pallas kernels for 0%

commit v1 on v0

v1 whole, which is shorter than its diff:
```python
import math

import jax
import jax.numpy as jnp
from jax import lax
from jax.sharding import PartitionSpec as P

HEAD_DIM = 128
EPSILON = 1e-06
ROPE_BASE = 1000000.0
MASKED = -1e30
LINE = 4
LANES = 128
BF = jnp.bfloat16
F32 = jnp.float32


def normalize(values):
    factor = lax.rsqrt(jnp.mean(values * values, axis=1, keepdims=True) + EPSILON)
    return (values * factor, factor)


def norm_back(grad_normed, normed, factor, gain_vec):
    scaled = grad_normed * gain_vec[None, :]
    row_inner = jnp.mean(scaled * normed, axis=1, keepdims=True)
    return (factor * (scaled - normed * row_inner), jnp.sum(grad_normed * normed, axis=0))


def rope_tables(positions, width):
    half_width = width // 2
    frequency = jnp.power(ROPE_BASE, -2.0 * jnp.arange(half_width, dtype=F32) / width)
    angles = positions.astype(F32)[:, None] * frequency[None, :]
    return (jnp.cos(angles), jnp.sin(angles))


def rotate(values, cosine_table, sine_table):
    half_width = values.shape[-1] // 2
    lower_half = values[..., :half_width]
    upper_half = values[..., half_width:]
    return jnp.concatenate(
        [
            lower_half * cosine_table - upper_half * sine_table,
            upper_half * cosine_table + lower_half * sine_table,
        ],
        axis=-1,
    )


def unrotate(values, cosine_table, sine_table):
    return rotate(values, cosine_table, -sine_table)


def segment_info(length_row, places):
    seq_ends = jnp.cumsum(length_row)
    starts = seq_ends - length_row
    segment = jnp.sum((places[:, None] >= seq_ends[None, :]).astype(jnp.int32), axis=1)
    slot_ids = jnp.arange(length_row.shape[0], dtype=jnp.int32)
    offset = jnp.sum(jnp.where(segment[:, None] == slot_ids[None, :], starts[None, :], 0), axis=1)
    return (segment, places - offset)


class Topo:
    def __init__(self):
        self.dp = lax.axis_size("dp")
        self.square = self.dp // LINE
        self.me = lax.axis_index("dp")
        self.core = lax.axis_index("tensor")
        self.line_at = self.me // self.square
        self.square_at = self.me % self.square
        line_bits = [self.square << i for i in range(LINE.bit_length() - 1)]
        square_bits = [1 << i for i in range(self.square.bit_length() - 1)]
        self.line = (line_bits, line_bits[::-1])
        self.squares = (square_bits, square_bits[::-1])

    def swap(self, array, bits, phase):
        perm = []
        for place in range(self.dp):
            for core in range(2):
                perm.append((place * 2 + core, (place ^ bits[core][phase]) * 2 + core))
        return lax.ppermute(array, ("dp", "tensor"), perm)

    def other_core(self, array):
        return lax.ppermute(array, "tensor", [(0, 1), (1, 0)])

    def offset(self, bits, index, unit):
        totals = [0, 0]
        for core in range(2):
            for phase, bit in enumerate(bits[core]):
                if index >> phase & 1:
                    totals[core] ^= bit // unit
        return jnp.where(self.core == 0, totals[0], totals[1])

    def gather(self, own, bits):
        pieces = [own]
        for phase in range(len(bits[0])):
            pieces = pieces + [self.swap(piece, bits, phase) for piece in pieces]
        return pieces

    def gather_joined(self, own, bits):
        joined = own
        for phase in range(len(bits[0])):
            joined = jnp.concatenate([joined, self.swap(joined, bits, phase)], axis=0)
        return joined

    def scatter_sum(self, array, bits):
        for phase in reversed(range(len(bits[0]))):
            half = array.shape[0] // 2
            got = self.swap(array[half:], bits, phase)
            array = (array[:half].astype(F32) + got.astype(F32)).astype(BF)
        return array

    def total(self, array):
        for bits in (self.line, self.squares):
            for phase in range(len(bits[0])):
                array = array + self.swap(array, bits, phase)
        return array

    def exchange(self, chunks, bits):
        rows = chunks[0].shape[0]
        held = [chunk for chunk in chunks]
        for phase in range(len(bits[0])):
            step = 1 << phase
            keep = [i for i in range(len(chunks)) if not i & step]
            keep = [i for i in keep if held[i] is not None]
            sent = jnp.concatenate([held[i + step] for i in keep], axis=0)
            got = self.swap(sent, bits, phase)
            parts = jnp.split(got, len(keep), axis=0)
            for i, part in zip(keep, parts):
                held[i] = jnp.concatenate([held[i], part], axis=0)
                held[i + step] = None
        return jnp.split(held[0], len(chunks), axis=0)

    def ordered(self, pieces, bits, unit, at):
        count = len(pieces)
        tables = []
        for core in range(2):
            table = [0] * count
            for index in range(count):
                total = 0
                for phase, bit in enumerate(bits[core]):
                    if index >> phase & 1:
                        total ^= bit // unit
                table[total] = index
            tables.append(table)
        tables = jnp.asarray(tables, jnp.int32)[self.core]
        stacked = jnp.stack(pieces)
        return [
            lax.dynamic_index_in_dim(
                stacked, lax.dynamic_index_in_dim(tables, place ^ at, 0, False), 0, False
            )
            for place in range(count)
        ]


def to_inner(rows, topo):
    count, width = rows.shape
    rest = width // topo.dp
    cut = rows.reshape(count, LINE, topo.square, rest).transpose(2, 0, 1, 3)
    cut = cut.reshape(topo.square, count, LINE * rest)
    return jnp.concatenate(
        [
            lax.dynamic_index_in_dim(cut, topo.square_at ^ i, 0, False)
            for i in range(topo.square)
        ],
        axis=1,
    )


def to_outer(rows, topo):
    count, width = rows.shape
    rest = width // topo.dp
    cut = rows.reshape(count, topo.square, LINE * rest).transpose(1, 0, 2)
    cut = jnp.stack(
        [
            lax.dynamic_index_in_dim(cut, topo.square_at ^ i, 0, False)
            for i in range(topo.square)
        ]
    )
    cut = cut.reshape(topo.square, count, LINE, rest).transpose(1, 2, 0, 3)
    return cut.reshape(count, width)


def dot(left, right):
    return jnp.dot(left, right, preferred_element_type=F32)


def dot_t(left, right):
    return lax.dot_general(left, right, (((1,), (1,)), ((), ())), preferred_element_type=F32)


def t_dot(left, right):
    return lax.dot_general(left, right, (((0,), (0,)), ((), ())), preferred_element_type=F32)


def attention_scores(queries, key_rows, allowed):
    score_scale = 1.0 / math.sqrt(queries.shape[-1])
    raw_scores = jnp.einsum("qgpd,kgd->gpqk", queries, key_rows, preferred_element_type=F32)
    return jnp.where(allowed[None, None], raw_scores * score_scale, MASKED)


def per_device(
    tokens,
    out_grad,
    lengths,
    attn_gain,
    q_weight,
    q_bias,
    k_weight,
    k_bias,
    v_weight,
    v_bias,
    o_weight,
    mlp_gain,
    gate_weight,
    up_weight,
    down_weight,
):
    topo = Topo()
    local_rows, width = tokens.shape
    group_rows = 2 * local_rows
    q_cols = q_weight.shape[1]
    kv_cols = k_weight.shape[1]
    qkv_cols = q_cols + 2 * kv_cols
    ff_cols = gate_weight.shape[1]
    part = -(-ff_cols // (LINE * LANES)) * LANES
    kv_groups = kv_cols // HEAD_DIM
    per_group = q_cols // HEAD_DIM // kv_groups
    score_scale = 1.0 / math.sqrt(HEAD_DIM)

    def line_gather(shard):
        pieces = jnp.split(topo.gather_joined(shard, topo.line), LINE, axis=0)
        return jnp.concatenate(topo.ordered(pieces, topo.line, topo.square, topo.line_at), axis=0)

    def square_gather(shard):
        pieces = topo.gather(shard, topo.squares)
        return jnp.concatenate(topo.ordered(pieces, topo.squares, 1, 0), axis=0)

    def square_scatter(grads):
        pieces = jnp.split(grads.astype(BF), topo.square, axis=0)
        by_index = topo.ordered(pieces, tuple(b for b in topo.squares), 1, 0)
        return topo.scatter_sum(jnp.concatenate(by_index, axis=0), topo.squares)

    def line_offset(index):
        return topo.line_at ^ topo.offset(topo.line, index, topo.square)

    def columns_in(shards):
        padded = [jnp.pad(s, ((0, 0), (0, LINE * part - ff_cols))) for s in shards]
        chunks = []
        for index in range(LINE):
            start = line_offset(index) * part
            chunks.append(
                jnp.concatenate(
                    [lax.dynamic_slice_in_dim(s, start, part, axis=1) for s in padded], axis=1
                )
            )
        got = topo.exchange(chunks, topo.line)
        return jnp.concatenate(topo.ordered(got, topo.line, topo.square, topo.line_at), axis=0)

    def columns_out(piece, count):
        rows = piece.shape[0] // LINE
        chunks = [
            lax.dynamic_slice_in_dim(piece, line_offset(index) * rows, rows, axis=0)
            for index in range(LINE)
        ]
        got = topo.ordered(
            topo.exchange(chunks, topo.line), topo.line, topo.square, topo.line_at
        )
        return [
            jnp.concatenate([g[:, i * part : (i + 1) * part] for g in got], axis=1)[
                :, :ff_cols
            ].astype(F32)
            for i in range(count)
        ]

    def rows_out(piece):
        rows = piece.shape[0] // LINE
        chunks = [
            lax.dynamic_slice_in_dim(piece, line_offset(index) * rows, rows, axis=0)
            for index in range(LINE)
        ]
        return topo.scatter_sum(jnp.concatenate(chunks, axis=0), topo.line).astype(F32)

    def both_cores(rows):
        return jnp.concatenate([rows, topo.other_core(rows)], axis=0)

    def core_sum(rows):
        half = rows.shape[0] // 2
        return rows[:half] + topo.other_core(rows[half:].astype(BF)).astype(F32)

    def line_tokens(rows):
        return both_cores(topo.gather_joined(rows, topo.line))

    def line_sum(partial):
        return topo.scatter_sum(core_sum(partial).astype(BF), topo.line).astype(F32)

    row_ids = jnp.arange(local_rows, dtype=jnp.int32)
    places = jnp.concatenate(
        [topo.core * local_rows + row_ids, (1 - topo.core) * local_rows + row_ids]
    )
    segment, positions = segment_info(lengths[0], places)
    allowed = (segment[:, None] == segment[None, :]) & (places[None, :] <= places[:, None])
    cosine_table, sine_table = rope_tables(positions, HEAD_DIM)
    q_cosine = cosine_table[:, None, None, :]
    q_sine = sine_table[:, None, None, :]
    k_cosine = cosine_table[:, None, :]
    k_sine = sine_table[:, None, :]

    inputs_low = to_inner(tokens, topo)
    out_grad_low = to_inner(out_grad, topo)
    gains = to_inner(jnp.stack([attn_gain, mlp_gain]), topo).astype(F32)
    gain_one, gain_two = gains[0], gains[1]
    inputs = inputs_low.astype(F32)
    bias_all = jnp.concatenate([q_bias, k_bias, v_bias]).astype(F32)

    qkv_local = jnp.concatenate([q_weight, k_weight, v_weight], axis=1)
    qkv_all = square_gather(line_gather(qkv_local))
    o_all = square_gather(line_gather(o_weight))
    down_all = square_gather(columns_in([down_weight]))
    grad_out_all = line_tokens(out_grad_low)
    gate_up = square_gather(columns_in([gate_weight, up_weight]))

    normed_one, factor_one = normalize(inputs)
    attn_in = both_cores((normed_one * gain_one[None, :]).astype(BF))
    linear = dot(attn_in, qkv_all) + bias_all[None, :]
    queries = rotate(
        linear[:, :q_cols].reshape(group_rows, kv_groups, per_group, HEAD_DIM), q_cosine, q_sine
    ).astype(BF)
    key_rows = rotate(
        linear[:, q_cols : q_cols + kv_cols].reshape(group_rows, kv_groups, HEAD_DIM),
        k_cosine,
        k_sine,
    ).astype(BF)
    values = linear[:, q_cols + kv_cols :].reshape(group_rows, kv_groups, HEAD_DIM).astype(BF)
    scores = attention_scores(queries, key_rows, allowed)
    row_peak = jnp.max(scores, axis=-1, keepdims=True)
    exponent = jnp.exp(scores - row_peak)
    row_mass = jnp.sum(exponent, axis=-1, keepdims=True)
    log_mass = row_peak + jnp.log(row_mass)
    probs_low = (exponent / row_mass).astype(BF)
    mixed_heads = jnp.einsum("gpqk,kgd->qgpd", probs_low, values, preferred_element_type=F32)
    mixed_heads = mixed_heads.reshape(group_rows, q_cols).astype(BF)
    hidden_state = inputs + core_sum(dot_t(mixed_heads, o_all))
    normed_two, factor_two = normalize(hidden_state)

    mlp_in = line_tokens((normed_two * gain_two[None, :]).astype(BF))
    grad_hidden = dot(grad_out_all, down_all)
    gate_up_out = dot(mlp_in, gate_up)
    gate_val = gate_up_out[:, :part]
    up_val = gate_up_out[:, part:]
    sigmoid_gate = jax.nn.sigmoid(gate_val)
    activated = gate_val * sigmoid_gate
    hidden_units = (activated * up_val).astype(BF)
    grad_gate = (
        grad_hidden * up_val * sigmoid_gate * (1.0 + gate_val * (1.0 - sigmoid_gate))
    ).astype(BF)
    grad_up = (grad_hidden * activated).astype(BF)
    grad_gate_up = jnp.concatenate([grad_gate, grad_up], axis=1)
    grad_normed_two = line_sum(dot_t(grad_gate_up, gate_up))
    block_out = (hidden_state + line_sum(dot_t(hidden_units, down_all))).astype(BF)
    gate_grads, up_grads = columns_out(square_scatter(t_dot(mlp_in, grad_gate_up)), 2)
    (down_grads,) = columns_out(square_scatter(t_dot(grad_out_all, hidden_units)), 1)

    back_two, gain_two_grad = norm_back(grad_normed_two, normed_two, factor_two, gain_two)
    grad_state = out_grad_low.astype(F32) + back_two
    grad_state_all = both_cores(grad_state.astype(BF))
    o_grads = rows_out(square_scatter(t_dot(grad_state_all, mixed_heads)))
    grad_mixed = dot(grad_state_all, o_all)
    grad_heads = grad_mixed.astype(BF).reshape(group_rows, kv_groups, per_group, HEAD_DIM)
    scores_again = attention_scores(queries, key_rows, allowed)
    prob_rows = jnp.exp(scores_again - log_mass)
    grad_probs = jnp.einsum("qgpd,kgd->gpqk", grad_heads, values, preferred_element_type=F32)
    row_inner = jnp.sum(prob_rows * grad_probs, axis=-1, keepdims=True)
    grad_scores = (prob_rows * (grad_probs - row_inner) * score_scale).astype(BF)
    grad_values = jnp.einsum(
        "gpqk,qgpd->kgd", prob_rows.astype(BF), grad_heads, preferred_element_type=F32
    )
    grad_queries = jnp.einsum("gpqk,kgd->qgpd", grad_scores, key_rows, preferred_element_type=F32)
    grad_keys = jnp.einsum("gpqk,qgpd->kgd", grad_scores, queries, preferred_element_type=F32)
    grad_linear = jnp.concatenate(
        [
            unrotate(grad_queries, q_cosine, q_sine).reshape(group_rows, q_cols),
            unrotate(grad_keys, k_cosine, k_sine).reshape(group_rows, kv_cols),
            grad_values.reshape(group_rows, kv_cols),
        ],
        axis=1,
    ).astype(BF)
    bias_grad = jnp.sum(grad_linear.astype(F32), axis=0)
    qkv_grads = rows_out(square_scatter(t_dot(attn_in, grad_linear)))
    grad_normed_one = core_sum(dot_t(grad_linear, qkv_all))
    back_one, gain_one_grad = norm_back(grad_normed_one, normed_one, factor_one, gain_one)
    tokens_grad = (grad_state + back_one).astype(BF)
    gain_grads = to_outer(jnp.stack([gain_one_grad, gain_two_grad]), topo)
    gain_grads = gain_grads + topo.other_core(gain_grads)
    small = topo.total(jnp.concatenate([bias_grad, gain_grads.reshape(-1)]).reshape(-1, LANES))
    small = small.reshape(-1)
    own_bias = small[:qkv_cols]
    gain_sum = small[qkv_cols:].reshape(2, width)
    return (
        to_outer(block_out, topo),
        to_outer(tokens_grad, topo),
        gain_sum[0],
        qkv_grads[:, :q_cols],
        own_bias[:q_cols],
        qkv_grads[:, q_cols : q_cols + kv_cols],
        own_bias[q_cols : q_cols + kv_cols],
        qkv_grads[:, q_cols + kv_cols : qkv_cols],
        own_bias[q_cols + kv_cols :],
        o_grads,
        gain_sum[1],
        gate_grads,
        up_grads,
        down_grads,
    )


def solution(mesh):
    rows = P(("dp", "tensor"), None)
    both = P("dp", "tensor")
    half = P("tensor")
    in_specs = (
        rows, rows, P("dp", None), P(), both, half, both, half, both, half, both, P(), both, both, both,
    )
    out_specs = (
        rows, rows, P(), both, half, both, half, both, half, both, P(), both, both, both,
    )
    return jax.shard_map(
        per_device, mesh=mesh, in_specs=in_specs, out_specs=out_specs, check_vma=False
    )
```

time: 2170 us -> 636 us (0.29)
  waiting for transfers between devices: 1870 us -> 246 us
  starting transfers between devices: 1.58 us -> 82.9 us
  blocking collectives: 40.8 us -> 0 us
  other arithmetic: 39.3 us -> 77.1 us
    reduce_scatter x6 -> x0, waiting for transfers between devices: 804 us -> none  [the longest x2 788 us: reduce_ff(): lax.psum_scatter(term_maker(grad_pairs), 'dp', scatter_dimension=0, tiled...]
    all_gather x8 -> x0, waiting for transfers between devices: 602 us -> none  [the longest x2 371 us: rows_product(): lax.all_gather(stacked, 'dp', axis=0, tiled=True)]
    unnamed x18 -> x0, waiting for transfers between devices: 461 us -> none
    ppermute x0 -> x57, waiting for transfers between devices: none -> 246 us  [the longest x48 245 us: swap(): return lax.ppermute(array, ('dp', 'tensor'), perm)]
    ppermute x0 -> x57, starting transfers between devices: none -> 82.9 us  [the longest x48 78.8 us: swap(): return lax.ppermute(array, ('dp', 'tensor'), perm)]
    psum x1 -> x0, blocking collectives: 40.8 us -> none  [per_device(): lax.psum((bias_table, jnp.stack([gain_one_grad, gain_two_grad])), ('dp',...]
    unnamed x108 -> x216, local copies, waits for them, and re-layouts: 50 us -> 14.3 us
    dot_general x17 -> x16, matrix products: 140 us -> 124 us  [the longest x4 49.5 us: dot(): return jnp.dot(left, right, preferred_element_type=F32)]
  transfers between devices with their start and end apart: 16 -> 57, of which waited for: 13 -> 26; matrix products, arithmetic and copies ran while one was open for 8% -> 35% of each run, Pallas kernels for 0% -> 0%
where the time goes in v1:
time: 636 us; the launch traced here: 627 us
  waiting for transfers between devices  246 us (39%)
  matrix products  126 us (20%)
  starting transfers between devices  82.9 us (13%)
  other arithmetic  77.1 us (12%)
  local copies, waits for them, and re-layouts  77 us (12%)
  between operations  18.6 us (3%)
    ppermute x48, waiting for transfers between devices, swap(): return lax.ppermute(array, ('dp', 'tensor'), perm)  245 us
    ppermute x48, starting transfers between devices, swap(): return lax.ppermute(array, ('dp', 'tensor'), perm)  78.8 us
    dot_general x4, matrix products, dot(): return jnp.dot(left, right, preferred_element_type=F32)  49.5 us
    dot_general x4, matrix products, dot_t(): lax.dot_general(left, right, (((1,), (1,)), ((), ())), preferred_element_...  34.4 us
    dot_general x4, matrix products, t_dot(): lax.dot_general(left, right, (((0,), (0,)), ((), ())), preferred_element_...  32.5 us
    another operation x19, other arithmetic, ordered(): stacked = jnp.stack(pieces)  14.9 us
    unnamed x216, local copies, waits for them, and re-layouts  14.3 us
  transfers between devices with their start and end apart: 57, of which 26 were waited for; matrix products, arithmetic and copies ran while one was open for 35% of the time, Pallas kernels for 0%

profile of v1, /device:TPU:0, one launch (start us, length us, event | category | flops | bytes accessed | tf_op | source)
XLA Modules:
  0.0 627.0 jit_solution(15613531388393741111)
XLA Ops:
  52.5 7.4 %collective-permute-done.7 = bf16[192,768]{1,0:T(8,128)(2,1)S(1)} collective-permute-done((bf16[192,768]{1,0:T(8,128)(2,1)S(1)}, bf16[192,768]{1,0:T(8,128)(2,1)S(1)}, u32[]{:S(2)}, u32[]{:S(2)}) %collective-permute-start.7) | collective-permute-done | bytes 294944 | tf_op jit(solution)/shard_map/ppermute | solution.py:80
  63.9 18.8 %collective-permute-done.2 = bf16[192,1024]{1,0:T(8,128)(2,1)S(1)} collective-permute-done((bf16[192,1024]{1,0:T(8,128)(2,1)S(1)}, bf16[192,1024]{1,0:T(8,128)(2,1)S(1)}, u32[]{:S(2)}, u32[]{:S(2)}) %collective-permute-start.2) | collective-permute-done | bytes 393248 | tf_op jit(solution)/shard_map/ppermute | solution.py:80
  91.9 5.9 collective-permute-done.21
  112.8 6.9 %collective-permute-done.16 = bf16[192,2304]{1,0:T(8,128)(2,1)S(1)} collective-permute-done((bf16[192,2304]{1,0:T(8,128)(2,1)S(1)}, bf16[192,2304]{1,0:T(8,128)(2,1)S(1)}, u32[]{:S(2)}, u32[]{:S(2)}) %collective-permute-start.16) | collective-permute-done | bytes 884768 | tf_op jit(solution)/shard_map/ppermute | solution.py:80
  120.0 6.3 %collective-permute-done.5 = bf16[384,1024]{1,0:T(8,128)(2,1)S(1)} collective-permute-done((bf16[384,1024]{1,0:T(8,128)(2,1)S(1)}, bf16[384,1024]{1,0:T(8,128)(2,1)S(1)}, u32[]{:S(2)}, u32[]{:S(2)}) %collective-permute-start.5) | collective-permute-done | bytes 786464 | tf_op jit(solution)/shard_map/ppermute | solution.py:80
  154.0 4.7 collective-permute-start.12
  160.9 8.9 %collective-permute-done.12 = bf16[192,1536]{1,0:T(8,128)(2,1)S(1)} collective-permute-done((bf16[192,1536]{1,0:T(8,128)(2,1)S(1)}, bf16[192,1536]{1,0:T(8,128)(2,1)S(1)}, u32[]{:S(2)}, u32[]{:S(2)}) %collective-permute-start.12) | collective-permute-done | bytes 589856 | tf_op jit(solution)/shard_map/ppermute | solution.py:80
  175.1 13.9 %collective-permute-done.22 = bf16[384,1152]{1,0:T(8,128)(2,1)} collective-permute-done((bf16[384,1152]{1,0:T(8,128)(2,1)}, bf16[384,1152]{1,0:T(8,128)(2,1)}, u32[]{:S(2)}, u32[]{:S(2)}) %collective-permute-start.22) | collective-permute-done | bytes 884768 | tf_op jit(solution)/shard_map/ppermute | solution.py:80
  192.3 4.4 pad_maximum_fusion.18
  197.4 4.4 collective-permute-done.13
  203.8 17.4 %collective-permute-done.24 = bf16[384,1152]{1,0:T(8,128)(2,1)S(1)} collective-permute-done((bf16[384,1152]{1,0:T(8,128)(2,1)}, bf16[384,1152]{1,0:T(8,128)(2,1)S(1)}, u32[]{:S(2)}, u32[]{:S(2)}) %collective-permute-start.24) | collective-permute-done | bytes 884768 | tf_op jit(solution)/shard_map/ppermute | solution.py:80
  224.7 15.5 %collective-permute-done.19 = bf16[384,2304]{1,0:T(8,128)(2,1)S(1)} collective-permute-done((bf16[384,2304]{1,0:T(8,128)(2,1)}, bf16[384,2304]{1,0:T(8,128)(2,1)S(1)}, u32[]{:S(2)}, u32[]{:S(2)}) %collective-permute-start.19) | collective-permute-done | bytes 1769504 | tf_op jit(solution)/shard_map/ppermute | solution.py:80
  246.8 19.8 %fusion.26 = f32[1536,2304]{1,0:T(8,128)} fusion(bf16[384,2304]{1,0:T(8,128)(2,1)S(1)} %get-tuple-element.36, bf16[384,2304]{1,0:T(8,128)(2,1)} %get-tuple-element.37, bf16[384,2304]{1,0:T(8,128)(2,1)} %get-tuple-element.38, bf16[384,2304]{1,0:T(8,128)(2,1)S(1)} %get-tuple-element.35, bf16[768,1536]{1,0:T(8,128)(2,1)} %copy-done.94, ...), kind=kOutput, calls=%fused_computation.94 | convolution fusion | flops 10918821888 | bytes 25952256 | tf_op jit(solution)/shard_map/dot_general | solution.py:184
  266.6 22.2 %multiply_convert_fusion.1 = (bf16[1536,1152]{1,0:T(8,128)(2,1)}, bf16[1536,1152]{1,0:T(8,128)(2,1)}, bf16[1536,1152]{1,0:T(8,128)(2,1)}) fusion(f32[1536,2304]{1,0:T(8,128)} %fusion.26, bf16[384,1152]{1,0:T(8,128)(2,1)} %get-tuple-element.48, bf16[384,1152]{1,0:T(8,128)(2,1)} %get-tuple-element.49, bf16[384,1152]{1,0:T(8,128)(2,1)} %get-tuple-element.50, ...), kind=kOutput, calls=%fused_computation.8 | convolution fusion | flops 5509545984 | bytes 33030144 | tf_op jit(solution)/shard_map/dot_general | solution.py:184
  288.8 12.0 %fusion.52 = f32[1536,1536]{1,0:T(8,128)} fusion(bf16[1536,1152]{1,0:T(8,128)(2,1)} %get-tuple-element.26, bf16[384,1152]{1,0:T(8,128)(2,1)S(1)} %copy-done.56, bf16[384,1152]{1,0:T(8,128)(2,1)} %get-tuple-element.49, bf16[384,1152]{1,0:T(8,128)(2,1)} %get-tuple-element.50, bf16[384,1152]{1,0:T(8,128)(2,1)S(1)} %copy-done.55), kind=kOutput, calls=%fused_computation.192 | convolution fusion | flops 5449973760 | bytes 16515072 | tf_op jit(solution)/shard_map/dot_general | solution.py:188
  300.8 11.3 %convolution_convert_fusion.1 = bf16[1536,1152]{1,0:T(8,128)(2,1)S(1)} fusion(bf16[1536,1152]{1,0:T(8,128)(2,1)S(1)} %copy-done.98, bf16[768,1536]{1,0:T(8,128)(2,1)} %collective-permute-done.30, bf16[384,1536]{1,0:T(8,128)(2,1)} %collective-permute-done.29, bf16[192,1536]{1,0:T(8,128)(2,1)S(1)} %copy-done.36, bf16[192,384]{1,0:T(8,128)(2,1)S(1)} %copy-done.24, ...), kind=kOutput, calls=%fused_computation.1 | convolution fusion | flops 5470617600 | bytes 11796480 | tf_op jit(solution)/shard_map/dot_general | solution.py:192
  317.1 18.4 %fusion.3 = f32[1536,1536]{1,0:T(8,128)} fusion(bf16[1536,1152]{1,0:T(8,128)(2,1)} %get-tuple-element.25, bf16[1536,1152]{1,0:T(8,128)(2,1)} %get-tuple-element.24, bf16[384,2304]{1,0:T(8,128)(2,1)} %copy-done.46, bf16[384,2304]{1,0:T(8,128)(2,1)} %get-tuple-element.37, bf16[384,2304]{1,0:T(8,128)(2,1)} %get-tuple-element.38, bf16[384,2304]{1,0:T(8,128)(2,1)} %copy-done.45), kind=kOutput, calls=%fused_computation.20 | convolution fusion | flops 10914103296 | bytes 23592960 | tf_op jit(solution)/shard_map/dot_general | solution.py:188
  335.6 15.3 %convolution_convert_fusion = bf16[1536,2304]{1,0:T(8,128)(2,1)S(1)} fusion(bf16[1536,1152]{1,0:T(8,128)(2,1)} %get-tuple-element.25, bf16[1536,1152]{1,0:T(8,128)(2,1)} %get-tuple-element.24, bf16[768,1536]{1,0:T(8,128)(2,1)} %copy-done.94, bf16[384,1536]{1,0:T(8,128)(2,1)} %collective-permute-done.13, bf16[192,1536]{1,0:T(8,128)(2,1)S(1)} %copy-done.39, ...), kind=kOutput, calls=%fused_computation | convolution fusion | flops 10908205056 | bytes 18874368 | tf_op jit(solution)/shard_map/dot_general | solution.py:192
  370.9 4.4 collective-permute-start.32
  375.3 10.0 %collective-permute-done.54 = bf16[384,1152]{1,0:T(8,128)(2,1)S(1)} collective-permute-done((bf16[384,1152]{1,0:T(8,128)(2,1)S(1)}, bf16[384,1152]{1,0:T(8,128)(2,1)S(1)}, u32[]{:S(2)}, u32[]{:S(2)}) %collective-permute-start.54) | collective-permute-done | bytes 884768 | tf_op jit(solution)/shard_map/ppermute | solution.py:80
  385.6 7.9 %collective-permute-start.55 = (bf16[192,1152]{1,0:T(8,128)(2,1)S(1)}, bf16[192,1152]{1,0:T(8,128)(2,1)S(1)}, u32[]{:S(2)}, u32[]{:S(2)}) collective-permute-start(bf16[192,1152]{1,0:T(8,128)(2,1)S(1)} %pad_maximum_fusion.68), channel_id=1, source_target_pairs={{0,8},{1,17},{2,10},{3,19},{4,12},{5,21},{6,14},{7,23},{8,0},{9,25... | collective-permute-start | bytes 1327112 | tf_op jit(solution)/shard_map/ppermute | solution.py:80
  396.3 13.1 %collective-permute-done.55 = bf16[192,1152]{1,0:T(8,128)(2,1)S(1)} collective-permute-done((bf16[192,1152]{1,0:T(8,128)(2,1)S(1)}, bf16[192,1152]{1,0:T(8,128)(2,1)S(1)}, u32[]{:S(2)}, u32[]{:S(2)}) %collective-permute-start.55) | collective-permute-done | bytes 442400 | tf_op jit(solution)/shard_map/ppermute | solution.py:80
  409.5 8.3 %collective-permute-start.56 = (bf16[192,1152]{1,0:T(8,128)(2,1)S(1)}, bf16[192,1152]{1,0:T(8,128)(2,1)S(1)}, u32[]{:S(2)}, u32[]{:S(2)}) collective-permute-start(bf16[192,1152]{1,0:T(8,128)(2,1)S(1)} %pad_maximum_fusion.69), channel_id=1, source_target_pairs={{0,16},{1,9},{2,18},{3,11},{4,20},{5,13},{6,22},{7,15},{8,24},{9,1... | collective-permute-start | bytes 1327112 | tf_op jit(solution)/shard_map/ppermute | solution.py:80
  422.6 29.7 %collective-permute-done.26 = bf16[384,1536]{1,0:T(8,128)(2,1)S(1)} collective-permute-done((bf16[384,1536]{1,0:T(8,128)(2,1)S(1)}, bf16[384,1536]{1,0:T(8,128)(2,1)S(1)}, u32[]{:S(2)}, u32[]{:S(2)}) %collective-permute-start.26) | collective-permute-done | bytes 1179680 | tf_op jit(solution)/shard_map/ppermute | solution.py:80
  452.7 17.1 %collective-permute-done.56 = bf16[192,1152]{1,0:T(8,128)(2,1)S(1)} collective-permute-done((bf16[192,1152]{1,0:T(8,128)(2,1)S(1)}, bf16[192,1152]{1,0:T(8,128)(2,1)S(1)}, u32[]{:S(2)}, u32[]{:S(2)}) %collective-permute-start.56) | collective-permute-done | bytes 442400 | tf_op jit(solution)/shard_map/ppermute | solution.py:80
  524.9 11.6 %collective-permute-done.37 = f32[32,128]{1,0:T(8,128)S(1)} collective-permute-done((f32[32,128]{1,0:T(8,128)S(1)}, f32[32,128]{1,0:T(8,128)S(1)}, u32[]{:S(2)}, u32[]{:S(2)}) %collective-permute-start.37) | collective-permute-done | bytes 16416 | tf_op jit(solution)/shard_map/ppermute | solution.py:80
  561.5 7.8 %collective-permute-done.46 = bf16[384,768]{1,0:T(8,128)(2,1)S(1)} collective-permute-done((bf16[384,768]{1,0:T(8,128)(2,1)S(1)}, bf16[384,768]{1,0:T(8,128)(2,1)S(1)}, u32[]{:S(2)}, u32[]{:S(2)}) %collective-permute-start.46) | collective-permute-done | bytes 589856 | tf_op jit(solution)/shard_map/ppermute | solution.py:80
  573.1 7.3 %collective-permute-done.47 = bf16[192,768]{1,0:T(8,128)(2,1)S(1)} collective-permute-done((bf16[192,768]{1,0:T(8,128)(2,1)S(1)}, bf16[192,768]{1,0:T(8,128)(2,1)S(1)}, u32[]{:S(2)}, u32[]{:S(2)}) %collective-permute-start.47) | collective-permute-done | bytes 294944 | tf_op jit(solution)/shard_map/ppermute | solution.py:80
  585.9 11.3 %collective-permute-done.48 = bf16[96,768]{1,0:T(8,128)(2,1)S(1)} collective-permute-done((bf16[96,768]{1,0:T(8,128)(2,1)S(1)}, bf16[96,768]{1,0:T(8,128)(2,1)S(1)}, u32[]{:S(2)}, u32[]{:S(2)}) %collective-permute-start.48) | collective-permute-done | bytes 147488 | tf_op jit(solution)/shard_map/ppermute | solution.py:80
  597.9 4.7 collective-permute-done.52
  605.1 14.5 %collective-permute-done.43 = bf16[192,1024]{1,0:T(8,128)(2,1)S(1)} collective-permute-done((bf16[192,1024]{1,0:T(8,128)(2,1)S(1)}, bf16[192,1024]{1,0:T(8,128)(2,1)S(1)}, u32[]{:S(2)}, u32[]{:S(2)}) %collective-permute-start.43) | collective-permute-done | bytes 393248 | tf_op jit(solution)/shard_map/ppermute | solution.py:80
  621.1 4.4 collective-permute-done.44
  (526 shorter events, 243.1 us)
Async XLA Ops:
  0.6 44.8 %collective-permute-start.6 = (bf16[96,768]{1,0:T(8,128)(2,1)}, bf16[96,768]{1,0:T(8,128)(2,1)}, u32[]{:S(2)}, u32[]{:S(2)}) collective-permute-start(bf16[96,768]{1,0:T(8,128)(2,1)} %param.39), channel_id=1, source_target_pairs={{0,8},{1,17},{2,10},{3,19},{4,12},{5,21},{6,14},{7,23},{8,0},{9,25... | collective-permute-start | bytes 442376 | tf_op jit(solution)/shard_map/ppermute | solution.py:80
  6.2 43.8 %collective-permute-start.1 = (bf16[96,1024]{1,0:T(8,128)(2,1)S(1)}, bf16[96,1024]{1,0:T(8,128)(2,1)}, u32[]{:S(2)}, u32[]{:S(2)}) collective-permute-start(bf16[96,1024]{1,0:T(8,128)(2,1)S(1)} %constant_dynamic-update-slice_fusion), channel_id=1, source_target_pairs={{0,8},{1,17},{2,10},{3,19},{4,12},{5,21},{6,14},{7,23},{8,0},{9,25... | collective-permute-start | bytes 589832 | tf_op jit(solution)/shard_map/ppermute | solution.py:80
  12.4 115.2 %collective-permute-start = (bf16[192,1536]{1,0:T(8,128)(2,1)}, bf16[192,1536]{1,0:T(8,128)(2,1)}, u32[]{:S(2)}, u32[]{:S(2)}) collective-permute-start(bf16[192,1536]{1,0:T(8,128)(2,1)} %fusion.31), channel_id=1, source_target_pairs={{0,1},{1,0},{2,3},{3,2},{4,5},{5,4},{6,7},{7,6},{8,9},{9,8},{10,11... | collective-permute-start | bytes 1769480 | tf_op jit(solution)/shard_map/ppermute | solution.py:83
  15.6 70.0 %collective-permute-start.28 = (bf16[192,1536]{1,0:T(8,128)(2,1)}, bf16[192,1536]{1,0:T(8,128)(2,1)S(1)}, u32[]{:S(2)}, u32[]{:S(2)}) collective-permute-start(bf16[192,1536]{1,0:T(8,128)(2,1)} %pad_maximum_fusion.62), channel_id=1, source_target_pairs={{0,8},{1,17},{2,10},{3,19},{4,12},{5,21},{6,14},{7,23},{8,0},{9,25... | collective-permute-start | bytes 1769480 | tf_op jit(solution)/shard_map/ppermute | solution.py:80
  19.3 41.9 %collective-permute-start.20 = (bf16[192,1152]{1,0:T(8,128)(2,1)}, bf16[192,1152]{1,0:T(8,128)(2,1)}, u32[]{:S(2)}, u32[]{:S(2)}) collective-permute-start(bf16[192,1152]{1,0:T(8,128)(2,1)} %pad_maximum_fusion.66), channel_id=1, source_target_pairs={{0,8},{1,17},{2,10},{3,19},{4,12},{5,21},{6,14},{7,23},{8,0},{9,25... | collective-permute-start | bytes 1327112 | tf_op jit(solution)/shard_map/ppermute | solution.py:80
  50.0 40.3 %collective-permute-start.15 = (bf16[192,2304]{1,0:T(8,128)(2,1)}, bf16[192,2304]{1,0:T(8,128)(2,1)S(1)}, u32[]{:S(2)}, u32[]{:S(2)}) collective-permute-start(bf16[192,2304]{1,0:T(8,128)(2,1)} %maximum_maximum_fusion), channel_id=1, source_target_pairs={{0,8},{1,17},{2,10},{3,19},{4,12},{5,21},{6,14},{7,23},{8,0},{9,25... | collective-permute-start | bytes 2654216 | tf_op jit(solution)/shard_map/ppermute | solution.py:80
  59.9 22.8 %collective-permute-start.2 = (bf16[192,1024]{1,0:T(8,128)(2,1)S(1)}, bf16[192,1024]{1,0:T(8,128)(2,1)S(1)}, u32[]{:S(2)}, u32[]{:S(2)}) collective-permute-start(bf16[192,1024]{1,0:T(8,128)(2,1)S(1)} %pad_maximum_fusion.72), channel_id=1, source_target_pairs={{0,16},{1,9},{2,18},{3,11},{4,20},{5,13},{6,22},{7,15},{8,24},{9,1... | collective-permute-start | bytes 1179656 | tf_op jit(solution)/shard_map/ppermute | solution.py:80
  61.2 38.4 %collective-permute-start.8 = (bf16[384,768]{1,0:T(8,128)(2,1)S(1)}, bf16[384,768]{1,0:T(8,128)(2,1)S(1)}, u32[]{:S(2)}, u32[]{:S(2)}) collective-permute-start(bf16[384,768]{1,0:T(8,128)(2,1)S(1)} %get-tuple-element.157), channel_id=1, source_target_pairs={{0,2},{1,5},{2,0},{3,7},{4,6},{5,1},{6,4},{7,3},{8,10},{9,13},{10,... | collective-permute-start | bytes 1769480 | tf_op jit(solution)/shard_map/ppermute | solution.py:80
  106.0 84.3 %collective-permute-start.29 = (bf16[384,1536]{1,0:T(8,128)(2,1)}, bf16[384,1536]{1,0:T(8,128)(2,1)}, u32[]{:S(2)}, u32[]{:S(2)}) collective-permute-start(bf16[384,1536]{1,0:T(8,128)(2,1)} %pad_maximum_fusion.29), channel_id=1, source_target_pairs={{0,16},{1,9},{2,18},{3,11},{4,20},{5,13},{6,22},{7,15},{8,24},{9,1... | collective-permute-start | bytes 3538952 | tf_op jit(solution)/shard_map/ppermute | solution.py:80
  150.3 40.7 %collective-permute-start.17 = (bf16[384,2304]{1,0:T(8,128)(2,1)}, bf16[384,2304]{1,0:T(8,128)(2,1)}, u32[]{:S(2)}, u32[]{:S(2)}) collective-permute-start(bf16[384,2304]{1,0:T(8,128)(2,1)} %get-tuple-element.86), channel_id=1, source_target_pairs={{0,2},{1,5},{2,0},{3,7},{4,6},{5,1},{6,4},{7,3},{8,10},{9,13},{10,... | collective-permute-start | bytes 5308424 | tf_op jit(solution)/shard_map/ppermute | solution.py:80
  160.2 28.8 %collective-permute-start.22 = (bf16[384,1152]{1,0:T(8,128)(2,1)}, bf16[384,1152]{1,0:T(8,128)(2,1)}, u32[]{:S(2)}, u32[]{:S(2)}) collective-permute-start(bf16[384,1152]{1,0:T(8,128)(2,1)} %get-tuple-element.109), channel_id=1, source_target_pairs={{0,2},{1,5},{2,0},{3,7},{4,6},{5,1},{6,4},{7,3},{8,10},{9,13},{10,... | collective-permute-start | bytes 2654216 | tf_op jit(solution)/shard_map/ppermute | solution.py:80
  171.7 30.1 %collective-permute-start.13 = (bf16[384,1536]{1,0:T(8,128)(2,1)}, bf16[384,1536]{1,0:T(8,128)(2,1)}, u32[]{:S(2)}, u32[]{:S(2)}) collective-permute-start(bf16[384,1536]{1,0:T(8,128)(2,1)} %pad_maximum_fusion.28), channel_id=1, source_target_pairs={{0,16},{1,9},{2,18},{3,11},{4,20},{5,13},{6,22},{7,15},{8,24},{9,1... | collective-permute-start | bytes 3538952 | tf_op jit(solution)/shard_map/ppermute | solution.py:80
  174.3 28.9 %collective-permute-start.23 = (bf16[384,1152]{1,0:T(8,128)(2,1)}, bf16[384,1152]{1,0:T(8,128)(2,1)S(1)}, u32[]{:S(2)}, u32[]{:S(2)}) collective-permute-start(bf16[384,1152]{1,0:T(8,128)(2,1)} %get-tuple-element.109), channel_id=1, source_target_pairs={{0,4},{1,3},{2,6},{3,1},{4,0},{5,7},{6,2},{7,5},{8,12},{9,11},{10,... | collective-permute-start | bytes 2654216 | tf_op jit(solution)/shard_map/ppermute | solution.py:80
  189.0 35.7 %collective-permute-start.18 = (bf16[384,2304]{1,0:T(8,128)(2,1)}, bf16[384,2304]{1,0:T(8,128)(2,1)S(1)}, u32[]{:S(2)}, u32[]{:S(2)}) collective-permute-start(bf16[384,2304]{1,0:T(8,128)(2,1)} %get-tuple-element.86), channel_id=1, source_target_pairs={{0,4},{1,3},{2,6},{3,1},{4,0},{5,7},{6,2},{7,5},{8,12},{9,11},{10,... | collective-permute-start | bytes 5308424 | tf_op jit(solution)/shard_map/ppermute | solution.py:80
  190.3 30.9 %collective-permute-start.24 = (bf16[384,1152]{1,0:T(8,128)(2,1)}, bf16[384,1152]{1,0:T(8,128)(2,1)S(1)}, u32[]{:S(2)}, u32[]{:S(2)}) collective-permute-start(bf16[384,1152]{1,0:T(8,128)(2,1)} %collective-permute-done.22), channel_id=1, source_target_pairs={{0,4},{1,3},{2,6},{3,1},{4,0},{5,7},{6,2},{7,5},{8,12},{9,11},{10,... | collective-permute-start | bytes 2654216 | tf_op jit(solution)/shard_map/ppermute | solution.py:80
  191.0 49.1 %collective-permute-start.19 = (bf16[384,2304]{1,0:T(8,128)(2,1)}, bf16[384,2304]{1,0:T(8,128)(2,1)S(1)}, u32[]{:S(2)}, u32[]{:S(2)}) collective-permute-start(bf16[384,2304]{1,0:T(8,128)(2,1)} %collective-permute-done.17), channel_id=1, source_target_pairs={{0,4},{1,3},{2,6},{3,1},{4,0},{5,7},{6,2},{7,5},{8,12},{9,11},{10,... | collective-permute-start | bytes 5308424 | tf_op jit(solution)/shard_map/ppermute | solution.py:80
  201.8 64.7 %collective-permute-start.30 = (bf16[768,1536]{1,0:T(8,128)(2,1)S(1)}, bf16[768,1536]{1,0:T(8,128)(2,1)}, u32[]{:S(2)}, u32[]{:S(2)}) collective-permute-start(bf16[768,1536]{1,0:T(8,128)(2,1)S(1)} %pad_maximum_fusion.18), channel_id=1, source_target_pairs={{0,1},{1,0},{2,3},{3,2},{4,5},{5,4},{6,7},{7,6},{8,9},{9,8},{10,11... | collective-permute-start | bytes 7077896 | tf_op jit(solution)/shard_map/ppermute | solution.py:83
  203.3 42.1 %collective-permute-start.14 = (bf16[768,1536]{1,0:T(8,128)(2,1)S(1)}, bf16[768,1536]{1,0:T(8,128)(2,1)S(1)}, u32[]{:S(2)}, u32[]{:S(2)}) collective-permute-start(bf16[768,1536]{1,0:T(8,128)(2,1)S(1)} %pad_maximum_fusion.17), channel_id=1, source_target_pairs={{0,1},{1,0},{2,3},{3,2},{4,5},{5,4},{6,7},{7,6},{8,9},{9,8},{10,11... | collective-permute-start | bytes 7077896 | tf_op jit(solution)/shard_map/ppermute | solution.py:83
  315.9 44.3 %collective-permute-start.53 = (bf16[768,1152]{1,0:T(8,128)(2,1)}, bf16[768,1152]{1,0:T(8,128)(2,1)}, u32[]{:S(2)}, u32[]{:S(2)}) collective-permute-start(bf16[768,1152]{1,0:T(8,128)(2,1)} %pad_maximum_fusion.23), channel_id=1, source_target_pairs={{0,4},{1,3},{2,6},{3,1},{4,0},{5,7},{6,2},{7,5},{8,12},{9,11},{10,... | collective-permute-start | bytes 5308424 | tf_op jit(solution)/shard_map/ppermute | solution.py:80
  358.0 35.5 %collective-permute-start.25 = (bf16[768,1536]{1,0:T(8,128)(2,1)S(1)}, bf16[768,1536]{1,0:T(8,128)(2,1)}, u32[]{:S(2)}, u32[]{:S(2)}) collective-permute-start(bf16[768,1536]{1,0:T(8,128)(2,1)S(1)} %slice.469), channel_id=1, source_target_pairs={{0,1},{1,0},{2,3},{3,2},{4,5},{5,4},{6,7},{7,6},{8,9},{9,8},{10,11... | collective-permute-start | bytes 7077896 | tf_op jit(solution)/shard_map/ppermute | solution.py:83
  363.2 22.1 %collective-permute-start.54 = (bf16[384,1152]{1,0:T(8,128)(2,1)S(1)}, bf16[384,1152]{1,0:T(8,128)(2,1)S(1)}, u32[]{:S(2)}, u32[]{:S(2)}) collective-permute-start(bf16[384,1152]{1,0:T(8,128)(2,1)S(1)} %slice.390), channel_id=1, source_target_pairs={{0,2},{1,5},{2,0},{3,7},{4,6},{5,1},{6,4},{7,3},{8,10},{9,13},{10,... | collective-permute-start | bytes 2654216 | tf_op jit(solution)/shard_map/ppermute | solution.py:80
  364.7 54.8 %collective-permute-start.49 = (bf16[768,2304]{1,0:T(8,128)(2,1)S(1)}, bf16[768,2304]{1,0:T(8,128)(2,1)S(1)}, u32[]{:S(2)}, u32[]{:S(2)}) collective-permute-start(bf16[768,2304]{1,0:T(8,128)(2,1)S(1)} %pad_maximum_fusion.10), channel_id=1, source_target_pairs={{0,4},{1,3},{2,6},{3,1},{4,0},{5,7},{6,2},{7,5},{8,12},{9,11},{10,... | collective-permute-start | bytes 10616840 | tf_op jit(solution)/shard_map/ppermute | solution.py:80
  370.9 46.9 %collective-permute-start.32 = (bf16[384,1536]{1,0:T(8,128)(2,1)S(1)}, bf16[384,1536]{1,0:T(8,128)(2,1)}, u32[]{:S(2)}, u32[]{:S(2)}) collective-permute-start(bf16[384,1536]{1,0:T(8,128)(2,1)S(1)} %slice.354), channel_id=1, source_target_pairs={{0,16},{1,9},{2,18},{3,11},{4,20},{5,13},{6,22},{7,15},{8,24},{9,1... | collective-permute-start | bytes 3538952 | tf_op jit(solution)/shard_map/ppermute | solution.py:80
  385.6 23.8 %collective-permute-start.55 = (bf16[192,1152]{1,0:T(8,128)(2,1)S(1)}, bf16[192,1152]{1,0:T(8,128)(2,1)S(1)}, u32[]{:S(2)}, u32[]{:S(2)}) collective-permute-start(bf16[192,1152]{1,0:T(8,128)(2,1)S(1)} %pad_maximum_fusion.68), channel_id=1, source_target_pairs={{0,8},{1,17},{2,10},{3,19},{4,12},{5,21},{6,14},{7,23},{8,0},{9,25... | collective-permute-start | bytes 1327112 | tf_op jit(solution)/shard_map/ppermute | solution.py:80
  396.2 56.1 %collective-permute-start.26 = (bf16[384,1536]{1,0:T(8,128)(2,1)S(1)}, bf16[384,1536]{1,0:T(8,128)(2,1)S(1)}, u32[]{:S(2)}, u32[]{:S(2)}) collective-permute-start(bf16[384,1536]{1,0:T(8,128)(2,1)S(1)} %slice.348), channel_id=1, source_target_pairs={{0,16},{1,9},{2,18},{3,11},{4,20},{5,13},{6,22},{7,15},{8,24},{9,1... | collective-permute-start | bytes 3538952 | tf_op jit(solution)/shard_map/ppermute | solution.py:80
  409.5 60.3 %collective-permute-start.56 = (bf16[192,1152]{1,0:T(8,128)(2,1)S(1)}, bf16[192,1152]{1,0:T(8,128)(2,1)S(1)}, u32[]{:S(2)}, u32[]{:S(2)}) collective-permute-start(bf16[192,1152]{1,0:T(8,128)(2,1)S(1)} %pad_maximum_fusion.69), channel_id=1, source_target_pairs={{0,16},{1,9},{2,18},{3,11},{4,20},{5,13},{6,22},{7,15},{8,24},{9,1... | collective-permute-start | bytes 1327112 | tf_op jit(solution)/shard_map/ppermute | solution.py:80
  419.4 50.7 %collective-permute-start.33 = (bf16[192,1536]{1,0:T(8,128)(2,1)S(1)}, bf16[192,1536]{1,0:T(8,128)(2,1)S(1)}, u32[]{:S(2)}, u32[]{:S(2)}) collective-permute-start(bf16[192,1536]{1,0:T(8,128)(2,1)S(1)} %slice.356), channel_id=1, source_target_pairs={{0,8},{1,17},{2,10},{3,19},{4,12},{5,21},{6,14},{7,23},{8,0},{9,25... | collective-permute-start | bytes 1769480 | tf_op jit(solution)/shard_map/ppermute | solution.py:80
  421.8 89.2 %collective-permute-start.50 = (bf16[384,2304]{1,0:T(8,128)(2,1)}, bf16[384,2304]{1,0:T(8,128)(2,1)}, u32[]{:S(2)}, u32[]{:S(2)}) collective-permute-start(bf16[384,2304]{1,0:T(8,128)(2,1)} %slice.380), channel_id=1, source_target_pairs={{0,2},{1,5},{2,0},{3,7},{4,6},{5,1},{6,4},{7,3},{8,10},{9,13},{10,... | collective-permute-start | bytes 5308424 | tf_op jit(solution)/shard_map/ppermute | solution.py:80
  495.9 61.6 %collective-permute-start.45 = (bf16[768,768]{1,0:T(8,128)(2,1)}, bf16[768,768]{1,0:T(8,128)(2,1)}, u32[]{:S(2)}, u32[]{:S(2)}) collective-permute-start(bf16[768,768]{1,0:T(8,128)(2,1)} %pad_maximum_fusion.31), channel_id=1, source_target_pairs={{0,4},{1,3},{2,6},{3,1},{4,0},{5,7},{6,2},{7,5},{8,12},{9,11},{10,... | collective-permute-start | bytes 3538952 | tf_op jit(solution)/shard_map/ppermute | solution.py:80
  508.7 74.1 %collective-permute-start.41 = (bf16[768,1024]{1,0:T(8,128)(2,1)}, bf16[768,1024]{1,0:T(8,128)(2,1)}, u32[]{:S(2)}, u32[]{:S(2)}) collective-permute-start(bf16[768,1024]{1,0:T(8,128)(2,1)} %pad_maximum_fusion.24), channel_id=1, source_target_pairs={{0,4},{1,3},{2,6},{3,1},{4,0},{5,7},{6,2},{7,5},{8,12},{9,11},{10,... | collective-permute-start | bytes 4718600 | tf_op jit(solution)/shard_map/ppermute | solution.py:80
  515.1 45.2 %collective-permute-start.51 = (bf16[192,2304]{1,0:T(8,128)(2,1)}, bf16[192,2304]{1,0:T(8,128)(2,1)}, u32[]{:S(2)}, u32[]{:S(2)}) collective-permute-start(bf16[192,2304]{1,0:T(8,128)(2,1)} %pad_maximum_fusion.35), channel_id=1, source_target_pairs={{0,8},{1,17},{2,10},{3,19},{4,12},{5,21},{6,14},{7,23},{8,0},{9,25... | collective-permute-start | bytes 2654216 | tf_op jit(solution)/shard_map/ppermute | solution.py:80
  570.4 32.2 %collective-permute-start.52 = (bf16[192,2304]{1,0:T(8,128)(2,1)S(1)}, bf16[192,2304]{1,0:T(8,128)(2,1)S(1)}, u32[]{:S(2)}, u32[]{:S(2)}) collective-permute-start(bf16[192,2304]{1,0:T(8,128)(2,1)S(1)} %pad_maximum_fusion.36), channel_id=1, source_target_pairs={{0,16},{1,9},{2,18},{3,11},{4,20},{5,13},{6,22},{7,15},{8,24},{9,1... | collective-permute-start | bytes 2654216 | tf_op jit(solution)/shard_map/ppermute | solution.py:80
  (127 other events, 2420.6 us)

commit v2 on v1

--- a/solution.py
+++ b/solution.py
@@ -1,8 +1,11 @@
+import functools
 import math
 
 import jax
 import jax.numpy as jnp
 from jax import lax
+from jax.experimental import pallas as pl
+from jax.experimental.pallas import tpu as pltpu
 from jax.sharding import PartitionSpec as P
 
 HEAD_DIM = 128
@@ -13,6 +16,8 @@
 LANES = 128
 BF = jnp.bfloat16
 F32 = jnp.float32
+VMEM_BYTES = 56 * 2**20
+ANY = pl.BlockSpec(memory_space=pl.ANY)
 
 
 def normalize(values):
@@ -20,7 +25,7 @@
     return (values * factor, factor)
 
 
-def norm_back(grad_normed, normed, factor, gain_vec):
+def plain_norm_back(grad_normed, normed, factor, gain_vec):
     scaled = grad_normed * gain_vec[None, :]
     row_inner = jnp.mean(scaled * normed, axis=1, keepdims=True)
     return (factor * (scaled - normed * row_inner), jnp.sum(grad_normed * normed, axis=0))
@@ -59,7 +64,7 @@
     return (segment, places - offset)
 
 
-class Topo:
+class PlainTopo:
     def __init__(self):
         self.dp = lax.axis_size("dp")
         self.square = self.dp // LINE
@@ -198,7 +203,7 @@
     return jnp.where(allowed[None, None], raw_scores * score_scale, MASKED)
 
 
-def per_device(
+def plain_device(
     tokens,
     out_grad,
     lengths,
@@ -215,7 +220,7 @@
     up_weight,
     down_weight,
 ):
-    topo = Topo()
+    topo = PlainTopo()
     local_rows, width = tokens.shape
     group_rows = 2 * local_rows
     q_cols = q_weight.shape[1]
@@ -360,7 +365,7 @@
     gate_grads, up_grads = columns_out(square_scatter(t_dot(mlp_in, grad_gate_up)), 2)
     (down_grads,) = columns_out(square_scatter(t_dot(grad_out_all, hidden_units)), 1)
 
-    back_two, gain_two_grad = norm_back(grad_normed_two, normed_two, factor_two, gain_two)
+    back_two, gain_two_grad = plain_norm_back(grad_normed_two, normed_two, factor_two, gain_two)
     grad_state = out_grad_low.astype(F32) + back_two
     grad_state_all = both_cores(grad_state.astype(BF))
     o_grads = rows_out(square_scatter(t_dot(grad_state_all, mixed_heads)))
@@ -387,7 +392,7 @@
     bias_grad = jnp.sum(grad_linear.astype(F32), axis=0)
     qkv_grads = rows_out(square_scatter(t_dot(attn_in, grad_linear)))
     grad_normed_one = core_sum(dot_t(grad_linear, qkv_all))
-    back_one, gain_one_grad = norm_back(grad_normed_one, normed_one, factor_one, gain_one)
+    back_one, gain_one_grad = plain_norm_back(grad_normed_one, normed_one, factor_one, gain_one)
     tokens_grad = (grad_state + back_one).astype(BF)
     gain_grads = to_outer(jnp.stack([gain_one_grad, gain_two_grad]), topo)
     gain_grads = gain_grads + topo.other_core(gain_grads)
@@ -413,6 +418,1025 @@
     )
 
 
+def nn(left, right):
+    return jnp.dot(left, right, preferred_element_type=F32)
+
+
+def nt(left, right):
+    return lax.dot_general(left, right, (((1,), (1,)), ((), ())), preferred_element_type=F32)
+
+
+def tn(left, right):
+    return lax.dot_general(left, right, (((0,), (0,)), ((), ())), preferred_element_type=F32)
+
+
+def shape(dims, kind):
+    return jax.ShapeDtypeStruct(dims, kind)
+
+
+def whole(dims):
+    return pl.BlockSpec(dims, lambda *_: (0,) * len(dims))
+
+
+OFF, NEIGHBOUR, INDEX, AT, OTHER = 0, 4, 8, 12, 13
+
+
+class Topo:
+    def __init__(self):
+        self.dp = lax.axis_size("dp")
+        me = lax.axis_index("dp")
+        core = lax.axis_index("tensor")
+        line_at, square_at = me >> 2, me & 3
+
+        def by_core(index):
+            return jnp.where(core == 0, index, (index >> 1) | ((index & 1) << 1))
+
+        self.core = core
+        self.square_at = square_at
+        self.line = ((LINE, 2 * LINE), (2 * LINE, LINE))
+        self.square = ((1, 2), (2, 1))
+        count = jnp.arange(LINE, dtype=jnp.int32)
+        self.info = jnp.concatenate(
+            [
+                by_core(count),
+                line_at ^ by_core(count),
+                by_core(line_at ^ count),
+                jnp.stack([square_at, 1 - core]),
+            ]
+        ).astype(jnp.int32)
+
+    def swap(self, array, bits, phase):
+        perm = []
+        for place in range(self.dp):
+            for core in range(2):
+                perm.append((place * 2 + core, (place ^ bits[core][phase]) * 2 + core))
+        return lax.ppermute(array, ("dp", "tensor"), perm)
+
+    def other_core(self, array):
+        return lax.ppermute(array, "tensor", [(0, 1), (1, 0)])
+
+    def both_ways(self, array):
+        return lax.all_to_all(array, "tensor", 0, 0, tiled=True)
+
+
+CLOCK = [None]
+TOKEN = jax.ShapeDtypeStruct((8, 128), F32)
+IN_VMEM = pl.BlockSpec(memory_space=pltpu.VMEM)
+IN_SMEM = pl.BlockSpec(memory_space=pltpu.SMEM)
+
+
+def in_order(body, ins, outs):
+    taken = 0 if CLOCK[0] is None else 1
+
+    def full(*refs):
+        body(*refs[:ins], *refs[ins + taken : ins + taken + outs], *refs[ins + taken + outs + 1 :])
+
+    return full
+
+
+def run(kernel, single, args):
+    taken = [] if CLOCK[0] is None else [CLOCK[0]]
+    *out, CLOCK[0] = kernel(*args, *taken)
+    return out[0] if single else out
+
+
+def as_list(value):
+    return list(value) if isinstance(value, (list, tuple)) else [value]
+
+
+def call(body, grid, in_specs, out_specs, out_shape, scratch, info, *args, mib=32):
+    outs = as_list(out_shape)
+    late = 0 if CLOCK[0] is None else 1
+    kernel = pl.pallas_call(
+        in_order(body, 1 + len(in_specs), len(outs)),
+        grid_spec=pltpu.PrefetchScalarGridSpec(
+            num_scalar_prefetch=1,
+            grid=grid,
+            in_specs=list(in_specs) + [IN_VMEM] * late,
+            out_specs=as_list(out_specs) + [IN_VMEM],
+            scratch_shapes=list(scratch),
+        ),
+        out_shape=outs + [TOKEN],
+        compiler_params=pltpu.CompilerParams(vmem_limit_bytes=mib * 2**20),
+        cost_estimate=pl.CostEstimate(flops=1000, bytes_accessed=1000, transcendentals=0),
+        name=body.__qualname__.split(".")[0],
+    )
+    return run(kernel, not isinstance(out_shape, (list, tuple)), (info,) + args)
+
+
+def small(body, out_shape, scratch, info, *args, mib=16):
+    outs = as_list(out_shape)
+    late = 0 if CLOCK[0] is None else 1
+    kernel = pl.pallas_call(
+        in_order(body, 1 + len(args), len(outs)),
+        in_specs=[IN_SMEM] + [IN_VMEM] * (len(args) + late),
+        out_specs=[IN_VMEM] * (len(outs) + 1),
+        scratch_shapes=list(scratch),
+        out_shape=outs + [TOKEN],
+        compiler_params=pltpu.CompilerParams(vmem_limit_bytes=mib * 2**20),
+        cost_estimate=pl.CostEstimate(flops=1000, bytes_accessed=1000, transcendentals=0),
+        name=body.__qualname__.split(".")[0],
+    )
+    return run(kernel, not isinstance(out_shape, (list, tuple)), (info,) + args)
+
+
+def tie(info, array):
+    def body(info_ref, in_ref, out_ref):
+        out_ref[...] = in_ref[...]
+
+    return small(body, shape(array.shape, array.dtype), [], info, array)
+
+
+def join(info, *args):
+    def body(info_ref, *refs):
+        start = 0
+        for ref in refs[:-1]:
+            refs[-1][start : start + ref.shape[0]] = ref[...]
+            start += ref.shape[0]
+
+    rows = sum(a.shape[0] for a in args)
+    return small(body, shape((rows,) + args[0].shape[1:], args[0].dtype), [], info, *args)
+
+
+def beside(info, *args):
+    def body(info_ref, *refs):
+        start = 0
+        for ref in refs[:-1]:
+            refs[-1][:, start : start + ref.shape[1]] = ref[...]
+            start += ref.shape[1]
+
+    cols = sum(a.shape[1] for a in args)
+    return small(body, shape((args[0].shape[0], cols), args[0].dtype), [], info, *args)
+
+
+def placed(info, rows, takes, *args):
+    def body(info_ref, *refs):
+        for index, (which, start) in enumerate(takes):
+            target = pl.multiple_of(info_ref[NEIGHBOUR + index] * rows, 16)
+            refs[-1][pl.ds(target, rows)] = refs[which][start : start + rows]
+
+    return small(body, shape((LINE * rows, args[0].shape[1]), BF), [], info, *args)
+
+
+def second_chunks(info, kept, got):
+    rows = kept.shape[0] // 2
+
+    def body(info_ref, kept_ref, got_ref, out_ref):
+        out_ref[:rows] = kept_ref[rows:]
+        out_ref[rows:] = got_ref[rows:]
+
+    return small(body, shape(kept.shape, BF), [], info, kept, got)
+
+
+def cut_columns(info, part, *weights):
+    count = len(weights)
+    rows, cols = weights[0].shape
+    short = cols - (LINE - 1) * part
+
+    def body(info_ref, *refs):
+        ins, outs = refs[:count], refs[count:]
+        for index in range(LINE):
+            at = info_ref[NEIGHBOUR + index]
+            out = outs[1 - index % 2]
+            low = index // 2 * rows
+            for which, ref in enumerate(ins):
+                start = pl.multiple_of(at * part, LANES)
+                first = which * part
+                out[low : low + rows, first : first + short] = ref[:, pl.ds(start, short)]
+                if short < part:
+                    rest = pl.multiple_of(jnp.minimum(at, LINE - 2) * part + short, LANES)
+                    tail = ref[:, pl.ds(rest, part - short)]
+                    out[low : low + rows, first + short : first + part] = jnp.where(
+                        at < LINE - 1, tail, jnp.zeros_like(tail)
+                    )
+
+    return small(body, [shape((2 * rows, count * part), BF)] * 2, [], info, *weights)
+
+
+def piece_copies(info_ref, pieces, target, sems, cols=None, first_col=0):
+    rows = target.shape[0] // LINE
+    low, high = cols or (0, pieces[0].shape[1])
+    index = 0
+    for piece in pieces:
+        for block in range(piece.shape[0] // rows):
+            start = pl.multiple_of(info_ref[OFF + index] * rows, rows)
+            yield pltpu.make_async_copy(
+                piece.at[pl.ds(block * rows, rows), pl.ds(low, high - low)],
+                target.at[pl.ds(start, rows), pl.ds(first_col + low, high - low)],
+                sems.at[index],
+            )
+            index += 1
+
+
+def square_blocks(info_ref, pieces, width):
+    rows = width // LINE
+    index = 0
+    for piece in pieces:
+        for block in range(piece.shape[0] // rows):
+            start = pl.multiple_of(info_ref[OFF + index] * rows, LANES)
+            yield pl.ds(start, rows), piece[block * rows : (block + 1) * rows]
+            index += 1
+
+
+def inward(values, at, store):
+    width = values.shape[1]
+    block = width // LINE
+    rest = block // LINE
+    for square in range(LINE):
+        parts = [
+            values[:, line * block + square * rest : line * block + (square + 1) * rest]
+            for line in range(LINE)
+        ]
+        start = pl.multiple_of((square ^ at) * block, LANES)
+        store(pl.ds(start, block), jnp.concatenate(parts, axis=1))
+
+
+def outward(ref, at):
+    width = ref.shape[1]
+    block = width // LINE
+    rest = block // LINE
+    blocks = []
+    for square in range(LINE):
+        start = pl.multiple_of((square ^ at) * block, LANES)
+        blocks.append(ref[:, pl.ds(start, block)])
+    parts = []
+    for line in range(LINE):
+        for square in range(LINE):
+            parts.append(blocks[square][:, line * rest : (line + 1) * rest])
+    return jnp.concatenate(parts, axis=1)
+
+
+def turn_rows(info, rows):
+    def body(info_ref, rows_ref, out_ref, held):
+        def store(cols, block):
+            held[:, cols] = block
+
+        inward(rows_ref[...].astype(F32), info_ref[AT], store)
+        out_ref[...] = held[...].astype(BF)
+
+    return small(body, shape(rows.shape, BF), [pltpu.VMEM(rows.shape, F32)], info, rows)
+
+
+def open_rows(info, rows, gains):
+    def body(info_ref, rows_ref, gains_ref, out_ref, in_ref, gain_ref, held):
+        def store_gain(cols, block):
+            gain_ref[:, cols] = block
+
+        def store(cols, block):
+            held[:, cols] = block
+
+        inward(gains_ref[...], info_ref[AT], store_gain)
+        inward(rows_ref[...].astype(F32), info_ref[AT], store)
+        values = held[...]
+        in_ref[...] = values.astype(BF)
+        factor = lax.rsqrt(jnp.mean(values * values, axis=1, keepdims=True) + EPSILON)
+        out_ref[...] = (values * factor * gain_ref[0:1, :]).astype(BF)
+
+    return small(
+        body,
+        [shape(rows.shape, BF), shape(rows.shape, BF), shape(gains.shape, F32)],
+        [pltpu.VMEM(rows.shape, F32)],
+        info,
+        rows,
+        gains,
+    )
+
+
+def state_rows(info, rows, own, got, gain):
+    def body(info_ref, rows_ref, own_ref, got_ref, gain_ref, out_ref, state_ref):
+        start = pl.multiple_of(info_ref[OTHER] * dims[0], 16)
+        got = got_ref[pl.ds(start, dims[0])] if got_ref.shape[0] > dims[0] else got_ref[...]
+        values = rows_ref[...].astype(F32) + (own_ref[...] + got.astype(F32))
+        state_ref[...] = values
+        factor = lax.rsqrt(jnp.mean(values * values, axis=1, keepdims=True) + EPSILON)
+        out_ref[...] = (values * factor * gain_ref[...]).astype(BF)
+
+    dims = rows.shape
+    return small(
+        body,
+        [shape(dims, BF), shape(dims, F32)],
+        [],
+        info,
+        rows,
+        own,
+        got,
+        gain,
+    )
+
+
+def close_rows(info, state, own, got):
+    def body(info_ref, state_ref, own_ref, got_ref, out_ref, held):
+        held[...] = state_ref[...] + (own_ref[...].astype(F32) + got_ref[...].astype(F32))
+        out_ref[...] = outward(held, info_ref[AT]).astype(BF)
+
+    dims = state.shape
+    return small(
+        body,
+        shape(dims, BF),
+        [pltpu.VMEM(dims, F32)],
+        info,
+        state,
+        own,
+        got,
+    )
+
+
+def norm_back(info, values, own, got, base, gain, turn):
+    def body(info_ref, values_ref, own_ref, got_ref, base_ref, gain_ref, *refs):
+        values = values_ref[...].astype(F32)
+        factor = lax.rsqrt(jnp.mean(values * values, axis=1, keepdims=True) + EPSILON)
+        normed = values * factor
+        grad = own_ref[...].astype(F32) + got_ref[...].astype(F32)
+        scaled = grad * gain_ref[...]
+        row_inner = jnp.mean(scaled * normed, axis=1, keepdims=True)
+        total = base_ref[...].astype(F32) + factor * (scaled - normed * row_inner)
+        gain_grad = jnp.sum(grad * normed, axis=0, keepdims=True)
+        if turn:
+            out_ref, gain_out_ref, held, gain_held = refs
+            held[...] = total
+            out_ref[...] = outward(held, info_ref[AT]).astype(BF)
+        else:
+            low_ref, out_ref, gain_out_ref, gain_held = refs
+            out_ref[...] = total
+            low_ref[...] = total.astype(BF)
+        gain_held[...] = gain_grad
+        gain_out_ref[...] = outward(gain_held, info_ref[AT])
+
+    dims = values.shape
+    kinds = (BF,) if turn else (BF, F32)
+    return small(
+        body,
+        [shape(dims, kind) for kind in kinds] + [shape(gain.shape, F32)],
+        ([pltpu.VMEM(dims, F32)] if turn else []) + [pltpu.VMEM(gain.shape, F32)],
+        info,
+        values,
+        own,
+        got,
+        base,
+        gain,
+    )
+
+
+def turned(values, cosine, sine):
+    return values * cosine + pltpu.roll(values, HEAD_DIM // 2, 1) * sine
+
+
+def attend(info, rows, pieces, bias, cosine, sine, row_info, col_info, q_heads, kv_heads):
+    count, cols = len(pieces), pieces[0].shape[1]
+    group, width = rows.shape
+    q_cols = q_heads * HEAD_DIM
+
+    def body(info_ref, in_ref, *refs):
+        pieces = refs[:count]
+        bias_ref, cos_ref, sin_ref, row_ref, col_ref = refs[count : count + 5]
+        mixed_ref, lin_ref, mass_ref = refs[count + 5 :]
+        cosine, sine = cos_ref[...], sin_ref[...]
+        scale = 1.0 / math.sqrt(HEAD_DIM)
+        linear = bias_ref[...]
+        for cols, piece in square_blocks(info_ref, pieces, width):
+            linear = linear + nn(in_ref[:, cols], piece)
+        for head in range(q_heads + 2 * kv_heads):
+            cols = slice(head * HEAD_DIM, (head + 1) * HEAD_DIM)
+            part = linear[:, cols]
+            if head < q_heads + kv_heads:
+                part = turned(part, cosine, sine)
+            lin_ref[:, cols] = part.astype(BF)
+        allowed = (row_ref[:, 0:1] <= col_ref[...]) & (col_ref[...] <= row_ref[:, 1:2])
+        for head in range(q_heads):
+            key = q_heads + head // (q_heads // kv_heads)
+            value = key + kv_heads
+            cols = slice(head * HEAD_DIM, (head + 1) * HEAD_DIM)
+            raw = nt(lin_ref[:, cols], lin_ref[:, key * HEAD_DIM : (key + 1) * HEAD_DIM])
+            scores = jnp.where(allowed, raw * scale, MASKED)
+            peak = jnp.max(scores, axis=1, keepdims=True)
+            exponent = jnp.exp(scores - peak)
+            mass = jnp.sum(exponent, axis=1, keepdims=True)
+            mass_ref[:, head : head + 1] = peak + jnp.log(mass)
+            probs = (exponent * (1.0 / mass)).astype(BF)
+            mixed_ref[:, cols] = nn(
+                probs, lin_ref[:, value * HEAD_DIM : (value + 1) * HEAD_DIM]
+            ).astype(BF)
+
+    plain = (bias, cosine, sine, row_info, col_info)
+    return small(
+        body,
+        [shape((group, q_cols), BF), shape((group, cols), BF), shape((group, LANES), F32)],
+        [],
+        info,
+        rows,
+        *pieces,
+        *plain,
+    )
+
+
+def project(info, rows, pieces, width):
+    count, cols = len(pieces), pieces[0].shape[1]
+    half = rows.shape[0] // 2
+
+    def body(info_ref, in_ref, *refs):
+        pieces = refs[:count]
+        other_ref, own_ref = refs[count:]
+        for cols, piece in square_blocks(info_ref, pieces, width):
+            both = nt(in_ref[...], piece)
+            own_ref[:, cols] = both[:half]
+            other_ref[:, cols] = both[half:].astype(BF)
+
+    return small(
+        body,
+        [shape((half, width), BF), shape((half, width), F32)],
+        [],
+        info,
+        rows,
+        *pieces,
+    )
+
+
+def attend_back(
+    info, state, o_pieces, pieces, linear, mass, cosine, sine, row_info, col_info, q_heads, kv_heads
+):
+    count, cols = len(pieces), pieces[0].shape[1]
+    group, width = state.shape
+    q_cols = q_heads * HEAD_DIM
+    half = group // 2
+
+    def body(info_ref, state_ref, *refs):
+        o_refs, q_refs = refs[:count], refs[count : 2 * count]
+        lin_ref, mass_ref, cos_ref, sin_ref, row_ref, col_ref = refs[2 * count : 2 * count + 6]
+        grad_ref, bias_ref, own_ref, other_ref = refs[2 * count + 6 : 2 * count + 10]
+        heads_ref = refs[-1]
+        cosine, sine = cos_ref[...], -sin_ref[...]
+        scale = 1.0 / math.sqrt(HEAD_DIM)
+        heads = 0.0
+        for cols, piece in square_blocks(info_ref, o_refs, width):
+            heads = heads + nn(state_ref[:, cols], piece)
+        heads_ref[...] = heads.astype(BF)
+        allowed = (row_ref[:, 0:1] <= col_ref[...]) & (col_ref[...] <= row_ref[:, 1:2])
+        per_group = q_heads // kv_heads
+        for place in range(kv_heads):
+            key_cols = slice((q_heads + place) * HEAD_DIM, (q_heads + place + 1) * HEAD_DIM)
+            first = q_heads + kv_heads + place
+            value_cols = slice(first * HEAD_DIM, (first + 1) * HEAD_DIM)
+            keys, values = lin_ref[:, key_cols], lin_ref[:, value_cols]
+            grad_keys, grad_values = 0.0, 0.0
+            for head in range(place * per_group, (place + 1) * per_group):
+                cols = slice(head * HEAD_DIM, (head + 1) * HEAD_DIM)
+                queries, grads = lin_ref[:, cols], heads_ref[:, cols]
+                scores = jnp.where(allowed, nt(queries, keys) * scale, MASKED)
+                probs = jnp.exp(scores - mass_ref[:, head : head + 1])
+                grad_probs = nt(grads, values)
+                inner = jnp.sum(probs * grad_probs, axis=1, keepdims=True)
+                grad_scores = (probs * (grad_probs - inner) * scale).astype(BF)
+                grad_values += tn(probs.astype(BF), grads)
+                grad_keys += tn(grad_scores, queries)
+                grad_ref[:, cols] = turned(nn(grad_scores, keys), cosine, sine).astype(BF)
+            grad_ref[:, key_cols] = turned(grad_keys, cosine, sine).astype(BF)
+            grad_ref[:, value_cols] = grad_values.astype(BF)
+        bias_ref[...] = jnp.sum(grad_ref[...].astype(F32), axis=0, keepdims=True)
+        for cols, piece in square_blocks(info_ref, q_refs, width):
+            both = nt(grad_ref[...], piece)
+            own_ref[:, cols] = both[:half]
+            other_ref[:, cols] = both[half:].astype(BF)
+
+    plain = (linear, mass, cosine, sine, row_info, col_info)
+    return small(
+        body,
+        [
+            shape((group, cols), BF),
+            shape((1, cols), F32),
+            shape((half, width), F32),
+            shape((half, width), BF),
+        ],
+        [pltpu.VMEM((group, q_cols), BF)],
+        info,
+        state,
+        *o_pieces,
+        *pieces,
+        *plain,
+    )
+
+
+def forward(info, x, gate_up, tile, step=256):
+    count, part = len(gate_up), gate_up[0].shape[1] // 2
+    total, width = x.shape
+    spans = [(low, min(low + step, part)) for low in range(0, part, step)]
+
+    def body(info_ref, x_ref, *refs):
+        pieces = refs[:count]
+        hid_ref, gate_ref, up_ref, weight, sems = refs[count:]
+
+        def span_copies(index):
+            low, high = spans[index]
+            yield from piece_copies(info_ref, pieces, weight, sems.at[2 * index], (low, high))
+            yield from piece_copies(
+                info_ref, pieces, weight, sems.at[2 * index + 1], (part + low, part + high)
+            )
+
+        opening = pl.program_id(0) == 0
+
+        @pl.when(opening)
+        def _():
+            for index in range(len(spans)):
+                for copy in span_copies(index):
+                    copy.start()
+
+        x = x_ref[...]
+        for index, (low, high) in enumerate(spans):
+
+            @pl.when(opening)
+            def _(index=index):
+                for copy in span_copies(index):
+                    copy.wait()
+
+            gate = nn(x, weight[:, low:high])
+            up = nn(x, weight[:, part + low : part + high])
+            share = 1.0 / (1.0 + jnp.exp(-gate))
+            active = gate * share
+            hid_ref[:, low:high] = (active * up).astype(BF)
+            gate_ref[:, low:high] = (up * share * (1.0 + gate * (1.0 - share))).astype(BF)
+            up_ref[:, low:high] = active.astype(BF)
+
+    return call(
+        body,
+        (total // tile,),
+        [pl.BlockSpec((tile, width), lambda i, _: (i, 0))] + [ANY] * count,
+        [pl.BlockSpec((tile, part), lambda i, _: (i, 0))] * 3,
+        [shape((total, part), BF)] * 3,
+        [
+            pltpu.VMEM((width, 2 * part), BF),
+            pltpu.SemaphoreType.DMA((2 * len(spans), LINE)),
+        ],
+        info,
+        x,
+        *gate_up,
+    )
+
+
+def halves_spec(tile, width, steps, spread):
+    half = steps // 2
+
+    def later(i, info_ref):
+        first = info_ref[OTHER] * half if spread else 0
+        return (first + jnp.maximum(i - half, 0), 0)
+
+    return [
+        pl.BlockSpec((tile, width), lambda i, _: (jnp.minimum(i, half - 1), 0)),
+        pl.BlockSpec((tile, width), later),
+    ]
+
+
+def store_half(value, steps, first_ref, second_ref):
+    early = pl.program_id(0) < steps // 2
+
+    @pl.when(early)
+    def _():
+        first_ref[...] = value
+
+    @pl.when(jnp.logical_not(early))
+    def _():
+        second_ref[...] = value
+
+
+def down_sum(info, hidden, down, tile, width):
+    count = len(down)
+    total, part = hidden.shape
+    steps = total // tile
+
+    def body(info_ref, hid_ref, *refs):
+        pieces = refs[:count]
+        own_ref, other_ref, weight, sems = refs[count:]
+
+        @pl.when(pl.program_id(0) == 0)
+        def _():
+            copies = list(piece_copies(info_ref, pieces, weight, sems))
+            for copy in copies:
+                copy.start()
+            for copy in copies:
+                copy.wait()
+
+        value = nt(hid_ref[...], weight[...]).astype(BF)
+        store_half(value, steps, own_ref, other_ref)
+
+    return call(
+        body,
+        (steps,),
+        [pl.BlockSpec((tile, part), lambda i, _: (i, 0))] + [ANY] * count,
+        halves_spec(tile, width, steps, False),
+        [shape((total // 2, width), BF)] * 2,
+        [pltpu.VMEM((width, part), BF), pltpu.SemaphoreType.DMA((LINE,))],
+        info,
+        hidden,
+        *down,
+    )
+
+
+def backward(info, g, gate_factor, up_factor, gate_up, down, tile, step=256):
+    count, part = len(down), down[0].shape[1]
+    total, width = g.shape
+    steps = total // tile
+    spans = [(low, min(low + step, part)) for low in range(0, part, step)]
+
+    def body(info_ref, g_ref, gate_ref, up_ref, *refs):
+        gate_up, down = refs[:count], refs[count : 2 * count]
+        grad_ref, own_ref, other_ref, weight, sems = refs[2 * count :]
+
+        def span_copies(index):
+            yield from piece_copies(info_ref, down, weight, sems.at[index], spans[index], 2 * part)
+
+        def late_copies():
+            yield from piece_copies(info_ref, gate_up, weight, sems.at[len(spans)])
+
+        opening = pl.program_id(0) == 0
+
+        @pl.when(opening)
+        def _():
+            for index in range(len(spans)):
+                for copy in span_copies(index):
+                    copy.start()
+            for copy in late_copies():
+                copy.start()
+
+        g = g_ref[...]
+        for index, (low, high) in enumerate(spans):
+
+            @pl.when(opening)
+            def _(index=index):
+                for copy in span_copies(index):
+                    copy.wait()
+
+            grad = nn(g, weight[:, 2 * part + low : 2 * part + high])
+            grad_ref[:, low:high] = (grad * gate_ref[:, low:high].astype(F32)).astype(BF)
+            grad_ref[:, part + low : part + high] = (
+                grad * up_ref[:, low:high].astype(F32)
+            ).astype(BF)
+
+        @pl.when(opening)
+        def _():
+            for copy in late_copies():
+                copy.wait()
+
+        value = nt(grad_ref[...], weight[:, : 2 * part]).astype(BF)
+        store_half(value, steps, own_ref, other_ref)
+
+    return call(
+        body,
+        (steps,),
+        [pl.BlockSpec((tile, cols), lambda i, _: (i, 0)) for cols in (width, part, part)]
+        + [ANY] * (2 * count),
+        [pl.BlockSpec((tile, 2 * part), lambda i, _: (i, 0))] + halves_spec(tile, width, steps, False),
+        [shape((total, 2 * part), BF)] + [shape((total // 2, width), BF)] * 2,
+        [
+            pltpu.VMEM((width, 3 * part), BF),
+            pltpu.SemaphoreType.DMA((len(spans) + 1, LINE)),
+        ],
+        info,
+        g,
+        gate_factor,
+        up_factor,
+        *gate_up,
+        *down,
+    )
+
+
+def grads_sent(info, left, right, block):
+    total, cols = right.shape
+
+    def body(info_ref, left_ref, right_ref, out_ref):
+        out_ref[...] = tn(left_ref[...], right_ref[...]).astype(BF)
+
+    return call(
+        body,
+        (2,),
+        [
+            pl.BlockSpec((total, block), lambda i, info_ref: (0, info_ref[OFF + 2 + i])),
+            whole(right.shape),
+        ],
+        pl.BlockSpec((block, cols), lambda i, _: (i, 0)),
+        shape((2 * block, cols), BF),
+        [],
+        info,
+        left,
+        right,
+    )
+
+
+def grads_kept(info, left, right, block, got):
+    total, cols = right.shape
+
+    def body(info_ref, left_ref, right_ref, got_ref, keep_ref, send_ref):
+        value = (tn(left_ref[...], right_ref[...]) + got_ref[...].astype(F32)).astype(BF)
+        store_half(value, 2, keep_ref, send_ref)
+
+    return call(
+        body,
+        (2,),
+        [
+            pl.BlockSpec((total, block), lambda i, info_ref: (0, info_ref[OFF + i])),
+            whole(right.shape),
+            pl.BlockSpec((block, cols), lambda i, _: (i, 0)),
+        ],
+        [whole((block, cols))] * 2,
+        [shape((block, cols), BF)] * 2,
+        [],
+        info,
+        left,
+        right,
+        got,
+    )
+
+
+def sum_split(info, block, count, keep_at, send_at, left, right):
+    cols = left.shape[1]
+
+    def body(info_ref, left_ref, right_ref, *outs):
+        for out, (first, stride, along) in zip(outs, (keep_at, send_at)):
+            for step in range(count):
+                index = first + stride * step
+                if along:
+                    rows = pl.ds(pl.multiple_of(info_ref[NEIGHBOUR + index] * block, 16), block)
+                else:
+                    rows = pl.ds(index * block, block)
+                total = left_ref[rows].astype(F32) + right_ref[rows].astype(F32)
+                out[step * block : (step + 1) * block] = total.astype(BF)
+
+    return small(body, [shape((count * block, cols), BF)] * 2, [], info, left, right)
+
+
+def sum_out(info, left, right, widths):
+    rows = left.shape[0]
+
+    def body(info_ref, left_ref, right_ref, *outs):
+        total = left_ref[...].astype(F32) + right_ref[...].astype(F32)
+        start = 0
+        for out, cols in zip(outs, widths):
+            out[...] = total[:, start : start + cols]
+            start += cols
+
+    return small(
+        body,
+        [shape((rows, cols), F32) for cols in widths],
+        [],
+        info,
+        left,
+        right,
+    )
+
+
+def columns_out(info, kept, got, last, part, cols):
+    rows = kept.shape[0] // 2
+    count = kept.shape[1] // part
+
+    def body(info_ref, kept_ref, got_ref, last_ref, *outs):
+        pieces = [kept_ref[:rows], got_ref[:rows], last_ref[:rows], last_ref[rows:]]
+        for place in range(LINE):
+            low = place * part
+            span = min(part, cols - low)
+            for index, piece in enumerate(pieces):
+
+                @pl.when(info_ref[INDEX + place] == index)
+                def _(piece=piece, low=low, span=span):
+                    for which, out in enumerate(outs):
+                        start = which * part
+                        out[:, low : low + span] = piece[:, start : start + span].astype(F32)
+
+    return small(
+        body,
+        [shape((rows, cols), F32)] * count,
+        [],
+        info,
+        kept,
+        got,
+        last,
+    )
+
+
+def sequence_info(length_row, places):
+    seq_ends = jnp.cumsum(length_row)
+    starts = seq_ends - length_row
+    inside = (places[:, None] >= starts[None, :]) & (places[:, None] < seq_ends[None, :])
+    return jnp.sum(jnp.where(inside, starts[None, :], 0), axis=1)
+
+
+def per_device(
+    tokens,
+    out_grad,
+    lengths,
+    attn_gain,
+    q_weight,
+    q_bias,
+    k_weight,
+    k_bias,
+    v_weight,
+    v_bias,
+    o_weight,
+    mlp_gain,
+    gate_weight,
+    up_weight,
+    down_weight,
+):
+    CLOCK[0] = None
+    topo = Topo()
+    info = topo.info
+    line, square = topo.line, topo.square
+    local_rows, width = tokens.shape
+    shard_rows = q_weight.shape[0]
+    block = width // LINE
+    q_cols = q_weight.shape[1]
+    kv_cols = k_weight.shape[1]
+    qkv_cols = q_cols + 2 * kv_cols
+    ff_cols = gate_weight.shape[1]
+    part = -(-ff_cols // (LINE * LANES)) * LANES
+    q_heads, kv_heads = q_cols // HEAD_DIM, kv_cols // HEAD_DIM
+    tile = local_rows * LINE // 2
+
+    q_own = beside(info, q_weight, k_weight, v_weight)
+    q_one = topo.swap(q_own, line, 0)
+    gate_up_send, gate_up_keep = cut_columns(info, part, gate_weight, up_weight)
+
+    q_joined = join(info, q_own, q_one)
+    q_two = topo.swap(q_joined, line, 1)
+    bias_all = jnp.concatenate([q_bias, k_bias, v_bias]).astype(F32)[None, :]
+    gains = jnp.stack([attn_gain, mlp_gain]).astype(F32)
+    attn_own, inputs, gains = open_rows(info, tokens, gains)
+    gain_one, gain_two = gains[0:1], gains[1:2]
+    attn_other = topo.other_core(attn_own)
+    out_grad_in = turn_rows(info, out_grad)
+    row_ids = jnp.arange(local_rows, dtype=jnp.int32)
+    places = jnp.concatenate(
+        [topo.core * local_rows + row_ids, (1 - topo.core) * local_rows + row_ids]
+    )
+    starts = sequence_info(lengths[0], places)
+    frequency = jnp.power(ROPE_BASE, -2.0 * jnp.arange(HEAD_DIM // 2, dtype=F32) / HEAD_DIM)
+    angles = (places - starts).astype(F32)[:, None] * frequency[None, :]
+    cosine_half, sine_half = jnp.cos(angles), jnp.sin(angles)
+    cosine = jnp.concatenate([cosine_half, cosine_half], axis=1)
+    sine = jnp.concatenate([-sine_half, sine_half], axis=1)
+    row_info = jnp.stack([starts, places], axis=1)
+    col_info = places[None, :]
+    from_line = [(0, 0), (0, shard_rows), (1, 0), (1, shard_rows)]
+    from_exchange = [(0, 0), (1, 0), (2, 0), (2, shard_rows)]
+
+    o_own = join(info, o_weight)
+    o_one = topo.swap(o_own, line, 0)
+    q_piece = placed(info, shard_rows, from_line, q_joined, q_two)
+    q_near = topo.swap(q_piece, square, 0)
+    gate_up_one = topo.swap(tie(info, gate_up_send), line, 0)
+    attn_in = join(info, attn_own, attn_other)
+    q_all = [join(info, q_piece, q_near)]
+    q_all.append(topo.swap(q_all[0], square, 1))
+    o_joined = join(info, o_own, o_one)
+    o_two = topo.swap(o_joined, line, 1)
+    o_piece = placed(info, shard_rows, from_line, o_joined, o_two)
+    o_near = topo.swap(o_piece, square, 0)
+    gate_up_two = topo.swap(second_chunks(info, gate_up_keep, gate_up_one), line, 1)
+    o_all = [join(info, o_piece, o_near)]
+    o_all.append(topo.swap(o_all[0], square, 1))
+    down_send, down_keep = cut_columns(info, part, down_weight)
+    down_one = topo.swap(down_send, line, 0)
+
+    mixed, linear, mass = attend(
+        info, attn_in, q_all, bias_all, cosine, sine, row_info, col_info, q_heads, kv_heads
+    )
+    gate_up_piece = placed(
+        info, shard_rows, from_exchange, gate_up_keep, gate_up_one, gate_up_two
+    )
+    gate_up_near = topo.swap(gate_up_piece, square, 0)
+    down_two = topo.swap(second_chunks(info, down_keep, down_one), line, 1)
+    other_attn, own_attn = project(info, mixed, o_all, width)
+    other_attn = topo.other_core(other_attn)
+    mlp_own, state = state_rows(info, inputs, own_attn, other_attn, gain_two)
+    mlp_one = topo.swap(mlp_own, line, 0)
+    grad_out_one = topo.swap(tie(info, out_grad_in), line, 0)
+
+    gate_up = [join(info, gate_up_piece, gate_up_near)]
+    gate_up.append(topo.swap(gate_up[0], square, 1))
+    down_piece = placed(info, shard_rows, from_exchange, down_keep, down_one, down_two)
+    down_near = topo.swap(down_piece, square, 0)
+    mlp_half = join(info, mlp_own, mlp_one)
+    mlp_two = topo.swap(mlp_half, line, 1)
+    mlp_early = topo.other_core(mlp_half)
+    grad_out_half = join(info, out_grad_in, grad_out_one)
+    grad_out_two = topo.swap(grad_out_half, line, 1)
+    mlp_late = topo.other_core(mlp_two)
+    mlp_in = join(info, mlp_half, mlp_two, mlp_early, mlp_late)
+    down = [join(info, down_piece, down_near)]
+    down.append(topo.swap(down[0], square, 1))
+    grad_out_early = topo.other_core(grad_out_half)
+
+    hidden, gate_factor, up_factor = forward(info, mlp_in, gate_up, tile)
+    grad_out_late = topo.other_core(grad_out_two)
+    out_own, out_other = down_sum(info, hidden, down, tile, width)
+    out_other = topo.other_core(out_other)
+    grad_out_all = join(info, grad_out_half, grad_out_two, grad_out_early, grad_out_late)
+    pair = (0, 1, False), (2, 1, False)
+    rows = local_rows
+    out_keep, out_send = sum_split(info, rows, 2, *pair, out_own, out_other)
+    out_one = topo.swap(out_send, line, 1)
+    down_full = grads_sent(info, grad_out_all, hidden, block)
+    down_got = topo.swap(down_full, square, 1)
+    grads, back_own, back_other = backward(
+        info, grad_out_all, gate_factor, up_factor, gate_up, down, tile
+    )
+    back_other = topo.other_core(back_other)
+    down_kept, down_send = grads_kept(info, grad_out_all, hidden, block, down_got)
+    down_last = topo.swap(down_send, square, 0)
+    single = (0, 1, False), (1, 1, False)
+    out_keep, out_send = sum_split(info, rows, 1, *single, out_keep, out_one)
+    out_two = topo.swap(out_send, line, 0)
+    back_keep, back_send = sum_split(info, rows, 2, *pair, back_own, back_other)
+    back_one = topo.swap(back_send, line, 1)
+    gate_up_full = grads_sent(info, mlp_in, grads, block)
+    gate_up_got = topo.swap(gate_up_full, square, 1)
+    chunks = (0, 2, True), (1, 2, True)
+    down_keep, down_send = sum_split(info, shard_rows, 2, *chunks, down_kept, down_last)
+    down_one = topo.swap(down_send, line, 0)
+    block_out = close_rows(info, state, out_keep, out_two)
+    back_keep, back_send = sum_split(info, rows, 1, *single, back_keep, back_one)
+    back_two = topo.swap(back_send, line, 0)
+    down_two = topo.swap(second_chunks(info, down_keep, down_one), line, 1)
+
+    grad_state_low, grad_state, gain_two_grad = norm_back(
+        info, state, back_keep, back_two, out_grad_in, gain_two, False
+    )
+    state_other = topo.other_core(grad_state_low)
+    gate_up_kept, gate_up_send = grads_kept(info, mlp_in, grads, block, gate_up_got)
+    gate_up_last = topo.swap(gate_up_send, square, 0)
+    grad_state_all = join(info, grad_state_low, state_other)
+    o_full = grads_sent(info, grad_state_all, mixed, block)
+    o_got = topo.swap(o_full, square, 1)
+    grad_linear, bias_grad, own_part, other_part = attend_back(
+        info,
+        grad_state_all,
+        o_all,
+        q_all,
+        linear,
+        mass,
+        cosine,
+        sine,
+        row_info,
+        col_info,
+        q_heads,
+        kv_heads,
+    )
+    part_other = topo.other_core(other_part)
+    q_full = grads_sent(info, attn_in, grad_linear, block)
+    q_got = topo.swap(q_full, square, 1)
+    (down_grads,) = columns_out(info, down_keep, down_one, down_two, part, ff_cols)
+    o_kept, o_send = grads_kept(info, grad_state_all, mixed, block, o_got)
+    o_last = topo.swap(o_send, square, 0)
+    gate_up_keep, gate_up_send = sum_split(
+        info, shard_rows, 2, *chunks, gate_up_kept, gate_up_last
+    )
+    gate_up_one = topo.swap(gate_up_send, line, 0)
+    tokens_grad, gain_one_grad = norm_back(
+        info, inputs, own_part, part_other, grad_state, gain_one, True
+    )
+    gain_grads = jnp.concatenate([gain_one_grad, gain_two_grad], axis=0)
+    gain_grads = gain_grads + topo.other_core(gain_grads)
+    sums = jnp.concatenate([bias_grad.reshape(-1), gain_grads.reshape(-1)]).reshape(-1, LANES)
+    sums = sums + topo.swap(sums, line, 0)
+
+    q_kept, q_send = grads_kept(info, attn_in, grad_linear, block, q_got)
+    q_last = topo.swap(q_send, square, 0)
+    sums = sums + topo.swap(sums, line, 1)
+    ordered = (0, 1, True), (2, 1, True)
+    o_keep, o_send = sum_split(info, shard_rows, 2, *ordered, o_kept, o_last)
+    o_one = topo.swap(o_send, line, 1)
+    sums = sums + topo.swap(sums, square, 0)
+    gate_up_two = topo.swap(second_chunks(info, gate_up_keep, gate_up_one), line, 1)
+    sums = sums + topo.swap(sums, square, 1)
+    sums = sums.reshape(-1)
+    own_bias = sums[:qkv_cols]
+    gain_sum = sums[qkv_cols:].reshape(2, width)
+    q_keep, q_send = sum_split(info, shard_rows, 2, *ordered, q_kept, q_last)
+    q_one = topo.swap(q_send, line, 1)
+    o_keep, o_send = sum_split(info, shard_rows, 1, *single, o_keep, o_one)
+    o_two = topo.swap(o_send, line, 0)
+    q_keep, q_send = sum_split(info, shard_rows, 1, *single, q_keep, q_one)
+    q_two = topo.swap(q_send, line, 0)
+    (o_grads,) = sum_out(info, o_keep, o_two, (q_cols,))
+    gate_grads, up_grads = columns_out(
+        info, gate_up_keep, gate_up_one, gate_up_two, part, ff_cols
+    )
+    q_grads, k_grads, v_grads = sum_out(info, q_keep, q_two, (q_cols, kv_cols, kv_cols))
+    CLOCK[0] = None
+    return (
+        block_out,
+        tokens_grad,
+        gain_sum[0],
+        q_grads,
+        own_bias[:q_cols],
+        k_grads,
+        own_bias[q_cols : q_cols + kv_cols],
+        v_grads,
+        own_bias[q_cols + kv_cols :],
+        o_grads,
+        gain_sum[1],
+        gate_grads,
+        up_grads,
+        down_grads,
+    )
+
+
 def solution(mesh):
     rows = P(("dp", "tensor"), None)
     both = P("dp", "tensor")
@@ -423,6 +1447,11 @@
     out_specs = (
         rows, rows, P(), both, half, both, half, both, half, both, P(), both, both, both,
     )
+    fast = mesh.shape["dp"] == LINE * LINE and mesh.shape["tensor"] == 2
     return jax.shard_map(
-        per_device, mesh=mesh, in_specs=in_specs, out_specs=out_specs, check_vma=False
-    )
+        per_device if fast else plain_device,
+        mesh=mesh,
+        in_specs=in_specs,
+        out_specs=out_specs,
+        check_vma=False,
+    )

time: 636 us -> 549 us (0.86)
  Pallas kernels: 0 us -> 161 us
  matrix products: 126 us -> 0 us
  other arithmetic: 77.1 us -> 1.55 us
  local copies, waits for them, and re-layouts: 77 us -> 35.1 us
  waiting for transfers between devices: 246 us -> 275 us
  starting transfers between devices: 82.9 us -> 64.2 us
  between operations: 18.6 us -> 2.06 us
    pallas_call x0 -> x60, Pallas kernels: none -> 161 us  [run(): *out, CLOCK[0] = kernel(*args, *taken)]
    dot_general x18 -> x0, matrix products: 126 us -> none  [the longest x4 49.5 us: dot(): return jnp.dot(left, right, preferred_element_type=F32)]
    convert_element_type x26 -> x3, other arithmetic: 28.5 us -> 0.1 us  [the longest x1 0.08 us: per_device(): angles = (places - starts).astype(F32)[:, None] * frequency[None, :]]
    concatenate x24 -> x3, other arithmetic: 22.8 us -> 0.25 us  [the longest x1 0.12 us: per_device(): sine = jnp.concatenate([-sine_half, sine_half], axis=1)]
    ppermute x48 -> x44, waiting for transfers between devices: 245 us -> 266 us  [swap(): return lax.ppermute(array, ('dp', 'tensor'), perm)]
    unnamed x216 -> x140, local copies, waits for them, and re-layouts: 14.3 us -> 33.1 us
    another operation x24 -> x2, other arithmetic: 17.5 us -> 0.19 us  [the longest x19 14.9 us: ordered(): stacked = jnp.stack(pieces)]
    ppermute x48 -> x44, starting transfers between devices: 78.8 us -> 62.2 us  [swap(): return lax.ppermute(array, ('dp', 'tensor'), perm)]
  transfers between devices with their start and end apart: 57 -> 55, of which waited for: 26 -> 30; matrix products, arithmetic and copies ran while one was open for 35% -> 1% of each run, Pallas kernels for 0% -> 20%
where the time goes in v2:
time: 549 us; the launch traced here: 539 us
  waiting for transfers between devices  275 us (50%)
  Pallas kernels  161 us (29%)
  starting transfers between devices  64.2 us (12%)
  local copies, waits for them, and re-layouts  35.1 us (6%)
    ppermute x44, waiting for transfers between devices, swap(): return lax.ppermute(array, ('dp', 'tensor'), perm)  266 us
    pallas_call x60, Pallas kernels, run(): *out, CLOCK[0] = kernel(*args, *taken)  161 us
    ppermute x44, starting transfers between devices, swap(): return lax.ppermute(array, ('dp', 'tensor'), perm)  62.2 us
    unnamed x140, local copies, waits for them, and re-layouts  33.1 us
  transfers between devices with their start and end apart: 55, of which 30 were waited for; matrix products, arithmetic and copies ran while one was open for 1% of the time, Pallas kernels for 20%

profile of v2, /device:TPU:0, one launch (start us, length us, event | category | flops | bytes accessed | tf_op | source)
XLA Modules:
  0.0 539.3 jit_solution(538599955009393734)
XLA Ops:
  3.7 3.1 collective-permute-start
  18.7 5.4 collective-permute-done.2.refs_2_
  31.2 5.8 %collective-permute-done.3.refs_2_ = bf16[384,1024]{1,0:T(8,128)(2,1)S(1)} collective-permute-done((bf16[384,1024]{1,0:T(8,128)(2,1)S(1)}, bf16[384,1024]{1,0:T(8,128)(2,1)S(1)}, u32[]{:S(2)}, u32[]{:S(2)}) %collective-permute-start.3) | collective-permute-done | bytes 786464 | tf_op jit(solution)/shard_map/ppermute | solution.py:473
  42.0 15.5 %collective-permute-done.6.refs_2_ = bf16[192,768]{1,0:T(8,128)(2,1)S(1)} collective-permute-done((bf16[192,768]{1,0:T(8,128)(2,1)S(1)}, bf16[192,768]{1,0:T(8,128)(2,1)S(1)}, u32[]{:S(2)}, u32[]{:S(2)}) %collective-permute-start.6) | collective-permute-done | bytes 294944 | tf_op jit(solution)/shard_map/ppermute | solution.py:473
  73.2 6.5 %attend.1 = (bf16[384,768]{1,0:T(8,128)(2,1)S(1)}, bf16[384,1024]{1,0:T(8,128)(2,1)S(1)}, f32[384,128]{1,0:T(8,128)S(1)}, f32[8,128]{1,0:T(8,128)S(1)}) custom-call(s32[14]{0:T(128)S(1)} %concatenate.38.refs_0_, bf16[384,1536]{1,0:T(8,128)(2,1)S(1)} %get-tuple-element.182.refs_1_, bf16[768,1024]{1,0:T(8,128)(2,1)S(1)} %get-tuple-element.185.refs_2_.refs_4_, ...), custom_call_target="tpu_custom_call" | custom-call | flops 1000 | bytes 1000 | tf_op jit(solution)/shard_map/attend/pallas_call | solution.py:499
  79.7 5.2 collective-permute-done.11.refs_3_
  87.1 5.4 %collective-permute-start.10 = (bf16[192,1152]{1,0:T(8,128)(2,1)S(1)}, bf16[192,1152]{1,0:T(8,128)(2,1)S(1)}, u32[]{:S(2)}, u32[]{:S(2)}) collective-permute-start(bf16[192,1152]{1,0:T(8,128)(2,1)S(1)} %get-tuple-element.200), channel_id=1, source_target_pairs={{0,8},{1,17},{2,10},{3,19},{4,12},{5,21},{6,14},{7,23},{8,0},{9,25... | collective-permute-start | bytes 1327112 | tf_op jit(solution)/shard_map/ppermute | solution.py:473
  92.5 10.9 %collective-permute-done.10.refs_2_ = bf16[192,1152]{1,0:T(8,128)(2,1)S(1)} collective-permute-done((bf16[192,1152]{1,0:T(8,128)(2,1)S(1)}, bf16[192,1152]{1,0:T(8,128)(2,1)S(1)}, u32[]{:S(2)}, u32[]{:S(2)}) %collective-permute-start.10) | collective-permute-done | bytes 442400 | tf_op jit(solution)/shard_map/ppermute | solution.py:473
  104.1 3.0 project.1
  114.9 18.9 %collective-permute-done.14.refs_3_ = bf16[192,1152]{1,0:T(8,128)(2,1)S(1)} collective-permute-done((bf16[192,1152]{1,0:T(8,128)(2,1)S(1)}, bf16[192,1152]{1,0:T(8,128)(2,1)S(1)}, u32[]{:S(2)}, u32[]{:S(2)}) %collective-permute-start.14) | collective-permute-done | bytes 442400 | tf_op jit(solution)/shard_map/ppermute | solution.py:473
  139.7 26.9 %collective-permute-done.16.refs_2_ = bf16[384,1536]{1,0:T(8,128)(2,1)S(1)} collective-permute-done((bf16[384,1536]{1,0:T(8,128)(2,1)S(1)}, bf16[384,1536]{1,0:T(8,128)(2,1)S(1)}, u32[]{:S(2)}, u32[]{:S(2)}) %collective-permute-start.16) | collective-permute-done | bytes 1179680 | tf_op jit(solution)/shard_map/ppermute | solution.py:473
  166.9 15.1 %collective-permute-done.19.refs_2_ = bf16[192,1536]{1,0:T(8,128)(2,1)S(1)} collective-permute-done((bf16[192,1536]{1,0:T(8,128)(2,1)S(1)}, bf16[192,1536]{1,0:T(8,128)(2,1)S(1)}, u32[]{:S(2)}, u32[]{:S(2)}) %collective-permute-start.19) | collective-permute-done | bytes 589856 | tf_op jit(solution)/shard_map/ppermute | solution.py:473
  183.5 3.4 collective-permute-done.21.refs_2_
  190.7 19.7 %forward.1 = (bf16[1536,1152]{1,0:T(8,128)(2,1)S(1)}, bf16[1536,1152]{1,0:T(8,128)(2,1)S(1)}, bf16[1536,1152]{1,0:T(8,128)(2,1)S(1)}, f32[8,128]{1,0:T(8,128)S(1)}) custom-call(s32[14]{0:T(128)S(1)} %concatenate.38.refs_0_, bf16[1536,1536]{1,0:T(8,128)(2,1)S(1)} %get-tuple-element.222.refs_1_, bf16[768,2304]{1,0:T(8,128)(2,1)S(1)} %get-tuple-element.223.refs_2_.refs_4_, ...), custom_call_target="tpu_custom_call" | custom-call | flops 1000 | bytes 1000 | tf_op jit(solution)/shard_map/forward/pallas_call | solution.py:499
  217.3 8.7 %down_sum.1 = (bf16[768,1536]{1,0:T(8,128)(2,1)S(1)}, bf16[768,1536]{1,0:T(8,128)(2,1)S(1)}, f32[8,128]{1,0:T(8,128)S(1)}) custom-call(s32[14]{0:T(128)S(1)} %concatenate.38.refs_0_, bf16[1536,1152]{1,0:T(8,128)(2,1)S(1)} %get-tuple-element.227.refs_1_.refs_2_, bf16[768,1152]{1,0:T(8,128)(2,1)S(1)} %get-tuple-element.228.refs_2_.refs_6_, ...), custom_call_target="tpu_custom_call" | custom-call | flops 1000 | bytes 1000 | tf_op jit(solution)/shard_map/down_sum/pallas_call | solution.py:499
  226.7 5.6 %collective-permute-done.25.refs_3_ = bf16[384,1536]{1,0:T(8,128)(2,1)S(1)} collective-permute-done((bf16[384,1536]{1,0:T(8,128)(2,1)S(1)}, bf16[384,1536]{1,0:T(8,128)(2,1)S(1)}, u32[]{:S(2)}, u32[]{:S(2)}) %collective-permute-start.25) | collective-permute-done | bytes 1179680 | tf_op jit(solution)/shard_map/ppermute | solution.py:476
  239.4 4.3 grads_sent.4
  251.3 31.5 %backward.1 = (bf16[1536,2304]{1,0:T(8,128)(2,1)}, bf16[768,1536]{1,0:T(8,128)(2,1)S(1)}, bf16[768,1536]{1,0:T(8,128)(2,1)}, f32[8,128]{1,0:T(8,128)S(1)}) custom-call(s32[14]{0:T(128)S(1)} %concatenate.38.refs_0_, bf16[1536,1536]{1,0:T(8,128)(2,1)} %copy-done, bf16[1536,1152]{1,0:T(8,128)(2,1)S(1)} %copy-done.25, bf16[1536,1152]{1,0:T(8,128)(2,1)S(1)} %copy-done.27, ...), custom_call_target="tpu_custom_call" | custom-call | flops 1000 | bytes 1000 | tf_op jit(solution)/shard_map/backward/pallas_call | solution.py:499
  285.3 20.4 %collective-permute-done.28.refs_3_ = bf16[768,1152]{1,0:T(8,128)(2,1)S(1)} collective-permute-done((bf16[768,1152]{1,0:T(8,128)(2,1)}, bf16[768,1152]{1,0:T(8,128)(2,1)S(1)}, u32[]{:S(2)}, u32[]{:S(2)}) %collective-permute-start.28) | collective-permute-done | bytes 1769504 | tf_op jit(solution)/shard_map/ppermute | solution.py:473
  307.8 4.5 grads_kept.4
  318.8 8.5 %grads_sent.5 = (bf16[768,2304]{1,0:T(8,128)(2,1)}, f32[8,128]{1,0:T(8,128)S(1)}) custom-call(s32[14]{0:T(128)S(1)} %concatenate.38.refs_0_, bf16[1536,1536]{1,0:T(8,128)(2,1)S(1)} %get-tuple-element.222.refs_1_, bf16[1536,2304]{1,0:T(8,128)(2,1)S(1)} %copy-done.4, f32[8,128]{1,0:T(8,128)S(1)} %get-tuple-element.253.refs_3_), custom_call_target="tpu_custom_call" | custom-call | flops 1000 | bytes 1000 | tf_op jit(solution)/shard_map/grads_sent/pallas_call | solution.py:499
  332.1 19.9 %collective-permute-done.30.refs_2_ = bf16[384,1152]{1,0:T(8,128)(2,1)S(1)} collective-permute-done((bf16[384,1152]{1,0:T(8,128)(2,1)}, bf16[384,1152]{1,0:T(8,128)(2,1)S(1)}, u32[]{:S(2)}, u32[]{:S(2)}) %collective-permute-start.30) | collective-permute-done | bytes 884768 | tf_op jit(solution)/shard_map/ppermute | solution.py:473
  353.9 12.2 %collective-permute-done.29.refs_3_ = bf16[192,1536]{1,0:T(8,128)(2,1)S(1)} collective-permute-done((bf16[192,1536]{1,0:T(8,128)(2,1)}, bf16[192,1536]{1,0:T(8,128)(2,1)S(1)}, u32[]{:S(2)}, u32[]{:S(2)}) %collective-permute-start.29) | collective-permute-done | bytes 589856 | tf_op jit(solution)/shard_map/ppermute | solution.py:473
  373.0 21.5 %collective-permute-done.34.refs_2_ = bf16[192,1152]{1,0:T(8,128)(2,1)S(1)} collective-permute-done((bf16[192,1152]{1,0:T(8,128)(2,1)S(1)}, bf16[192,1152]{1,0:T(8,128)(2,1)S(1)}, u32[]{:S(2)}, u32[]{:S(2)}) %collective-permute-start.34) | collective-permute-done | bytes 442400 | tf_op jit(solution)/shard_map/ppermute | solution.py:473
  396.5 7.1 %grads_kept.5 = (bf16[384,2304]{1,0:T(8,128)(2,1)S(1)}, bf16[384,2304]{1,0:T(8,128)(2,1)S(1)}, f32[8,128]{1,0:T(8,128)S(1)}) custom-call(s32[14]{0:T(128)S(1)} %concatenate.38.refs_0_, bf16[1536,1536]{1,0:T(8,128)(2,1)S(1)} %get-tuple-element.222.refs_1_, bf16[1536,2304]{1,0:T(8,128)(2,1)S(1)} %bitcast.32, ...), custom_call_target="tpu_custom_call" | custom-call | flops 1000 | bytes 1000 | tf_op jit(solution)/shard_map/grads_kept/pallas_call | solution.py:499
  407.5 9.8 %attend_back.1 = (bf16[384,1024]{1,0:T(8,128)(2,1)S(1)}, f32[1,1024]{1,0:T(1,128)S(1)}, f32[192,1536]{1,0:T(8,128)S(1)}, bf16[192,1536]{1,0:T(8,128)(2,1)S(1)}, f32[8,128]{1,0:T(8,128)S(1)}) custom-call(s32[14]{0:T(128)S(1)} %concatenate.38.refs_0_, bf16[384,1536]{1,0:T(8,128)(2,1)S(1)} %get-tuple-element.270.refs_1_, ...), custom_call_target="tpu_custom_call" | custom-call | flops 1000 | bytes 1000 | tf_op jit(solution)/shard_map/attend_back/pallas_call | solution.py:499
  421.4 13.4 %collective-permute-done.40.refs_3_ = bf16[192,1152]{1,0:T(8,128)(2,1)S(1)} collective-permute-done((bf16[192,1152]{1,0:T(8,128)(2,1)S(1)}, bf16[192,1152]{1,0:T(8,128)(2,1)S(1)}, u32[]{:S(2)}, u32[]{:S(2)}) %collective-permute-start.40) | collective-permute-done | bytes 442400 | tf_op jit(solution)/shard_map/ppermute | solution.py:473
  436.8 18.5 %collective-permute-done.39.refs_3_ = bf16[768,768]{1,0:T(8,128)(2,1)S(1)} collective-permute-done((bf16[768,768]{1,0:T(8,128)(2,1)S(1)}, bf16[768,768]{1,0:T(8,128)(2,1)S(1)}, u32[]{:S(2)}, u32[]{:S(2)}) %collective-permute-start.39) | collective-permute-done | bytes 1179680 | tf_op jit(solution)/shard_map/ppermute | solution.py:473
  471.7 10.9 %collective-permute-done.42 = f32[32,128]{1,0:T(8,128)S(1)} collective-permute-done((f32[32,128]{1,0:T(8,128)S(1)}, f32[32,128]{1,0:T(8,128)S(1)}, u32[]{:S(2)}, u32[]{:S(2)}) %collective-permute-start.42) | collective-permute-done | bytes 16416 | tf_op jit(solution)/shard_map/ppermute | solution.py:473
  499.9 14.9 %collective-permute-done.51.refs_2_ = bf16[192,768]{1,0:T(8,128)(2,1)S(1)} collective-permute-done((bf16[192,768]{1,0:T(8,128)(2,1)S(1)}, bf16[192,768]{1,0:T(8,128)(2,1)S(1)}, u32[]{:S(2)}, u32[]{:S(2)}) %collective-permute-start.51) | collective-permute-done | bytes 294944 | tf_op jit(solution)/shard_map/ppermute | solution.py:473
  515.5 4.1 collective-permute-start.54
  519.6 11.8 %collective-permute-done.50.refs_2_ = bf16[192,1024]{1,0:T(8,128)(2,1)S(1)} collective-permute-done((bf16[192,1024]{1,0:T(8,128)(2,1)S(1)}, bf16[192,1024]{1,0:T(8,128)(2,1)S(1)}, u32[]{:S(2)}, u32[]{:S(2)}) %collective-permute-start.50) | collective-permute-done | bytes 393248 | tf_op jit(solution)/shard_map/ppermute | solution.py:473
  (315 shorter events, 164.7 us)
Async XLA Ops:
  30.4 29.0 %collective-permute-start.8 = (bf16[192,2304]{1,0:T(8,128)(2,1)}, bf16[192,2304]{1,0:T(8,128)(2,1)}, u32[]{:S(2)}, u32[]{:S(2)}) collective-permute-start(bf16[192,2304]{1,0:T(8,128)(2,1)} %get-tuple-element.192), channel_id=1, source_target_pairs={{0,8},{1,17},{2,10},{3,19},{4,12},{5,21},{6,14},{7,23},{8,0},{9,25... | collective-permute-start | bytes 2654216 | tf_op jit(solution)/shard_map/ppermute | solution.py:473
  40.4 32.8 %collective-permute-start.4 = (bf16[768,1024]{1,0:T(8,128)(2,1)S(1)}, bf16[768,1024]{1,0:T(8,128)(2,1)}, u32[]{:S(2)}, u32[]{:S(2)}) collective-permute-start(bf16[768,1024]{1,0:T(8,128)(2,1)S(1)} %get-tuple-element.185.refs_2_.refs_4_), channel_id=1, source_target_pairs={{0,4},{1,3},{2,6},{3,1},{4,0},{5,7},{6,2},{7,5},{8,12},{9,11},{10,... | collective-permute-start | bytes 4718600 | tf_op jit(solution)/shard_map/ppermute | solution.py:473
  62.8 22.2 %collective-permute-start.11 = (bf16[192,2304]{1,0:T(8,128)(2,1)}, bf16[192,2304]{1,0:T(8,128)(2,1)}, u32[]{:S(2)}, u32[]{:S(2)}) collective-permute-start(bf16[192,2304]{1,0:T(8,128)(2,1)} %get-tuple-element.201), channel_id=1, source_target_pairs={{0,16},{1,9},{2,18},{3,11},{4,20},{5,13},{6,22},{7,15},{8,24},{9,1... | collective-permute-start | bytes 2654216 | tf_op jit(solution)/shard_map/ppermute | solution.py:473
  69.7 34.4 %collective-permute-start.9 = (bf16[768,768]{1,0:T(8,128)(2,1)}, bf16[768,768]{1,0:T(8,128)(2,1)}, u32[]{:S(2)}, u32[]{:S(2)}) collective-permute-start(bf16[768,768]{1,0:T(8,128)(2,1)} %get-tuple-element.198.refs_2_), channel_id=1, source_target_pairs={{0,4},{1,3},{2,6},{3,1},{4,0},{5,7},{6,2},{7,5},{8,12},{9,11},{10,... | collective-permute-start | bytes 3538952 | tf_op jit(solution)/shard_map/ppermute | solution.py:473
  86.5 27.6 %collective-permute-start.15 = (bf16[384,2304]{1,0:T(8,128)(2,1)S(1)}, bf16[384,2304]{1,0:T(8,128)(2,1)S(1)}, u32[]{:S(2)}, u32[]{:S(2)}) collective-permute-start(bf16[384,2304]{1,0:T(8,128)(2,1)S(1)} %get-tuple-element.212.refs_1_), channel_id=1, source_target_pairs={{0,2},{1,5},{2,0},{3,7},{4,6},{5,1},{6,4},{7,3},{8,10},{9,13},{10,... | collective-permute-start | bytes 5308424 | tf_op jit(solution)/shard_map/ppermute | solution.py:473
  111.2 25.0 %collective-permute-start.13 = (bf16[192,1536]{1,0:T(8,128)(2,1)S(1)}, bf16[192,1536]{1,0:T(8,128)(2,1)S(1)}, u32[]{:S(2)}, u32[]{:S(2)}) collective-permute-start(bf16[192,1536]{1,0:T(8,128)(2,1)S(1)} %get-tuple-element.210.refs_1_), channel_id=1, source_target_pairs={{0,8},{1,17},{2,10},{3,19},{4,12},{5,21},{6,14},{7,23},{8,0},{9,25... | collective-permute-start | bytes 1769480 | tf_op jit(solution)/shard_map/ppermute | solution.py:473
  111.2 22.6 %collective-permute-start.14 = (bf16[192,1152]{1,0:T(8,128)(2,1)S(1)}, bf16[192,1152]{1,0:T(8,128)(2,1)S(1)}, u32[]{:S(2)}, u32[]{:S(2)}) collective-permute-start(bf16[192,1152]{1,0:T(8,128)(2,1)S(1)} %get-tuple-element.211), channel_id=1, source_target_pairs={{0,16},{1,9},{2,18},{3,11},{4,20},{5,13},{6,22},{7,15},{8,24},{9,1... | collective-permute-start | bytes 1327112 | tf_op jit(solution)/shard_map/ppermute | solution.py:473
  136.8 29.8 %collective-permute-start.16 = (bf16[384,1536]{1,0:T(8,128)(2,1)S(1)}, bf16[384,1536]{1,0:T(8,128)(2,1)S(1)}, u32[]{:S(2)}, u32[]{:S(2)}) collective-permute-start(bf16[384,1536]{1,0:T(8,128)(2,1)S(1)} %get-tuple-element.218.refs_1_), channel_id=1, source_target_pairs={{0,16},{1,9},{2,18},{3,11},{4,20},{5,13},{6,22},{7,15},{8,24},{9,1... | collective-permute-start | bytes 3538952 | tf_op jit(solution)/shard_map/ppermute | solution.py:473
  138.6 52.1 %collective-permute-start.20 = (bf16[768,2304]{1,0:T(8,128)(2,1)S(1)}, bf16[768,2304]{1,0:T(8,128)(2,1)S(1)}, u32[]{:S(2)}, u32[]{:S(2)}) collective-permute-start(bf16[768,2304]{1,0:T(8,128)(2,1)S(1)} %get-tuple-element.223.refs_2_.refs_4_), channel_id=1, source_target_pairs={{0,4},{1,3},{2,6},{3,1},{4,0},{5,7},{6,2},{7,5},{8,12},{9,11},{10,... | collective-permute-start | bytes 10616840 | tf_op jit(solution)/shard_map/ppermute | solution.py:473
  139.7 43.0 %collective-permute-start.17 = (bf16[384,1536]{1,0:T(8,128)(2,1)S(1)}, bf16[384,1536]{1,0:T(8,128)(2,1)S(1)}, u32[]{:S(2)}, u32[]{:S(2)}) collective-permute-start(bf16[384,1536]{1,0:T(8,128)(2,1)S(1)} %get-tuple-element.218.refs_1_), channel_id=1, source_target_pairs={{0,1},{1,0},{2,3},{3,2},{4,5},{5,4},{6,7},{7,6},{8,9},{9,8},{10,11... | collective-permute-start | bytes 3538952 | tf_op jit(solution)/shard_map/ppermute | solution.py:476
  166.6 20.4 %collective-permute-start.21 = (bf16[384,1152]{1,0:T(8,128)(2,1)S(1)}, bf16[384,1152]{1,0:T(8,128)(2,1)S(1)}, u32[]{:S(2)}, u32[]{:S(2)}) collective-permute-start(bf16[384,1152]{1,0:T(8,128)(2,1)S(1)} %get-tuple-element.224.refs_1_), channel_id=1, source_target_pairs={{0,2},{1,5},{2,0},{3,7},{4,6},{5,1},{6,4},{7,3},{8,10},{9,13},{10,... | collective-permute-start | bytes 2654216 | tf_op jit(solution)/shard_map/ppermute | solution.py:473
  187.6 26.4 %collective-permute-start.22 = (bf16[768,1152]{1,0:T(8,128)(2,1)S(1)}, bf16[768,1152]{1,0:T(8,128)(2,1)S(1)}, u32[]{:S(2)}, u32[]{:S(2)}) collective-permute-start(bf16[768,1152]{1,0:T(8,128)(2,1)S(1)} %get-tuple-element.228.refs_2_.refs_6_), channel_id=1, source_target_pairs={{0,4},{1,3},{2,6},{3,1},{4,0},{5,7},{6,2},{7,5},{8,12},{9,11},{10,... | collective-permute-start | bytes 5308424 | tf_op jit(solution)/shard_map/ppermute | solution.py:473
  188.9 37.7 %collective-permute-start.24 = (bf16[384,1536]{1,0:T(8,128)(2,1)S(1)}, bf16[384,1536]{1,0:T(8,128)(2,1)S(1)}, u32[]{:S(2)}, u32[]{:S(2)}) collective-permute-start(bf16[384,1536]{1,0:T(8,128)(2,1)S(1)} %get-tuple-element.232.refs_1_), channel_id=1, source_target_pairs={{0,16},{1,9},{2,18},{3,11},{4,20},{5,13},{6,22},{7,15},{8,24},{9,1... | collective-permute-start | bytes 3538952 | tf_op jit(solution)/shard_map/ppermute | solution.py:473
  282.8 31.8 %collective-permute-start.31 = (bf16[768,1536]{1,0:T(8,128)(2,1)}, bf16[768,1536]{1,0:T(8,128)(2,1)S(1)}, u32[]{:S(2)}, u32[]{:S(2)}) collective-permute-start(bf16[768,1536]{1,0:T(8,128)(2,1)} %get-tuple-element.251), channel_id=1, source_target_pairs={{0,1},{1,0},{2,3},{3,2},{4,5},{5,4},{6,7},{7,6},{8,9},{9,8},{10,11... | collective-permute-start | bytes 7077896 | tf_op jit(solution)/shard_map/ppermute | solution.py:476
  283.0 22.7 %collective-permute-start.28 = (bf16[768,1152]{1,0:T(8,128)(2,1)}, bf16[768,1152]{1,0:T(8,128)(2,1)S(1)}, u32[]{:S(2)}, u32[]{:S(2)}) collective-permute-start(bf16[768,1152]{1,0:T(8,128)(2,1)} %copy-done.56), channel_id=1, source_target_pairs={{0,4},{1,3},{2,6},{3,1},{4,0},{5,7},{6,2},{7,5},{8,12},{9,11},{10,... | collective-permute-start | bytes 5308424 | tf_op jit(solution)/shard_map/ppermute | solution.py:473
  283.7 30.0 %collective-permute-start.27 = (bf16[384,1536]{1,0:T(8,128)(2,1)}, bf16[384,1536]{1,0:T(8,128)(2,1)S(1)}, u32[]{:S(2)}, u32[]{:S(2)}) collective-permute-start(bf16[384,1536]{1,0:T(8,128)(2,1)} %copy-done.57), channel_id=1, source_target_pairs={{0,16},{1,9},{2,18},{3,11},{4,20},{5,13},{6,22},{7,15},{8,24},{9,1... | collective-permute-start | bytes 3538952 | tf_op jit(solution)/shard_map/ppermute | solution.py:473
  327.4 69.1 %collective-permute-start.36 = (bf16[768,2304]{1,0:T(8,128)(2,1)}, bf16[768,2304]{1,0:T(8,128)(2,1)S(1)}, u32[]{:S(2)}, u32[]{:S(2)}) collective-permute-start(bf16[768,2304]{1,0:T(8,128)(2,1)} %get-tuple-element.267), channel_id=1, source_target_pairs={{0,4},{1,3},{2,6},{3,1},{4,0},{5,7},{6,2},{7,5},{8,12},{9,11},{10,... | collective-permute-start | bytes 10616840 | tf_op jit(solution)/shard_map/ppermute | solution.py:473
  328.7 41.3 %collective-permute-start.32 = (bf16[384,1536]{1,0:T(8,128)(2,1)}, bf16[384,1536]{1,0:T(8,128)(2,1)S(1)}, u32[]{:S(2)}, u32[]{:S(2)}) collective-permute-start(bf16[384,1536]{1,0:T(8,128)(2,1)} %get-tuple-element.258), channel_id=1, source_target_pairs={{0,16},{1,9},{2,18},{3,11},{4,20},{5,13},{6,22},{7,15},{8,24},{9,1... | collective-permute-start | bytes 3538952 | tf_op jit(solution)/shard_map/ppermute | solution.py:473
  329.1 22.8 %collective-permute-start.30 = (bf16[384,1152]{1,0:T(8,128)(2,1)}, bf16[384,1152]{1,0:T(8,128)(2,1)S(1)}, u32[]{:S(2)}, u32[]{:S(2)}) collective-permute-start(bf16[384,1152]{1,0:T(8,128)(2,1)} %copy-done.58), channel_id=1, source_target_pairs={{0,2},{1,5},{2,0},{3,7},{4,6},{5,1},{6,4},{7,3},{8,10},{9,13},{10,... | collective-permute-start | bytes 2654216 | tf_op jit(solution)/shard_map/ppermute | solution.py:473
  330.3 35.8 %collective-permute-start.29 = (bf16[192,1536]{1,0:T(8,128)(2,1)}, bf16[192,1536]{1,0:T(8,128)(2,1)S(1)}, u32[]{:S(2)}, u32[]{:S(2)}) collective-permute-start(bf16[192,1536]{1,0:T(8,128)(2,1)} %copy-done.59), channel_id=1, source_target_pairs={{0,8},{1,17},{2,10},{3,19},{4,12},{5,21},{6,14},{7,23},{8,0},{9,25... | collective-permute-start | bytes 1769480 | tf_op jit(solution)/shard_map/ppermute | solution.py:473
  370.9 24.2 %collective-permute-start.33 = (bf16[192,1536]{1,0:T(8,128)(2,1)S(1)}, bf16[192,1536]{1,0:T(8,128)(2,1)S(1)}, u32[]{:S(2)}, u32[]{:S(2)}) collective-permute-start(bf16[192,1536]{1,0:T(8,128)(2,1)S(1)} %get-tuple-element.261), channel_id=1, source_target_pairs={{0,8},{1,17},{2,10},{3,19},{4,12},{5,21},{6,14},{7,23},{8,0},{9,25... | collective-permute-start | bytes 1769480 | tf_op jit(solution)/shard_map/ppermute | solution.py:473
  371.4 23.1 %collective-permute-start.34 = (bf16[192,1152]{1,0:T(8,128)(2,1)S(1)}, bf16[192,1152]{1,0:T(8,128)(2,1)S(1)}, u32[]{:S(2)}, u32[]{:S(2)}) collective-permute-start(bf16[192,1152]{1,0:T(8,128)(2,1)S(1)} %get-tuple-element.263), channel_id=1, source_target_pairs={{0,8},{1,17},{2,10},{3,19},{4,12},{5,21},{6,14},{7,23},{8,0},{9,25... | collective-permute-start | bytes 1327112 | tf_op jit(solution)/shard_map/ppermute | solution.py:473
  403.7 54.4 %collective-permute-start.38 = (bf16[384,2304]{1,0:T(8,128)(2,1)S(1)}, bf16[384,2304]{1,0:T(8,128)(2,1)S(1)}, u32[]{:S(2)}, u32[]{:S(2)}) collective-permute-start(bf16[384,2304]{1,0:T(8,128)(2,1)S(1)} %get-tuple-element.279), channel_id=1, source_target_pairs={{0,2},{1,5},{2,0},{3,7},{4,6},{5,1},{6,4},{7,3},{8,10},{9,13},{10,... | collective-permute-start | bytes 5308424 | tf_op jit(solution)/shard_map/ppermute | solution.py:473
  419.2 44.9 %collective-permute-start.46 = (bf16[768,1024]{1,0:T(8,128)(2,1)S(1)}, bf16[768,1024]{1,0:T(8,128)(2,1)S(1)}, u32[]{:S(2)}, u32[]{:S(2)}) collective-permute-start(bf16[768,1024]{1,0:T(8,128)(2,1)S(1)} %get-tuple-element.292), channel_id=1, source_target_pairs={{0,4},{1,3},{2,6},{3,1},{4,0},{5,7},{6,2},{7,5},{8,12},{9,11},{10,... | collective-permute-start | bytes 4718600 | tf_op jit(solution)/shard_map/ppermute | solution.py:473
  421.2 34.1 %collective-permute-start.39 = (bf16[768,768]{1,0:T(8,128)(2,1)S(1)}, bf16[768,768]{1,0:T(8,128)(2,1)S(1)}, u32[]{:S(2)}, u32[]{:S(2)}) collective-permute-start(bf16[768,768]{1,0:T(8,128)(2,1)S(1)} %get-tuple-element.280), channel_id=1, source_target_pairs={{0,4},{1,3},{2,6},{3,1},{4,0},{5,7},{6,2},{7,5},{8,12},{9,11},{10,... | collective-permute-start | bytes 3538952 | tf_op jit(solution)/shard_map/ppermute | solution.py:473
  421.3 38.6 %collective-permute-start.37 = (bf16[192,1536]{1,0:T(8,128)(2,1)S(1)}, bf16[192,1536]{1,0:T(8,128)(2,1)S(1)}, u32[]{:S(2)}, u32[]{:S(2)}) collective-permute-start(bf16[192,1536]{1,0:T(8,128)(2,1)S(1)} %get-tuple-element.276), channel_id=1, source_target_pairs={{0,1},{1,0},{2,3},{3,2},{4,5},{5,4},{6,7},{7,6},{8,9},{9,8},{10,11... | collective-permute-start | bytes 1769480 | tf_op jit(solution)/shard_map/ppermute | solution.py:476
  459.9 26.1 %collective-permute-start.48 = (bf16[192,2304]{1,0:T(8,128)(2,1)}, bf16[192,2304]{1,0:T(8,128)(2,1)S(1)}, u32[]{:S(2)}, u32[]{:S(2)}) collective-permute-start(bf16[192,2304]{1,0:T(8,128)(2,1)} %get-tuple-element.297), channel_id=1, source_target_pairs={{0,8},{1,17},{2,10},{3,19},{4,12},{5,21},{6,14},{7,23},{8,0},{9,25... | collective-permute-start | bytes 2654216 | tf_op jit(solution)/shard_map/ppermute | solution.py:473
  463.5 20.2 %collective-permute-start.49 = (bf16[384,768]{1,0:T(8,128)(2,1)}, bf16[384,768]{1,0:T(8,128)(2,1)}, u32[]{:S(2)}, u32[]{:S(2)}) collective-permute-start(bf16[384,768]{1,0:T(8,128)(2,1)} %get-tuple-element.299), channel_id=1, source_target_pairs={{0,2},{1,5},{2,0},{3,7},{4,6},{5,1},{6,4},{7,3},{8,10},{9,13},{10,... | collective-permute-start | bytes 1769480 | tf_op jit(solution)/shard_map/ppermute | solution.py:473
  467.9 28.2 %collective-permute-start.47 = (bf16[384,1024]{1,0:T(8,128)(2,1)}, bf16[384,1024]{1,0:T(8,128)(2,1)}, u32[]{:S(2)}, u32[]{:S(2)}) collective-permute-start(bf16[384,1024]{1,0:T(8,128)(2,1)} %get-tuple-element.295), channel_id=1, source_target_pairs={{0,2},{1,5},{2,0},{3,7},{4,6},{5,1},{6,4},{7,3},{8,10},{9,13},{10,... | collective-permute-start | bytes 2359304 | tf_op jit(solution)/shard_map/ppermute | solution.py:473
  486.6 47.3 %collective-permute-start.53 = (bf16[192,2304]{1,0:T(8,128)(2,1)S(1)}, bf16[192,2304]{1,0:T(8,128)(2,1)S(1)}, u32[]{:S(2)}, u32[]{:S(2)}) collective-permute-start(bf16[192,2304]{1,0:T(8,128)(2,1)S(1)} %get-tuple-element.311), channel_id=1, source_target_pairs={{0,16},{1,9},{2,18},{3,11},{4,20},{5,13},{6,22},{7,15},{8,24},{9,1... | collective-permute-start | bytes 2654216 | tf_op jit(solution)/shard_map/ppermute | solution.py:473
  494.4 20.5 %collective-permute-start.51 = (bf16[192,768]{1,0:T(8,128)(2,1)S(1)}, bf16[192,768]{1,0:T(8,128)(2,1)S(1)}, u32[]{:S(2)}, u32[]{:S(2)}) collective-permute-start(bf16[192,768]{1,0:T(8,128)(2,1)S(1)} %get-tuple-element.306), channel_id=1, source_target_pairs={{0,16},{1,9},{2,18},{3,11},{4,20},{5,13},{6,22},{7,15},{8,24},{9,1... | collective-permute-start | bytes 884744 | tf_op jit(solution)/shard_map/ppermute | solution.py:473
  497.5 33.9 %collective-permute-start.50 = (bf16[192,1024]{1,0:T(8,128)(2,1)S(1)}, bf16[192,1024]{1,0:T(8,128)(2,1)S(1)}, u32[]{:S(2)}, u32[]{:S(2)}) collective-permute-start(bf16[192,1024]{1,0:T(8,128)(2,1)S(1)} %get-tuple-element.304), channel_id=1, source_target_pairs={{0,16},{1,9},{2,18},{3,11},{4,20},{5,13},{6,22},{7,15},{8,24},{9,1... | collective-permute-start | bytes 1179656 | tf_op jit(solution)/shard_map/ppermute | solution.py:473
  (93 other events, 1127.5 us)

commit v3 on v2

--- a/solution.py
+++ b/solution.py
@@ -469,7 +469,8 @@
         perm = []
         for place in range(self.dp):
             for core in range(2):
-                perm.append((place * 2 + core, (place ^ bits[core][phase]) * 2 + core))
+                flip = bits[core][phase] if phase < 2 else bits[core][0] ^ bits[core][1]
+                perm.append((place * 2 + core, (place ^ flip) * 2 + core))
         return lax.ppermute(array, ("dp", "tensor"), perm)
 
     def other_core(self, array):
@@ -524,7 +525,7 @@
     return run(kernel, not isinstance(out_shape, (list, tuple)), (info,) + args)
 
 
-def small(body, out_shape, scratch, info, *args, mib=16):
+def small(body, out_shape, scratch, info, *args, mib=10):
     outs = as_list(out_shape)
     late = 0 if CLOCK[0] is None else 1
     kernel = pl.pallas_call(
@@ -547,6 +548,27 @@
     return small(body, shape(array.shape, array.dtype), [], info, array)
 
 
+def spacer(topo):
+    CLOCK[0] = topo.other_core(CLOCK[0])
+
+
+def wait_for(info, *arrays):
+    def body(*refs):
+        del refs
+
+    late = 0 if CLOCK[0] is None else 1
+    kernel = pl.pallas_call(
+        body,
+        in_specs=[ANY] * len(arrays) + [IN_VMEM] * late,
+        out_specs=[IN_VMEM],
+        out_shape=[TOKEN],
+        compiler_params=pltpu.CompilerParams(vmem_limit_bytes=16 * 2**20),
+        cost_estimate=pl.CostEstimate(flops=1, bytes_accessed=1, transcendentals=0),
+        name="wait_for",
+    )
+    (CLOCK[0],) = kernel(*arrays, *([CLOCK[0]] if late else []))
+
+
 def join(info, *args):
     def body(info_ref, *refs):
         start = 0
@@ -556,6 +578,22 @@
 
     rows = sum(a.shape[0] for a in args)
     return small(body, shape((rows,) + args[0].shape[1:], args[0].dtype), [], info, *args)
+
+
+def join_split(info, widths, *args):
+    rows = sum(a.shape[0] for a in args)
+
+    def body(info_ref, *refs):
+        ins, outs = refs[: len(args)], refs[len(args) :]
+        low = 0
+        for ref in ins:
+            start = 0
+            for out, cols in zip(outs, widths):
+                out[low : low + ref.shape[0]] = ref[:, start : start + cols]
+                start += cols
+            low += ref.shape[0]
+
+    return small(body, [shape((rows, cols), BF) for cols in widths], [], info, *args)
 
 
 def beside(info, *args):
@@ -703,24 +741,18 @@
 
 
 def state_rows(info, rows, own, got, gain):
-    def body(info_ref, rows_ref, own_ref, got_ref, gain_ref, out_ref, state_ref):
-        start = pl.multiple_of(info_ref[OTHER] * dims[0], 16)
-        got = got_ref[pl.ds(start, dims[0])] if got_ref.shape[0] > dims[0] else got_ref[...]
-        values = rows_ref[...].astype(F32) + (own_ref[...] + got.astype(F32))
-        state_ref[...] = values
-        factor = lax.rsqrt(jnp.mean(values * values, axis=1, keepdims=True) + EPSILON)
-        out_ref[...] = (values * factor * gain_ref[...]).astype(BF)
+    def body(info_ref, rows_ref, own_ref, early_ref, late_ref, gain_ref, out_ref, state_ref):
+        half = dims[0] // 2
+        for start, got_ref in ((0, early_ref), (half, late_ref)):
+            span = pl.ds(start, half)
+            values = rows_ref[span].astype(F32) + (own_ref[span] + got_ref[...].astype(F32))
+            state_ref[span] = values
+            factor = lax.rsqrt(jnp.mean(values * values, axis=1, keepdims=True) + EPSILON)
+            out_ref[span] = (values * factor * gain_ref[...]).astype(BF)
 
     dims = rows.shape
     return small(
-        body,
-        [shape(dims, BF), shape(dims, F32)],
-        [],
-        info,
-        rows,
-        own,
-        got,
-        gain,
+        body, [shape(dims, BF), shape(dims, F32)], [], info, rows, own, *got, gain
     )
 
 
@@ -826,6 +858,7 @@
         rows,
         *pieces,
         *plain,
+        mib=20,
     )
 
 
@@ -835,15 +868,16 @@
 
     def body(info_ref, in_ref, *refs):
         pieces = refs[:count]
-        other_ref, own_ref = refs[count:]
+        early_ref, late_ref, own_ref = refs[count:]
         for cols, piece in square_blocks(info_ref, pieces, width):
             both = nt(in_ref[...], piece)
             own_ref[:, cols] = both[:half]
-            other_ref[:, cols] = both[half:].astype(BF)
+            early_ref[:, cols] = both[half : half + half // 2].astype(BF)
+            late_ref[:, cols] = both[half + half // 2 :].astype(BF)
 
     return small(
         body,
-        [shape((half, width), BF), shape((half, width), F32)],
+        [shape((half // 2, width), BF)] * 2 + [shape((half, width), F32)],
         [],
         info,
         rows,
@@ -912,6 +946,7 @@
         *o_pieces,
         *pieces,
         *plain,
+        mib=24,
     )
 
 
@@ -968,6 +1003,7 @@
         info,
         x,
         *gate_up,
+        mib=24,
     )
 
 
@@ -982,6 +1018,16 @@
         pl.BlockSpec((tile, width), lambda i, _: (jnp.minimum(i, half - 1), 0)),
         pl.BlockSpec((tile, width), later),
     ]
+
+
+def cut_rows(info, array, count):
+    rows = array.shape[0] // count
+
+    def body(info_ref, in_ref, *outs):
+        for index, out in enumerate(outs):
+            out[...] = in_ref[index * rows : (index + 1) * rows]
+
+    return small(body, [shape((rows, array.shape[1]), array.dtype)] * count, [], info, array)
 
 
 def store_half(value, steps, first_ref, second_ref):
@@ -1026,18 +1072,19 @@
         info,
         hidden,
         *down,
-    )
-
-
-def backward(info, g, gate_factor, up_factor, gate_up, down, tile, step=256):
-    count, part = len(down), down[0].shape[1]
-    total, width = g.shape
+        mib=18,
+    )
+
+
+def backward(info, half, g, gate_factor, up_factor, gate_up, down, tile, step=256):
+    count, up_count, part = len(down), len(gate_up), down[0].shape[1]
+    total, width = g.shape[0] // 2, g.shape[1]
     steps = total // tile
     spans = [(low, min(low + step, part)) for low in range(0, part, step)]
 
     def body(info_ref, g_ref, gate_ref, up_ref, *refs):
-        gate_up, down = refs[:count], refs[count : 2 * count]
-        grad_ref, own_ref, other_ref, weight, sems = refs[2 * count :]
+        gate_up, down = refs[:up_count], refs[up_count : up_count + count]
+        back_ref, grad_ref, weight, sems = refs[up_count + count :]
 
         def span_copies(index):
             yield from piece_copies(info_ref, down, weight, sems.at[index], spans[index], 2 * part)
@@ -1074,16 +1121,15 @@
             for copy in late_copies():
                 copy.wait()
 
-        value = nt(grad_ref[...], weight[:, : 2 * part]).astype(BF)
-        store_half(value, steps, own_ref, other_ref)
+        back_ref[...] = nt(grad_ref[...], weight[:, : 2 * part]).astype(BF)
 
     return call(
         body,
         (steps,),
-        [pl.BlockSpec((tile, cols), lambda i, _: (i, 0)) for cols in (width, part, part)]
-        + [ANY] * (2 * count),
-        [pl.BlockSpec((tile, 2 * part), lambda i, _: (i, 0))] + halves_spec(tile, width, steps, False),
-        [shape((total, 2 * part), BF)] + [shape((total // 2, width), BF)] * 2,
+        [pl.BlockSpec((tile, cols), lambda i, _: (half * steps + i, 0)) for cols in (width, part, part)]
+        + [ANY] * (up_count + count),
+        [pl.BlockSpec((tile, cols), lambda i, _: (i, 0)) for cols in (width, 2 * part)],
+        [shape((total, cols), BF) for cols in (width, 2 * part)],
         [
             pltpu.VMEM((width, 3 * part), BF),
             pltpu.SemaphoreType.DMA((len(spans) + 1, LINE)),
@@ -1097,6 +1143,45 @@
     )
 
 
+def rows_spec(block, rights, where):
+    rows = rights[0].shape[0]
+    return [
+        pl.BlockSpec((rows, block), lambda i, info_ref, r=r: (r, info_ref[OFF + where(i)]))
+        for r in range(len(rights))
+    ]
+
+
+def grads_of(info, left, rights, block, index, got=None):
+    rows, cols = rights[0].shape
+    parts = len(rights)
+    tile = next(t for t in (768, 512, 384, 256, 128) if cols % t == 0)
+
+    def body(info_ref, *refs):
+        value = 0.0
+        for r in range(parts):
+            value = value + tn(refs[r][...], refs[parts + r][...])
+        if got is not None:
+            value = value + refs[2 * parts][...].astype(F32)
+        refs[-1][...] = value.astype(BF)
+
+    out = pl.BlockSpec((block, tile), lambda i, _: (0, i))
+    return call(
+        body,
+        (cols // tile,),
+        rows_spec(block, rights, lambda i: index)
+        + [pl.BlockSpec((rows, tile), lambda i, _: (0, i))] * parts
+        + ([] if got is None else [out]),
+        out,
+        shape((block, cols), BF),
+        [],
+        info,
+        *([left] * parts),
+        *rights,
+        *([] if got is None else [got]),
+        mib=20,
+    )
+
+
 def grads_sent(info, left, right, block):
     total, cols = right.shape
 
@@ -1106,16 +1191,14 @@
     return call(
         body,
         (2,),
-        [
-            pl.BlockSpec((total, block), lambda i, info_ref: (0, info_ref[OFF + 2 + i])),
-            whole(right.shape),
-        ],
+        rows_spec(block, [right], lambda i: 2 + i) + [whole(right.shape)],
         pl.BlockSpec((block, cols), lambda i, _: (i, 0)),
         shape((2 * block, cols), BF),
         [],
         info,
         left,
         right,
+        mib=20,
     )
 
 
@@ -1129,11 +1212,8 @@
     return call(
         body,
         (2,),
-        [
-            pl.BlockSpec((total, block), lambda i, info_ref: (0, info_ref[OFF + i])),
-            whole(right.shape),
-            pl.BlockSpec((block, cols), lambda i, _: (i, 0)),
-        ],
+        rows_spec(block, [right], lambda i: i)
+        + [whole(right.shape), pl.BlockSpec((block, cols), lambda i, _: (i, 0))],
         [whole((block, cols))] * 2,
         [shape((block, cols), BF)] * 2,
         [],
@@ -1141,24 +1221,37 @@
         left,
         right,
         got,
-    )
-
-
-def sum_split(info, block, count, keep_at, send_at, left, right):
+        mib=20,
+    )
+
+
+def sum_split(info, block, count, keep_at, send_at, left, *rights):
     cols = left.shape[1]
-
-    def body(info_ref, left_ref, right_ref, *outs):
+    pieces = len(rights)
+    rows_each = rights[0].shape[0]
+
+    def body(info_ref, left_ref, *refs):
+        right_refs, outs = refs[:pieces], refs[pieces:]
         for out, (first, stride, along) in zip(outs, (keep_at, send_at)):
             for step in range(count):
                 index = first + stride * step
                 if along:
                     rows = pl.ds(pl.multiple_of(info_ref[NEIGHBOUR + index] * block, 16), block)
-                else:
-                    rows = pl.ds(index * block, block)
-                total = left_ref[rows].astype(F32) + right_ref[rows].astype(F32)
-                out[step * block : (step + 1) * block] = total.astype(BF)
-
-    return small(body, [shape((count * block, cols), BF)] * 2, [], info, left, right)
+                    total = left_ref[rows].astype(F32) + right_refs[0][rows].astype(F32)
+                    out[step * block : (step + 1) * block] = total.astype(BF)
+                    continue
+                low, high = index * block, (index + 1) * block
+                while low < high:
+                    which = low // rows_each
+                    end = min(high, (which + 1) * rows_each)
+                    base = which * rows_each
+                    total = left_ref[low:end].astype(F32)
+                    total = total + right_refs[which][low - base : end - base].astype(F32)
+                    start = step * block + low - index * block
+                    out[start : start + end - low] = total.astype(BF)
+                    low = end
+
+    return small(body, [shape((count * block, cols), BF)] * 2, [], info, left, *rights)
 
 
 def sum_out(info, left, right, widths):
@@ -1179,6 +1272,15 @@
         left,
         right,
     )
+
+
+def sum_rows(info, own, got, first):
+    def body(info_ref, own_ref, got_ref, out_ref):
+        if first:
+            out_ref[:first] = own_ref[:first]
+        out_ref[first:] = own_ref[first:] + got_ref[first:]
+
+    return small(body, shape(own.shape, F32), [], info, own, got)
 
 
 def columns_out(info, kept, got, last, part, cols):
@@ -1248,12 +1350,12 @@
     q_heads, kv_heads = q_cols // HEAD_DIM, kv_cols // HEAD_DIM
     tile = local_rows * LINE // 2
 
-    q_own = beside(info, q_weight, k_weight, v_weight)
-    q_one = topo.swap(q_own, line, 0)
+    attn_own_weight = beside(info, q_weight, k_weight, v_weight, o_weight)
+    attn_one = topo.swap(attn_own_weight, line, 0)
     gate_up_send, gate_up_keep = cut_columns(info, part, gate_weight, up_weight)
 
-    q_joined = join(info, q_own, q_one)
-    q_two = topo.swap(q_joined, line, 1)
+    attn_joined = join(info, attn_own_weight, attn_one)
+    attn_two = topo.swap(attn_joined, line, 1)
     bias_all = jnp.concatenate([q_bias, k_bias, v_bias]).astype(F32)[None, :]
     gains = jnp.stack([attn_gain, mlp_gain]).astype(F32)
     attn_own, inputs, gains = open_rows(info, tokens, gains)
@@ -1275,94 +1377,92 @@
     from_line = [(0, 0), (0, shard_rows), (1, 0), (1, shard_rows)]
     from_exchange = [(0, 0), (1, 0), (2, 0), (2, shard_rows)]
 
-    o_own = join(info, o_weight)
-    o_one = topo.swap(o_own, line, 0)
-    q_piece = placed(info, shard_rows, from_line, q_joined, q_two)
-    q_near = topo.swap(q_piece, square, 0)
+    attn_piece = placed(info, shard_rows, from_line, attn_joined, attn_two)
+    attn_near = topo.swap(attn_piece, square, 0)
     gate_up_one = topo.swap(tie(info, gate_up_send), line, 0)
     attn_in = join(info, attn_own, attn_other)
-    q_all = [join(info, q_piece, q_near)]
-    q_all.append(topo.swap(q_all[0], square, 1))
-    o_joined = join(info, o_own, o_one)
-    o_two = topo.swap(o_joined, line, 1)
-    o_piece = placed(info, shard_rows, from_line, o_joined, o_two)
-    o_near = topo.swap(o_piece, square, 0)
+    q_joined, o_joined = join_split(info, (qkv_cols, q_cols), attn_piece, attn_near)
+    q_all = [q_joined, topo.swap(q_joined, square, 1)]
+    o_all = [o_joined, topo.swap(o_joined, square, 1)]
     gate_up_two = topo.swap(second_chunks(info, gate_up_keep, gate_up_one), line, 1)
-    o_all = [join(info, o_piece, o_near)]
-    o_all.append(topo.swap(o_all[0], square, 1))
+
+    mixed, linear, mass = attend(
+        info, attn_in, q_all, bias_all, cosine, sine, row_info, col_info, q_heads, kv_heads
+    )
     down_send, down_keep = cut_columns(info, part, down_weight)
     down_one = topo.swap(down_send, line, 0)
-
-    mixed, linear, mass = attend(
-        info, attn_in, q_all, bias_all, cosine, sine, row_info, col_info, q_heads, kv_heads
-    )
     gate_up_piece = placed(
         info, shard_rows, from_exchange, gate_up_keep, gate_up_one, gate_up_two
     )
     gate_up_near = topo.swap(gate_up_piece, square, 0)
-    down_two = topo.swap(second_chunks(info, down_keep, down_one), line, 1)
-    other_attn, own_attn = project(info, mixed, o_all, width)
-    other_attn = topo.other_core(other_attn)
+    *other_attn, own_attn = project(info, mixed, o_all, width)
+    gate_up_far = topo.swap(gate_up_piece, square, 1)
+    other_attn = [topo.other_core(half_rows) for half_rows in other_attn]
     mlp_own, state = state_rows(info, inputs, own_attn, other_attn, gain_two)
     mlp_one = topo.swap(mlp_own, line, 0)
-    grad_out_one = topo.swap(tie(info, out_grad_in), line, 0)
-
-    gate_up = [join(info, gate_up_piece, gate_up_near)]
-    gate_up.append(topo.swap(gate_up[0], square, 1))
-    down_piece = placed(info, shard_rows, from_exchange, down_keep, down_one, down_two)
-    down_near = topo.swap(down_piece, square, 0)
+
+    down_two = topo.swap(second_chunks(info, down_keep, down_one), line, 1)
     mlp_half = join(info, mlp_own, mlp_one)
     mlp_two = topo.swap(mlp_half, line, 1)
     mlp_early = topo.other_core(mlp_half)
-    grad_out_half = join(info, out_grad_in, grad_out_one)
-    grad_out_two = topo.swap(grad_out_half, line, 1)
-    mlp_late = topo.other_core(mlp_two)
-    mlp_in = join(info, mlp_half, mlp_two, mlp_early, mlp_late)
+    down_piece = placed(info, shard_rows, from_exchange, down_keep, down_one, down_two)
+    wait_for(info, gate_up_near, gate_up_far)
+    gate_up_last = topo.swap(tie(info, gate_up_near), square, 1)
+    down_near = topo.swap(down_piece, square, 0)
+    wait_for(info, mlp_two)
+    mlp_late = topo.other_core(tie(info, mlp_two))
+    grad_out_one = topo.swap(tie(info, out_grad_in), line, 0)
+    wait_for(info, gate_up_last)
+    gate_up = [gate_up_piece, gate_up_near, gate_up_far, gate_up_last]
     down = [join(info, down_piece, down_near)]
     down.append(topo.swap(down[0], square, 1))
-    grad_out_early = topo.other_core(grad_out_half)
+    mlp_in = join(info, mlp_half, mlp_two, mlp_early, mlp_late)
+    grad_out_two = topo.swap(tie(info, out_grad_in), line, 1)
 
     hidden, gate_factor, up_factor = forward(info, mlp_in, gate_up, tile)
-    grad_out_late = topo.other_core(grad_out_two)
+    wait_for(info, grad_out_one, grad_out_two)
+    grad_out_last = topo.swap(tie(info, grad_out_one), line, 1)
     out_own, out_other = down_sum(info, hidden, down, tile, width)
     out_other = topo.other_core(out_other)
-    grad_out_all = join(info, grad_out_half, grad_out_two, grad_out_early, grad_out_late)
     pair = (0, 1, False), (2, 1, False)
+    single = (0, 1, False), (1, 1, False)
+    chunks = (0, 2, True), (1, 2, True)
     rows = local_rows
+    grad_out_half = join(info, out_grad_in, grad_out_one, grad_out_two, grad_out_last)
+    grad_out_all = join(info, grad_out_half, topo.other_core(grad_out_half))
     out_keep, out_send = sum_split(info, rows, 2, *pair, out_own, out_other)
     out_one = topo.swap(out_send, line, 1)
-    down_full = grads_sent(info, grad_out_all, hidden, block)
-    down_got = topo.swap(down_full, square, 1)
-    grads, back_own, back_other = backward(
-        info, grad_out_all, gate_factor, up_factor, gate_up, down, tile
-    )
-    back_other = topo.other_core(back_other)
-    down_kept, down_send = grads_kept(info, grad_out_all, hidden, block, down_got)
-    down_last = topo.swap(down_send, square, 0)
-    single = (0, 1, False), (1, 1, False)
+    factors = (grad_out_all, gate_factor, up_factor, gate_up, down)
+    back_other, grads_other = backward(info, 1, *factors, tile)
+    back_other = [topo.other_core(part_rows) for part_rows in cut_rows(info, back_other, 2)]
+    down_grad = functools.partial(grads_of, info, grad_out_all, [hidden], block)
+    down_first = topo.swap(down_grad(3), square, 1)
+    down_next = topo.swap(down_grad(2), square, 1)
     out_keep, out_send = sum_split(info, rows, 1, *single, out_keep, out_one)
     out_two = topo.swap(out_send, line, 0)
-    back_keep, back_send = sum_split(info, rows, 2, *pair, back_own, back_other)
+    back_own, grads_own = backward(info, 0, *factors, tile)
+    wait_for(info, out_two, down_first, down_next)
+    back_keep, back_send = sum_split(info, rows, 2, *pair, back_own, *back_other)
     back_one = topo.swap(back_send, line, 1)
-    gate_up_full = grads_sent(info, mlp_in, grads, block)
-    gate_up_got = topo.swap(gate_up_full, square, 1)
-    chunks = (0, 2, True), (1, 2, True)
-    down_keep, down_send = sum_split(info, shard_rows, 2, *chunks, down_kept, down_last)
-    down_one = topo.swap(down_send, line, 0)
-    block_out = close_rows(info, state, out_keep, out_two)
+    gate_up_grad = functools.partial(grads_of, info, mlp_in, [grads_own, grads_other], block)
+    down_last = topo.swap(down_grad(1, down_first), square, 0)
+    gate_up_first = topo.swap(gate_up_grad(3), square, 1)
+    gate_up_send = gate_up_grad(2)
+    down_kept = down_grad(0, down_next)
     back_keep, back_send = sum_split(info, rows, 1, *single, back_keep, back_one)
     back_two = topo.swap(back_send, line, 0)
-    down_two = topo.swap(second_chunks(info, down_keep, down_one), line, 1)
+    down_keep, down_send = sum_split(info, shard_rows, 2, *chunks, down_kept, down_last)
+    gate_up_next = topo.swap(tie(info, gate_up_send), square, 1)
+    gate_up_send = gate_up_grad(1, gate_up_first)
+    gate_up_last = topo.swap(gate_up_send, square, 0)
+    block_out = close_rows(info, state, out_keep, out_two)
 
     grad_state_low, grad_state, gain_two_grad = norm_back(
         info, state, back_keep, back_two, out_grad_in, gain_two, False
     )
     state_other = topo.other_core(grad_state_low)
-    gate_up_kept, gate_up_send = grads_kept(info, mlp_in, grads, block, gate_up_got)
-    gate_up_last = topo.swap(gate_up_send, square, 0)
+    down_one = topo.swap(tie(info, down_send), line, 0)
     grad_state_all = join(info, grad_state_low, state_other)
-    o_full = grads_sent(info, grad_state_all, mixed, block)
-    o_got = topo.swap(o_full, square, 1)
     grad_linear, bias_grad, own_part, other_part = attend_back(
         info,
         grad_state_all,
@@ -1378,46 +1478,55 @@
         kv_heads,
     )
     part_other = topo.other_core(other_part)
+    down_two = topo.swap(second_chunks(info, down_keep, down_one), line, 1)
+    gate_up_kept = gate_up_grad(0, gate_up_next)
+    gate_up_keep, gate_up_send = sum_split(
+        info, shard_rows, 2, *chunks, gate_up_kept, gate_up_last
+    )
+    gate_up_one = topo.swap(gate_up_send, line, 0)
     q_full = grads_sent(info, attn_in, grad_linear, block)
     q_got = topo.swap(q_full, square, 1)
+    o_full = grads_sent(info, grad_state_all, mixed, block)
+    o_got = topo.swap(o_full, square, 1)
+    tokens_grad, gain_one_grad = norm_back(
+        info, inputs, own_part, part_other, grad_state, gain_one, True
+    )
+    sums = jnp.concatenate([bias_grad, gain_one_grad, gain_two_grad], axis=1)
+    sums = sums.reshape(-1, LANES)
+    shared = qkv_cols // LANES
+    sums_got = topo.other_core(sums)
     (down_grads,) = columns_out(info, down_keep, down_one, down_two, part, ff_cols)
+    sums = sum_rows(info, sums, sums_got, shared)
+    sums_got = topo.swap(sums, square, 0)
+
+    gate_up_two = topo.swap(second_chunks(info, gate_up_keep, gate_up_one), line, 1)
+    q_kept, q_send = grads_kept(info, attn_in, grad_linear, block, q_got)
+    q_last = topo.swap(q_send, square, 0)
     o_kept, o_send = grads_kept(info, grad_state_all, mixed, block, o_got)
     o_last = topo.swap(o_send, square, 0)
-    gate_up_keep, gate_up_send = sum_split(
-        info, shard_rows, 2, *chunks, gate_up_kept, gate_up_last
-    )
-    gate_up_one = topo.swap(gate_up_send, line, 0)
-    tokens_grad, gain_one_grad = norm_back(
-        info, inputs, own_part, part_other, grad_state, gain_one, True
-    )
-    gain_grads = jnp.concatenate([gain_one_grad, gain_two_grad], axis=0)
-    gain_grads = gain_grads + topo.other_core(gain_grads)
-    sums = jnp.concatenate([bias_grad.reshape(-1), gain_grads.reshape(-1)]).reshape(-1, LANES)
-    sums = sums + topo.swap(sums, line, 0)
-
-    q_kept, q_send = grads_kept(info, attn_in, grad_linear, block, q_got)
-    q_last = topo.swap(q_send, square, 0)
-    sums = sums + topo.swap(sums, line, 1)
+    sums = sum_rows(info, sums, sums_got, 0)
+    sums_got = topo.swap(sums, square, 1)
     ordered = (0, 1, True), (2, 1, True)
+    q_keep, q_send = sum_split(info, shard_rows, 2, *ordered, q_kept, q_last)
+    q_one = topo.swap(q_send, line, 1)
     o_keep, o_send = sum_split(info, shard_rows, 2, *ordered, o_kept, o_last)
     o_one = topo.swap(o_send, line, 1)
-    sums = sums + topo.swap(sums, square, 0)
-    gate_up_two = topo.swap(second_chunks(info, gate_up_keep, gate_up_one), line, 1)
-    sums = sums + topo.swap(sums, square, 1)
-    sums = sums.reshape(-1)
+    sums = sum_rows(info, sums, sums_got, 0)
+    sums_got = topo.swap(sums, line, 0)
+    q_keep, q_send = sum_split(info, shard_rows, 1, *single, q_keep, q_one)
+    q_two = topo.swap(q_send, line, 0)
+    sums = sum_rows(info, sums, sums_got, 0)
+    sums_got = topo.swap(sums, line, 1)
+    o_keep, o_send = sum_split(info, shard_rows, 1, *single, o_keep, o_one)
+    o_two = topo.swap(o_send, line, 0)
+    gate_grads, up_grads = columns_out(
+        info, gate_up_keep, gate_up_one, gate_up_two, part, ff_cols
+    )
+    q_grads, k_grads, v_grads = sum_out(info, q_keep, q_two, (q_cols, kv_cols, kv_cols))
+    (o_grads,) = sum_out(info, o_keep, o_two, (q_cols,))
+    sums = sum_rows(info, sums, sums_got, 0).reshape(-1)
     own_bias = sums[:qkv_cols]
     gain_sum = sums[qkv_cols:].reshape(2, width)
-    q_keep, q_send = sum_split(info, shard_rows, 2, *ordered, q_kept, q_last)
-    q_one = topo.swap(q_send, line, 1)
-    o_keep, o_send = sum_split(info, shard_rows, 1, *single, o_keep, o_one)
-    o_two = topo.swap(o_send, line, 0)
-    q_keep, q_send = sum_split(info, shard_rows, 1, *single, q_keep, q_one)
-    q_two = topo.swap(q_send, line, 0)
-    (o_grads,) = sum_out(info, o_keep, o_two, (q_cols,))
-    gate_grads, up_grads = columns_out(
-        info, gate_up_keep, gate_up_one, gate_up_two, part, ff_cols
-    )
-    q_grads, k_grads, v_grads = sum_out(info, q_keep, q_two, (q_cols, kv_cols, kv_cols))
     CLOCK[0] = None
     return (
         block_out,

time: 549 us -> 475 us (0.87)
  waiting for transfers between devices: 275 us -> 193 us
  Pallas kernels: 161 us -> 178 us
  local copies, waits for them, and re-layouts: 35.1 us -> 24 us
    ppermute x44 -> x45, waiting for transfers between devices: 266 us -> 186 us  [swap(): return lax.ppermute(array, ('dp', 'tensor'), perm)]
    pallas_call x60 -> x72, Pallas kernels: 161 us -> 178 us  [run(): *out, CLOCK[0] = kernel(*args, *taken)]
    unnamed x140 -> x164, local copies, waits for them, and re-layouts: 33.1 us -> 20.8 us
    ppermute x44 -> x45, starting transfers between devices: 62.2 us -> 62.9 us  [swap(): return lax.ppermute(array, ('dp', 'tensor'), perm)]
  transfers between devices with their start and end apart: 55 -> 57, of which waited for: 30 -> 28; matrix products, arithmetic and copies ran while one was open for 1% -> 1% of each run, Pallas kernels for 20% -> 34%
where the time goes in v3:
time: 475 us; the launch traced here: 466 us
  waiting for transfers between devices  193 us (41%)
  Pallas kernels  178 us (37%)
  starting transfers between devices  65.7 us (14%)
  local copies, waits for them, and re-layouts  24 us (5%)
    ppermute x45, waiting for transfers between devices, swap(): return lax.ppermute(array, ('dp', 'tensor'), perm)  186 us
    pallas_call x72, Pallas kernels, run(): *out, CLOCK[0] = kernel(*args, *taken)  178 us
    ppermute x45, starting transfers between devices, swap(): return lax.ppermute(array, ('dp', 'tensor'), perm)  62.9 us
    unnamed x164, local copies, waits for them, and re-layouts  20.8 us
  transfers between devices with their start and end apart: 57, of which 28 were waited for; matrix products, arithmetic and copies ran while one was open for 1% of the time, Pallas kernels for 34%

profile of v3, /device:TPU:0, one launch (start us, length us, event | category | flops | bytes accessed | tf_op | source)
XLA Modules:
  0.0 465.7 jit_solution(157147517839979867)
XLA Ops:
  10.8 5.5 %collective-permute-done.refs_2_ = bf16[96,1792]{1,0:T(8,128)(2,1)S(1)} collective-permute-done((bf16[96,1792]{1,0:T(8,128)(2,1)S(1)}, bf16[96,1792]{1,0:T(8,128)(2,1)S(1)}, u32[]{:S(2)}, u32[]{:S(2)}) %collective-permute-start) | collective-permute-done | bytes 344096 | tf_op jit(solution)/shard_map/ppermute | solution.py:474
  22.2 12.3 %collective-permute-done.2.refs_2_ = bf16[192,1792]{1,0:T(8,128)(2,1)S(1)} collective-permute-done((bf16[192,1792]{1,0:T(8,128)(2,1)S(1)}, bf16[192,1792]{1,0:T(8,128)(2,1)S(1)}, u32[]{:S(2)}, u32[]{:S(2)}) %collective-permute-start.2) | collective-permute-done | bytes 688160 | tf_op jit(solution)/shard_map/ppermute | solution.py:474
  44.5 9.4 %collective-permute-done.3.refs_2_ = bf16[384,1792]{1,0:T(8,128)(2,1)} collective-permute-done((bf16[384,1792]{1,0:T(8,128)(2,1)S(1)}, bf16[384,1792]{1,0:T(8,128)(2,1)}, u32[]{:S(2)}, u32[]{:S(2)}) %collective-permute-start.3) | collective-permute-done | bytes 1376288 | tf_op jit(solution)/shard_map/ppermute | solution.py:474
  70.8 7.6 %collective-permute-done.4.refs_3_.refs_5_ = bf16[768,1024]{1,0:T(8,128)(2,1)} collective-permute-done((bf16[768,1024]{1,0:T(8,128)(2,1)S(1)}, bf16[768,1024]{1,0:T(8,128)(2,1)}, u32[]{:S(2)}, u32[]{:S(2)}) %collective-permute-start.4) | collective-permute-done | bytes 1572896 | tf_op jit(solution)/shard_map/ppermute | solution.py:474
  78.4 6.6 %attend.1 = (bf16[384,768]{1,0:T(8,128)(2,1)S(1)}, bf16[384,1024]{1,0:T(8,128)(2,1)S(1)}, f32[384,128]{1,0:T(8,128)S(1)}, f32[8,128]{1,0:T(8,128)S(1)}) custom-call(s32[14]{0:T(128)S(1)} %concatenate.35.refs_0_, bf16[384,1536]{1,0:T(8,128)(2,1)S(1)} %get-tuple-element.206.refs_1_, bf16[768,1024]{1,0:T(8,128)(2,1)S(1)} %get-tuple-element.209.refs_2_.refs_4_, ...), custom_call_target="tpu_custom_call" | custom-call | flops 1000 | bytes 1000 | tf_op jit(solution)/shard_map/attend/pallas_call | solution.py:500
  100.0 11.4 %collective-permute-done.11.refs_2_ = bf16[192,1152]{1,0:T(8,128)(2,1)S(1)} collective-permute-done((bf16[192,1152]{1,0:T(8,128)(2,1)S(1)}, bf16[192,1152]{1,0:T(8,128)(2,1)S(1)}, u32[]{:S(2)}, u32[]{:S(2)}) %collective-permute-start.11) | collective-permute-done | bytes 442400 | tf_op jit(solution)/shard_map/ppermute | solution.py:474
  112.0 14.5 %collective-permute-done.10.refs_2_ = bf16[192,1536]{1,0:T(8,128)(2,1)S(1)} collective-permute-done((bf16[192,1536]{1,0:T(8,128)(2,1)S(1)}, bf16[192,1536]{1,0:T(8,128)(2,1)S(1)}, u32[]{:S(2)}, u32[]{:S(2)}) %collective-permute-start.10) | collective-permute-done | bytes 589856 | tf_op jit(solution)/shard_map/ppermute | solution.py:474
  135.4 21.6 %collective-permute-done.12.refs_0_.refs_1_.refs_2_ = bf16[384,1536]{1,0:T(8,128)(2,1)S(1)} collective-permute-done((bf16[384,1536]{1,0:T(8,128)(2,1)S(1)}, bf16[384,1536]{1,0:T(8,128)(2,1)S(1)}, u32[]{:S(2)}, u32[]{:S(2)}) %collective-permute-start.12) | collective-permute-done | bytes 1179680 | tf_op jit(solution)/shard_map/ppermute | solution.py:474
  168.6 19.9 %forward.1 = (bf16[1536,1152]{1,0:T(8,128)(2,1)S(1)}, bf16[1536,1152]{1,0:T(8,128)(2,1)S(1)}, bf16[1536,1152]{1,0:T(8,128)(2,1)S(1)}, f32[8,128]{1,0:T(8,128)S(1)}) custom-call(s32[14]{0:T(128)S(1)} %concatenate.35.refs_0_, bf16[1536,1536]{1,0:T(8,128)(2,1)S(1)} %get-tuple-element.244.refs_1_.refs_2_, ...), custom_call_target="tpu_custom_call" | custom-call | flops 1000 | bytes 1000 | tf_op jit(solution)/shard_map/forward/pallas_call | solution.py:500
  190.8 3.5 collective-permute-start.24
  194.3 8.7 %down_sum.1 = (bf16[768,1536]{1,0:T(8,128)(2,1)S(1)}, bf16[768,1536]{1,0:T(8,128)(2,1)S(1)}, f32[8,128]{1,0:T(8,128)S(1)}) custom-call(s32[14]{0:T(128)S(1)} %concatenate.35.refs_0_, bf16[1536,1152]{1,0:T(8,128)(2,1)S(1)} %get-tuple-element.247.refs_1_.refs_2_, bf16[768,1152]{1,0:T(8,128)(2,1)S(1)} %get-tuple-element.248.refs_2_.refs_8_, ...), custom_call_target="tpu_custom_call" | custom-call | flops 1000 | bytes 1000 | tf_op jit(solution)/shard_map/down_sum/pallas_call | solution.py:500
  203.0 4.0 collective-permute-done.24.refs_4_
  208.3 4.0 collective-permute-done.25.refs_2_
  222.8 16.4 %backward.2 = (bf16[768,1536]{1,0:T(8,128)(2,1)S(1)}, bf16[768,2304]{1,0:T(8,128)(2,1)S(1)}, f32[8,128]{1,0:T(8,128)S(1)}) custom-call(s32[14]{0:T(128)S(1)} %concatenate.35.refs_0_, bf16[1536,1536]{1,0:T(8,128)(2,1)} %copy-done, bf16[1536,1152]{1,0:T(8,128)(2,1)S(1)} %copy-done.16, bf16[1536,1152]{1,0:T(8,128)(2,1)} %copy-done.17, ...), custom_call_target="tpu_custom_call" | custom-call | flops 1000 | bytes 1000 | tf_op jit(solution)/shard_map/backward/pallas_call | solution.py:500
  242.7 4.4 grads_of.8
  247.1 4.2 grads_of.9
  256.6 3.8 collective-permute-start.27
  260.5 16.3 %backward.3 = (bf16[768,1536]{1,0:T(8,128)(2,1)S(1)}, bf16[768,2304]{1,0:T(8,128)(2,1)S(1)}, f32[8,128]{1,0:T(8,128)S(1)}) custom-call(s32[14]{0:T(128)S(1)} %concatenate.35.refs_0_, bf16[1536,1536]{1,0:T(8,128)(2,1)} %copy-done, bf16[1536,1152]{1,0:T(8,128)(2,1)S(1)} %copy-done.16, bf16[1536,1152]{1,0:T(8,128)(2,1)} %copy-done.17, ...), custom_call_target="tpu_custom_call" | custom-call | flops 1000 | bytes 1000 | tf_op jit(solution)/shard_map/backward/pallas_call | solution.py:500
  279.1 4.8 %grads_of.10 = (bf16[384,1152]{1,0:T(8,128)(2,1)S(1)}, f32[8,128]{1,0:T(8,128)S(1)}) custom-call(s32[14]{0:T(128)S(1)} %concatenate.35.refs_0_, bf16[1536,1536]{1,0:T(8,128)(2,1)S(1)} %bitcast.26, bf16[1536,1152]{1,0:T(8,128)(2,1)S(1)} %get-tuple-element.247.refs_1_.refs_2_, bf16[384,1152]{1,0:T(8,128)(2,1)} %collective-permute-done.28.refs_1_.refs_3_, ...), custom_call_target="tpu_custom_call" | custom-call | flops 1000 | bytes 1000 | tf_op jit(solution)/shard_map/grads_of/pallas_call | solution.py:500
  283.9 4.6 grads_of.11
  290.4 4.6 grads_of.12
  295.0 4.4 grads_of.13
  299.4 19.8 %collective-permute-done.34.refs_2_ = bf16[384,1536]{1,0:T(8,128)(2,1)S(1)} collective-permute-done((bf16[384,1536]{1,0:T(8,128)(2,1)S(1)}, bf16[384,1536]{1,0:T(8,128)(2,1)S(1)}, u32[]{:S(2)}, u32[]{:S(2)}) %collective-permute-start.34) | collective-permute-done | bytes 1179680 | tf_op jit(solution)/shard_map/ppermute | solution.py:474
  322.7 5.0 %grads_of.14 = (bf16[384,2304]{1,0:T(8,128)(2,1)S(1)}, f32[8,128]{1,0:T(8,128)S(1)}) custom-call(s32[14]{0:T(128)S(1)} %concatenate.35.refs_0_, bf16[1536,1536]{1,0:T(8,128)(2,1)S(1)} %get-tuple-element.244.refs_1_.refs_2_, bf16[1536,1536]{1,0:T(8,128)(2,1)S(1)} %get-tuple-element.244.refs_1_.refs_2_, bf16[768,2304]{1,0:T(8,128)(2,1)S(1)} %get-tuple-element.274.refs_3_, ...), custom_call_target="tpu_custom_call" | custom-call | flops 1000 | bytes 1000 | tf_op jit(solution)/shard_map/grads_of/pallas_call | solution.py:500
  330.9 12.3 %collective-permute-done.35.refs_3_ = bf16[192,1536]{1,0:T(8,128)(2,1)S(1)} collective-permute-done((bf16[192,1536]{1,0:T(8,128)(2,1)S(1)}, bf16[192,1536]{1,0:T(8,128)(2,1)S(1)}, u32[]{:S(2)}, u32[]{:S(2)}) %collective-permute-start.35) | collective-permute-done | bytes 589856 | tf_op jit(solution)/shard_map/ppermute | solution.py:474
  347.3 9.1 %attend_back.1 = (bf16[384,1024]{1,0:T(8,128)(2,1)S(1)}, f32[1,1024]{1,0:T(1,128)S(1)}, f32[192,1536]{1,0:T(8,128)S(1)}, bf16[192,1536]{1,0:T(8,128)(2,1)S(1)}, f32[8,128]{1,0:T(8,128)S(1)}) custom-call(s32[14]{0:T(128)S(1)} %concatenate.35.refs_0_, bf16[384,1536]{1,0:T(8,128)(2,1)S(1)} %get-tuple-element.305.refs_1_, bf16[768,768]{1,0:T(8,128)(2,1)S(1)} %copy-done.29, ...), custom_call_target="tpu_custom_call" | custom-call | flops 1000 | bytes 1000 | tf_op jit(solution)/shard_map/attend_back/pallas_call | solution.py:500
  358.4 3.4 collective-permute-done.38.refs_5_
  361.8 4.8 %grads_of.15 = (bf16[384,2304]{1,0:T(8,128)(2,1)S(1)}, f32[8,128]{1,0:T(8,128)S(1)}) custom-call(s32[14]{0:T(128)S(1)} %concatenate.35.refs_0_, bf16[1536,1536]{1,0:T(8,128)(2,1)S(1)} %get-tuple-element.244.refs_1_.refs_2_, bf16[1536,1536]{1,0:T(8,128)(2,1)S(1)} %get-tuple-element.244.refs_1_.refs_2_, bf16[768,2304]{1,0:T(8,128)(2,1)S(1)} %get-tuple-element.274.refs_3_, ...), custom_call_target="tpu_custom_call" | custom-call | flops 1000 | bytes 1000 | tf_op jit(solution)/shard_map/grads_of/pallas_call | solution.py:500
  376.6 23.8 %collective-permute-done.42.refs_3_ = bf16[192,1152]{1,0:T(8,128)(2,1)S(1)} collective-permute-done((bf16[192,1152]{1,0:T(8,128)(2,1)S(1)}, bf16[192,1152]{1,0:T(8,128)(2,1)S(1)}, u32[]{:S(2)}, u32[]{:S(2)}) %collective-permute-start.42) | collective-permute-done | bytes 442400 | tf_op jit(solution)/shard_map/ppermute | solution.py:474
  413.5 10.7 %collective-permute-done.43.refs_2_ = f32[32,128]{1,0:T(8,128)S(1)} collective-permute-done((f32[32,128]{1,0:T(8,128)S(1)}, f32[32,128]{1,0:T(8,128)S(1)}, u32[]{:S(2)}, u32[]{:S(2)}) %collective-permute-start.43) | collective-permute-done | bytes 16416 | tf_op jit(solution)/shard_map/ppermute | solution.py:474
  434.0 13.1 %collective-permute-done.51.refs_2_ = bf16[192,1024]{1,0:T(8,128)(2,1)S(1)} collective-permute-done((bf16[192,1024]{1,0:T(8,128)(2,1)S(1)}, bf16[192,1024]{1,0:T(8,128)(2,1)S(1)}, u32[]{:S(2)}, u32[]{:S(2)}) %collective-permute-start.51) | collective-permute-done | bytes 393248 | tf_op jit(solution)/shard_map/ppermute | solution.py:474
  449.8 4.7 %collective-permute-done.50.refs_2_ = f32[32,128]{1,0:T(8,128)S(1)} collective-permute-done((f32[32,128]{1,0:T(8,128)S(1)}, f32[32,128]{1,0:T(8,128)S(1)}, u32[]{:S(2)}, u32[]{:S(2)}) %collective-permute-start.50) | collective-permute-done | bytes 16416 | tf_op jit(solution)/shard_map/ppermute | solution.py:474
  (353 shorter events, 164.0 us)
Async XLA Ops:
  39.0 23.2 %collective-permute-start.5 = (bf16[192,2304]{1,0:T(8,128)(2,1)}, bf16[192,2304]{1,0:T(8,128)(2,1)}, u32[]{:S(2)}, u32[]{:S(2)}) collective-permute-start(bf16[192,2304]{1,0:T(8,128)(2,1)} %get-tuple-element.211), channel_id=1, source_target_pairs={{0,8},{1,17},{2,10},{3,19},{4,12},{5,21},{6,14},{7,23},{8,0},{9,25... | collective-permute-start | bytes 2654216 | tf_op jit(solution)/shard_map/ppermute | solution.py:474
  57.8 20.5 %collective-permute-start.4 = (bf16[768,1024]{1,0:T(8,128)(2,1)S(1)}, bf16[768,1024]{1,0:T(8,128)(2,1)}, u32[]{:S(2)}, u32[]{:S(2)}) collective-permute-start(bf16[768,1024]{1,0:T(8,128)(2,1)S(1)} %get-tuple-element.209.refs_2_.refs_4_), channel_id=1, source_target_pairs={{0,4},{1,3},{2,6},{3,1},{4,0},{5,7},{6,2},{7,5},{8,12},{9,11},{10,... | collective-permute-start | bytes 4718600 | tf_op jit(solution)/shard_map/ppermute | solution.py:474
  64.8 23.5 %collective-permute-start.7 = (bf16[192,2304]{1,0:T(8,128)(2,1)S(1)}, bf16[192,2304]{1,0:T(8,128)(2,1)S(1)}, u32[]{:S(2)}, u32[]{:S(2)}) collective-permute-start(bf16[192,2304]{1,0:T(8,128)(2,1)S(1)} %get-tuple-element.216), channel_id=1, source_target_pairs={{0,16},{1,9},{2,18},{3,11},{4,20},{5,13},{6,22},{7,15},{8,24},{9,1... | collective-permute-start | bytes 2654216 | tf_op jit(solution)/shard_map/ppermute | solution.py:474
  68.2 25.2 %collective-permute-start.6 = (bf16[768,768]{1,0:T(8,128)(2,1)S(1)}, bf16[768,768]{1,0:T(8,128)(2,1)S(1)}, u32[]{:S(2)}, u32[]{:S(2)}) collective-permute-start(bf16[768,768]{1,0:T(8,128)(2,1)S(1)} %copy-done.28), channel_id=1, source_target_pairs={{0,4},{1,3},{2,6},{3,1},{4,0},{5,7},{6,2},{7,5},{8,12},{9,11},{10,... | collective-permute-start | bytes 3538952 | tf_op jit(solution)/shard_map/ppermute | solution.py:474
  89.7 41.1 %collective-permute-start.15 = (bf16[384,2304]{1,0:T(8,128)(2,1)S(1)}, bf16[384,2304]{1,0:T(8,128)(2,1)S(1)}, u32[]{:S(2)}, u32[]{:S(2)}) collective-permute-start(bf16[384,2304]{1,0:T(8,128)(2,1)S(1)} %get-tuple-element.232.refs_2_.refs_4_), channel_id=1, source_target_pairs={{0,4},{1,3},{2,6},{3,1},{4,0},{5,7},{6,2},{7,5},{8,12},{9,11},{10,... | collective-permute-start | bytes 5308424 | tf_op jit(solution)/shard_map/ppermute | solution.py:474
  90.9 39.9 %collective-permute-start.14 = (bf16[384,2304]{1,0:T(8,128)(2,1)S(1)}, bf16[384,2304]{1,0:T(8,128)(2,1)S(1)}, u32[]{:S(2)}, u32[]{:S(2)}) collective-permute-start(bf16[384,2304]{1,0:T(8,128)(2,1)S(1)} %get-tuple-element.232.refs_2_.refs_4_), channel_id=1, source_target_pairs={{0,2},{1,5},{2,0},{3,7},{4,6},{5,1},{6,4},{7,3},{8,10},{9,13},{10,... | collective-permute-start | bytes 5308424 | tf_op jit(solution)/shard_map/ppermute | solution.py:474
  98.4 28.2 %collective-permute-start.10 = (bf16[192,1536]{1,0:T(8,128)(2,1)S(1)}, bf16[192,1536]{1,0:T(8,128)(2,1)S(1)}, u32[]{:S(2)}, u32[]{:S(2)}) collective-permute-start(bf16[192,1536]{1,0:T(8,128)(2,1)S(1)} %get-tuple-element.226.refs_1_), channel_id=1, source_target_pairs={{0,8},{1,17},{2,10},{3,19},{4,12},{5,21},{6,14},{7,23},{8,0},{9,25... | collective-permute-start | bytes 1769480 | tf_op jit(solution)/shard_map/ppermute | solution.py:474
  127.1 29.9 %collective-permute-start.12 = (bf16[384,1536]{1,0:T(8,128)(2,1)S(1)}, bf16[384,1536]{1,0:T(8,128)(2,1)S(1)}, u32[]{:S(2)}, u32[]{:S(2)}) collective-permute-start(bf16[384,1536]{1,0:T(8,128)(2,1)S(1)} %get-tuple-element.231.refs_1_), channel_id=1, source_target_pairs={{0,16},{1,9},{2,18},{3,11},{4,20},{5,13},{6,22},{7,15},{8,24},{9,1... | collective-permute-start | bytes 3538952 | tf_op jit(solution)/shard_map/ppermute | solution.py:474
  131.5 29.7 %collective-permute-start.19 = (bf16[384,2304]{1,0:T(8,128)(2,1)S(1)}, bf16[384,2304]{1,0:T(8,128)(2,1)S(1)}, u32[]{:S(2)}, u32[]{:S(2)}) collective-permute-start(bf16[384,2304]{1,0:T(8,128)(2,1)S(1)} %get-tuple-element.239), channel_id=1, source_target_pairs={{0,4},{1,3},{2,6},{3,1},{4,0},{5,7},{6,2},{7,5},{8,12},{9,11},{10,... | collective-permute-start | bytes 5308424 | tf_op jit(solution)/shard_map/ppermute | solution.py:474
  133.2 28.0 %collective-permute-start.18 = (bf16[384,1152]{1,0:T(8,128)(2,1)S(1)}, bf16[384,1152]{1,0:T(8,128)(2,1)S(1)}, u32[]{:S(2)}, u32[]{:S(2)}) collective-permute-start(bf16[384,1152]{1,0:T(8,128)(2,1)S(1)} %get-tuple-element.238.refs_1_), channel_id=1, source_target_pairs={{0,2},{1,5},{2,0},{3,7},{4,6},{5,1},{6,4},{7,3},{8,10},{9,13},{10,... | collective-permute-start | bytes 2654216 | tf_op jit(solution)/shard_map/ppermute | solution.py:474
  161.9 32.4 %collective-permute-start.20 = (bf16[768,1152]{1,0:T(8,128)(2,1)S(1)}, bf16[768,1152]{1,0:T(8,128)(2,1)S(1)}, u32[]{:S(2)}, u32[]{:S(2)}) collective-permute-start(bf16[768,1152]{1,0:T(8,128)(2,1)S(1)} %get-tuple-element.248.refs_2_.refs_8_), channel_id=1, source_target_pairs={{0,4},{1,3},{2,6},{3,1},{4,0},{5,7},{6,2},{7,5},{8,12},{9,11},{10,... | collective-permute-start | bytes 5308424 | tf_op jit(solution)/shard_map/ppermute | solution.py:474
  163.7 25.9 %collective-permute-start.21 = (bf16[192,1536]{1,0:T(8,128)(2,1)S(1)}, bf16[192,1536]{1,0:T(8,128)(2,1)S(1)}, u32[]{:S(2)}, u32[]{:S(2)}) collective-permute-start(bf16[192,1536]{1,0:T(8,128)(2,1)S(1)} %get-tuple-element.249), channel_id=1, source_target_pairs={{0,8},{1,17},{2,10},{3,19},{4,12},{5,21},{6,14},{7,23},{8,0},{9,25... | collective-permute-start | bytes 1769480 | tf_op jit(solution)/shard_map/ppermute | solution.py:474
  166.4 23.8 %collective-permute-start.22 = (bf16[192,1536]{1,0:T(8,128)(2,1)S(1)}, bf16[192,1536]{1,0:T(8,128)(2,1)S(1)}, u32[]{:S(2)}, u32[]{:S(2)}) collective-permute-start(bf16[192,1536]{1,0:T(8,128)(2,1)S(1)} %get-tuple-element.250), channel_id=1, source_target_pairs={{0,16},{1,9},{2,18},{3,11},{4,20},{5,13},{6,22},{7,15},{8,24},{9,1... | collective-permute-start | bytes 1769480 | tf_op jit(solution)/shard_map/ppermute | solution.py:474
  218.8 34.6 %collective-permute-start.26 = (bf16[384,1536]{1,0:T(8,128)(2,1)}, bf16[384,1536]{1,0:T(8,128)(2,1)}, u32[]{:S(2)}, u32[]{:S(2)}) collective-permute-start(bf16[384,1536]{1,0:T(8,128)(2,1)} %get-tuple-element.261), channel_id=1, source_target_pairs={{0,16},{1,9},{2,18},{3,11},{4,20},{5,13},{6,22},{7,15},{8,24},{9,1... | collective-permute-start | bytes 3538952 | tf_op jit(solution)/shard_map/ppermute | solution.py:474
  241.7 35.2 %collective-permute-start.29 = (bf16[384,1536]{1,0:T(8,128)(2,1)}, bf16[384,1536]{1,0:T(8,128)(2,1)}, u32[]{:S(2)}, u32[]{:S(2)}) collective-permute-start(bf16[384,1536]{1,0:T(8,128)(2,1)} %get-tuple-element.278), channel_id=1, source_target_pairs={{0,1},{1,0},{2,3},{3,2},{4,5},{5,4},{6,7},{7,6},{8,9},{9,8},{10,11... | collective-permute-start | bytes 3538952 | tf_op jit(solution)/shard_map/ppermute | solution.py:477
  242.7 34.2 %collective-permute-start.30 = (bf16[384,1536]{1,0:T(8,128)(2,1)}, bf16[384,1536]{1,0:T(8,128)(2,1)}, u32[]{:S(2)}, u32[]{:S(2)}) collective-permute-start(bf16[384,1536]{1,0:T(8,128)(2,1)} %get-tuple-element.279), channel_id=1, source_target_pairs={{0,1},{1,0},{2,3},{3,2},{4,5},{5,4},{6,7},{7,6},{8,9},{9,8},{10,11... | collective-permute-start | bytes 3538952 | tf_op jit(solution)/shard_map/ppermute | solution.py:477
  251.4 25.5 %collective-permute-start.31 = (bf16[384,1152]{1,0:T(8,128)(2,1)}, bf16[384,1152]{1,0:T(8,128)(2,1)}, u32[]{:S(2)}, u32[]{:S(2)}) collective-permute-start(bf16[384,1152]{1,0:T(8,128)(2,1)} %get-tuple-element.280), channel_id=1, source_target_pairs={{0,4},{1,3},{2,6},{3,1},{4,0},{5,7},{6,2},{7,5},{8,12},{9,11},{10,... | collective-permute-start | bytes 2654216 | tf_op jit(solution)/shard_map/ppermute | solution.py:474
  252.6 24.2 %collective-permute-start.28 = (bf16[384,1152]{1,0:T(8,128)(2,1)}, bf16[384,1152]{1,0:T(8,128)(2,1)}, u32[]{:S(2)}, u32[]{:S(2)}) collective-permute-start(bf16[384,1152]{1,0:T(8,128)(2,1)} %get-tuple-element.276), channel_id=1, source_target_pairs={{0,4},{1,3},{2,6},{3,1},{4,0},{5,7},{6,2},{7,5},{8,12},{9,11},{10,... | collective-permute-start | bytes 2654216 | tf_op jit(solution)/shard_map/ppermute | solution.py:474
  288.5 34.2 %collective-permute-start.32 = (bf16[384,2304]{1,0:T(8,128)(2,1)S(1)}, bf16[384,2304]{1,0:T(8,128)(2,1)S(1)}, u32[]{:S(2)}, u32[]{:S(2)}) collective-permute-start(bf16[384,2304]{1,0:T(8,128)(2,1)S(1)} %get-tuple-element.284), channel_id=1, source_target_pairs={{0,4},{1,3},{2,6},{3,1},{4,0},{5,7},{6,2},{7,5},{8,12},{9,11},{10,... | collective-permute-start | bytes 5308424 | tf_op jit(solution)/shard_map/ppermute | solution.py:474
  289.5 29.7 %collective-permute-start.34 = (bf16[384,1536]{1,0:T(8,128)(2,1)S(1)}, bf16[384,1536]{1,0:T(8,128)(2,1)S(1)}, u32[]{:S(2)}, u32[]{:S(2)}) collective-permute-start(bf16[384,1536]{1,0:T(8,128)(2,1)S(1)} %get-tuple-element.291), channel_id=1, source_target_pairs={{0,16},{1,9},{2,18},{3,11},{4,20},{5,13},{6,22},{7,15},{8,24},{9,1... | collective-permute-start | bytes 3538952 | tf_op jit(solution)/shard_map/ppermute | solution.py:474
  290.1 30.0 %collective-permute-start.33 = (bf16[384,1152]{1,0:T(8,128)(2,1)S(1)}, bf16[384,1152]{1,0:T(8,128)(2,1)S(1)}, u32[]{:S(2)}, u32[]{:S(2)}) collective-permute-start(bf16[384,1152]{1,0:T(8,128)(2,1)S(1)} %get-tuple-element.289), channel_id=1, source_target_pairs={{0,2},{1,5},{2,0},{3,7},{4,6},{5,1},{6,4},{7,3},{8,10},{9,13},{10,... | collective-permute-start | bytes 2654216 | tf_op jit(solution)/shard_map/ppermute | solution.py:474
  321.5 40.3 %collective-permute-start.38 = (bf16[384,2304]{1,0:T(8,128)(2,1)S(1)}, bf16[384,2304]{1,0:T(8,128)(2,1)S(1)}, u32[]{:S(2)}, u32[]{:S(2)}) collective-permute-start(bf16[384,2304]{1,0:T(8,128)(2,1)S(1)} %get-tuple-element.313), channel_id=1, source_target_pairs={{0,4},{1,3},{2,6},{3,1},{4,0},{5,7},{6,2},{7,5},{8,12},{9,11},{10,... | collective-permute-start | bytes 5308424 | tf_op jit(solution)/shard_map/ppermute | solution.py:474
  327.7 38.9 %collective-permute-start.40 = (bf16[384,2304]{1,0:T(8,128)(2,1)S(1)}, bf16[384,2304]{1,0:T(8,128)(2,1)S(1)}, u32[]{:S(2)}, u32[]{:S(2)}) collective-permute-start(bf16[384,2304]{1,0:T(8,128)(2,1)S(1)} %get-tuple-element.319), channel_id=1, source_target_pairs={{0,2},{1,5},{2,0},{3,7},{4,6},{5,1},{6,4},{7,3},{8,10},{9,13},{10,... | collective-permute-start | bytes 5308424 | tf_op jit(solution)/shard_map/ppermute | solution.py:474
  369.7 33.9 %collective-permute-start.45 = (bf16[768,1024]{1,0:T(8,128)(2,1)S(1)}, bf16[768,1024]{1,0:T(8,128)(2,1)S(1)}, u32[]{:S(2)}, u32[]{:S(2)}) collective-permute-start(bf16[768,1024]{1,0:T(8,128)(2,1)S(1)} %get-tuple-element.333), channel_id=1, source_target_pairs={{0,4},{1,3},{2,6},{3,1},{4,0},{5,7},{6,2},{7,5},{8,12},{9,11},{10,... | collective-permute-start | bytes 4718600 | tf_op jit(solution)/shard_map/ppermute | solution.py:474
  371.0 32.0 %collective-permute-start.46 = (bf16[192,2304]{1,0:T(8,128)(2,1)S(1)}, bf16[192,2304]{1,0:T(8,128)(2,1)S(1)}, u32[]{:S(2)}, u32[]{:S(2)}) collective-permute-start(bf16[192,2304]{1,0:T(8,128)(2,1)S(1)} %get-tuple-element.335), channel_id=1, source_target_pairs={{0,8},{1,17},{2,10},{3,19},{4,12},{5,21},{6,14},{7,23},{8,0},{9,25... | collective-permute-start | bytes 2654216 | tf_op jit(solution)/shard_map/ppermute | solution.py:474
  373.0 33.3 %collective-permute-start.44 = (bf16[768,768]{1,0:T(8,128)(2,1)S(1)}, bf16[768,768]{1,0:T(8,128)(2,1)S(1)}, u32[]{:S(2)}, u32[]{:S(2)}) collective-permute-start(bf16[768,768]{1,0:T(8,128)(2,1)S(1)} %get-tuple-element.332), channel_id=1, source_target_pairs={{0,4},{1,3},{2,6},{3,1},{4,0},{5,7},{6,2},{7,5},{8,12},{9,11},{10,... | collective-permute-start | bytes 3538952 | tf_op jit(solution)/shard_map/ppermute | solution.py:474
  373.8 26.5 %collective-permute-start.42 = (bf16[192,1152]{1,0:T(8,128)(2,1)S(1)}, bf16[192,1152]{1,0:T(8,128)(2,1)S(1)}, u32[]{:S(2)}, u32[]{:S(2)}) collective-permute-start(bf16[192,1152]{1,0:T(8,128)(2,1)S(1)} %get-tuple-element.328), channel_id=1, source_target_pairs={{0,16},{1,9},{2,18},{3,11},{4,20},{5,13},{6,22},{7,15},{8,24},{9,1... | collective-permute-start | bytes 1327112 | tf_op jit(solution)/shard_map/ppermute | solution.py:474
  376.5 25.9 %collective-permute-start.41 = (f32[32,128]{1,0:T(8,128)S(1)}, f32[32,128]{1,0:T(8,128)S(1)}, u32[]{:S(2)}, u32[]{:S(2)}) collective-permute-start(f32[32,128]{1,0:T(8,128)S(1)} %bitcast.27), channel_id=1, source_target_pairs={{0,1},{1,0},{2,3},{3,2},{4,5},{5,4},{6,7},{7,6},{8,9},{9,8},{10,11... | collective-permute-start | bytes 49160 | tf_op jit(solution)/shard_map/ppermute | solution.py:477
  408.1 20.8 %collective-permute-start.48 = (bf16[384,768]{1,0:T(8,128)(2,1)S(1)}, bf16[384,768]{1,0:T(8,128)(2,1)S(1)}, u32[]{:S(2)}, u32[]{:S(2)}) collective-permute-start(bf16[384,768]{1,0:T(8,128)(2,1)S(1)} %get-tuple-element.342), channel_id=1, source_target_pairs={{0,2},{1,5},{2,0},{3,7},{4,6},{5,1},{6,4},{7,3},{8,10},{9,13},{10,... | collective-permute-start | bytes 1769480 | tf_op jit(solution)/shard_map/ppermute | solution.py:474
  409.6 46.2 %collective-permute-start.56 = (bf16[192,2304]{1,0:T(8,128)(2,1)S(1)}, bf16[192,2304]{1,0:T(8,128)(2,1)S(1)}, u32[]{:S(2)}, u32[]{:S(2)}) collective-permute-start(bf16[192,2304]{1,0:T(8,128)(2,1)S(1)} %get-tuple-element.361), channel_id=1, source_target_pairs={{0,16},{1,9},{2,18},{3,11},{4,20},{5,13},{6,22},{7,15},{8,24},{9,1... | collective-permute-start | bytes 2654216 | tf_op jit(solution)/shard_map/ppermute | solution.py:474
  425.5 21.6 %collective-permute-start.51 = (bf16[192,1024]{1,0:T(8,128)(2,1)S(1)}, bf16[192,1024]{1,0:T(8,128)(2,1)S(1)}, u32[]{:S(2)}, u32[]{:S(2)}) collective-permute-start(bf16[192,1024]{1,0:T(8,128)(2,1)S(1)} %get-tuple-element.350), channel_id=1, source_target_pairs={{0,16},{1,9},{2,18},{3,11},{4,20},{5,13},{6,22},{7,15},{8,24},{9,1... | collective-permute-start | bytes 1179656 | tf_op jit(solution)/shard_map/ppermute | solution.py:474
  429.6 25.5 %collective-permute-start.53 = (bf16[192,768]{1,0:T(8,128)(2,1)S(1)}, bf16[192,768]{1,0:T(8,128)(2,1)S(1)}, u32[]{:S(2)}, u32[]{:S(2)}) collective-permute-start(bf16[192,768]{1,0:T(8,128)(2,1)S(1)} %get-tuple-element.355), channel_id=1, source_target_pairs={{0,16},{1,9},{2,18},{3,11},{4,20},{5,13},{6,22},{7,15},{8,24},{9,1... | collective-permute-start | bytes 884744 | tf_op jit(solution)/shard_map/ppermute | solution.py:474
  (107 other events, 1236.1 us)
